TPU v7x, 32 devices: a whole 2x2x4 slice. The times are simulated.
32 devices in a mesh: seq: 8 (over z, x), head: 4 (over y, core).
Axes of the slice: x: 2, y: 2, z: 4, core: 2. Of those that a mesh axis runs over, the one named last changes fastest.
Arguments:
- stream: bfloat16 [3072, 2048], P('seq'), may hold values from -9 to 9
- seg_ids: int32 [3072], P('seq'), may hold values from 0 to 3, never falling along the last dimension, each value on 1 to 1536 neighbouring positions
- attn_gain: float32 [2048], replicated, may hold values from 0.5 to 1.5
- w_query: bfloat16 [2048, 2048], P(None, 'head'), may hold values from -0.375 to 0.375
- w_key: bfloat16 [2048, 2048], P(None, 'head'), may hold values from -0.375 to 0.375
- w_value: bfloat16 [2048, 2048], P(None, 'head'), may hold values from -0.125 to 0.125
- w_outgate: bfloat16 [2048, 2048], P(None, 'head'), may hold values from -0.125 to 0.125
- w_low: bfloat16 [2048, 64], P(None, 'head'), may hold values from -0.125 to 0.125
- w_slot: float32 [4, 16, 64], P('head'), may hold values from -1.5 to 1.5
- forget_bias: float32 [4, 64], P('head'), may hold values from 1 to 7
- head_gain: float32 [4, 512], P('head'), may hold values from 0.5 to 1.5
- w_out: bfloat16 [2048, 2048], P('head'), may hold values from -0.1875 to 0.1875
- mlp_gain: float32 [2048], replicated, may hold values from 0.5 to 1.5
- w_gate: bfloat16 [2048, 5632], P(None, 'head'), may hold values from -0.125 to 0.125
- w_up: bfloat16 [2048, 5632], P(None, 'head'), may hold values from -0.125 to 0.125
- w_down: bfloat16 [5632, 2048], P('head'), may hold values from -0.109375 to 0.109375
- cotangent: bfloat16 [3072, 2048], P('seq'), may hold values from -6 to 6
Outputs:
- out: bfloat16 [3072, 2048], P('seq')
- grad_stream: bfloat16 [3072, 2048], P('seq')
- grad_attn_gain: float32 [2048], P('seq')
- grad_w_query: float32 [2048, 2048], P('seq', 'head')
- grad_w_key: float32 [2048, 2048], P('seq', 'head')
- grad_w_value: float32 [2048, 2048], P('seq', 'head')
- grad_w_outgate: float32 [2048, 2048], P('seq', 'head')
- grad_w_low: float32 [2048, 64], P('seq', 'head')
- grad_w_slot: float32 [4, 16, 64], P('head', None, 'seq')
- grad_forget_bias: float32 [4, 64], P('head', 'seq')
- grad_head_gain: float32 [4, 512], P('head', 'seq')
- grad_w_out: float32 [2048, 2048], P('head', 'seq')
- grad_mlp_gain: float32 [2048], P('seq')
- grad_w_gate: float32 [2048, 5632], P('seq', 'head')
- grad_w_up: float32 [2048, 5632], P('seq', 'head')
- grad_w_down: float32 [5632, 2048], P('head', 'seq')
- stream_rms: float32 [3], replicated
Inputs may be any that keep to these rules, and one draw needn't show every extreme that they name: `seg_ids`: document numbers never fall along the sequence; every document has 1 to 1536 tokens and one has exactly 1536.
All inputs are finite; a program needn't handle non-finite values.
Results may differ from a plain program's by a relative error of at most 0.013.
Values sent between devices are 32-bit elements; how exact they have to be, the bound alone decides.
A program may use at most 256 MiB of HBM per device.

v0:
```python
import jax
import jax.numpy as jnp
from jax import lax
from jax.sharding import PartitionSpec as P

BLOCK = 64


EPSILON = 1e-06
GATE_NORM = 8.0
PRECISE = lax.Precision.HIGHEST


def passed_along(array, axis, by):
    devices = lax.axis_size(axis)
    pairs = [(i, i + by) for i in range(devices) if 0 <= i + by < devices]
    return lax.ppermute(array, axis, pairs)


def entering(part, axis, combine, identity, reverse):
    count = lax.axis_size(axis)
    place = lax.axis_index(axis)
    ahead = count - 1 - place if reverse else place
    gathered = jax.tree.map(lambda a: lax.all_gather(a, axis), part)
    state = jax.tree.map(lambda a, e: jnp.zeros_like(a) + jnp.asarray(e, a.dtype), part, identity)

    def one(turn, state):
        source = count - 1 - turn if reverse else turn
        return combine(
            state, jax.tree.map(lambda a: lax.dynamic_index_in_dim(a, source, 0, False), gathered)
        )

    return lax.fori_loop(0, ahead, one, state)


def rounded_float(value):
    return lax.optimization_barrier(value.astype(jnp.bfloat16)).astype(jnp.float32)


def keep_round(value):
    return value + lax.stop_gradient(rounded_float(value) - value)


def precise_dot(left, right):
    return jnp.dot(left, right, precision=PRECISE, preferred_element_type=jnp.float32)


def plain_dot(left, right):
    return jnp.dot(left, right, preferred_element_type=jnp.float32)


def dot_right_t(left, right):
    return lax.dot_general(
        left, right, (((1,), (1,)), ((), ())), preferred_element_type=jnp.float32
    )


def dot_left_t(left, right):
    return lax.dot_general(
        left, right, (((0,), (0,)), ((), ())), preferred_element_type=jnp.float32
    )


def precise_left_t(left, right):
    return lax.dot_general(
        left, right, (((0,), (0,)), ((), ())), precision=PRECISE, preferred_element_type=jnp.float32
    )


def precise_right_t(left, right):
    return lax.dot_general(
        left, right, (((1,), (1,)), ((), ())), precision=PRECISE, preferred_element_type=jnp.float32
    )


def rms_scale(value):
    return lax.rsqrt(jnp.mean(value * value, axis=-1, keepdims=True) + EPSILON)


def block_step(state_in, inputs):
    key_state, value_state, seg_before = state_in
    queries, key_rows, value_rows, log_decay, segment = inputs
    positions = log_decay.shape[0]
    running = jnp.cumsum(log_decay, axis=0)
    position = jnp.arange(positions)
    same_doc = (segment[:, None] == segment[None, :]) & (position[:, None] >= position[None, :])
    same_doc = same_doc[:, :, None]
    decay_span = jnp.where(same_doc, running[:, None, :] - running[None, :, :], 0.0)
    weights = jnp.where(same_doc, jnp.exp(decay_span), 0.0) * (-jnp.expm1(log_decay))[None, :, :]
    carried = jnp.where((segment == seg_before)[:, None], jnp.exp(running), 0.0)
    scaling = queries.shape[1] ** (-0.5)
    affinity = precise_right_t(queries, key_rows)
    scores = scaling * (
        carried * precise_right_t(queries, key_state)
        + jnp.einsum("tjm,tj->tm", weights, affinity, precision=PRECISE)
    )
    slot_probs = keep_round(jax.nn.softmax(scores, axis=1))
    mixing = jnp.einsum("tm,tjm->tj", slot_probs, weights, precision=PRECISE)
    output = precise_dot(slot_probs * carried, value_state) + precise_dot(mixing, value_rows)
    last_row = weights[positions - 1]
    keep_last = carried[positions - 1][:, None]
    key_next = keep_last * key_state + precise_left_t(last_row, key_rows)
    value_next = keep_last * value_state + precise_left_t(last_row, value_rows)
    return ((key_next, value_next, segment[positions - 1]), output)


def to_blocks(array):
    return array.reshape((array.shape[0] // BLOCK, BLOCK) + array.shape[1:])


def compose(earlier, later):
    factor = later[0][:, None]
    return (earlier[0] * later[0], factor * earlier[1] + later[1], factor * earlier[2] + later[2])


def body(
    stream,
    seg_ids,
    attn_gain,
    w_query,
    w_key,
    w_value,
    w_outgate,
    w_low,
    w_slot,
    forget_bias,
    head_gain,
    w_out,
    mlp_gain,
    w_gate,
    w_up,
    w_down,
    cotangent,
):
    tok_rows = stream.shape[0]
    width = stream.shape[1]
    slots = w_slot.shape[2]
    head_width = w_query.shape[1]
    prior = passed_along(seg_ids[tok_rows - 1 :], "seq", 1)[0]
    stream_f = stream.astype(jnp.float32)
    scale_in = rms_scale(stream_f)
    normed_in = (stream_f * scale_in * attn_gain).astype(jnp.bfloat16)
    query_f = rounded_float(plain_dot(normed_in, w_query))
    key_f = rounded_float(plain_dot(normed_in, w_key))
    value_f = rounded_float(plain_dot(normed_in, w_value))
    gate_act = plain_dot(normed_in, w_outgate)
    ranked = plain_dot(normed_in, w_low)

    def decay_logs(ranked_in, slot_map, bias_row):
        return jax.nn.log_sigmoid(precise_dot(ranked_in, slot_map[0]) + bias_row[0]) / GATE_NORM

    log_decay, gate_pull = jax.vjp(decay_logs, ranked, w_slot, forget_bias)

    def attend(queries, key_rows, value_rows, decay_in, key_in, value_in):
        final_state, reads = lax.scan(
            block_step,
            (key_in, value_in, prior),
            (
                to_blocks(queries),
                to_blocks(key_rows),
                to_blocks(value_rows),
                to_blocks(decay_in),
                to_blocks(seg_ids),
            ),
        )
        return reads.reshape(tok_rows, head_width)

    def finish(key_rows, value_rows, decay_in, key_in, value_in):
        running = jnp.cumsum(decay_in, axis=0)
        total = running[tok_rows - 1]
        same_doc = (seg_ids == seg_ids[tok_rows - 1])[:, None]
        factor = jnp.where(
            same_doc, jnp.exp(jnp.where(same_doc, total[None, :] - running, 0.0)), 0.0
        ) * -jnp.expm1(decay_in)
        through = jnp.where(seg_ids[tok_rows - 1] == prior, jnp.exp(total), 0.0)[:, None]
        return (
            through * key_in + precise_left_t(factor, key_rows),
            through * value_in + precise_left_t(factor, value_rows),
        )

    zero_state = jnp.zeros((slots, head_width), jnp.float32)
    local_key, local_value = finish(key_f, value_f, log_decay, zero_state, zero_state)
    decay_all = jnp.where(seg_ids[tok_rows - 1] == prior, jnp.exp(jnp.sum(log_decay, axis=0)), 0.0)
    identity = (jnp.ones((slots,), jnp.float32), zero_state, zero_state)
    prefix = entering((decay_all, local_key, local_value), "seq", compose, identity, False)
    key_in = prefix[1]
    value_in = prefix[2]
    slot_read, attend_pull = jax.vjp(attend, query_f, key_f, value_f, log_decay, key_in, value_in)
    scale_read = rms_scale(slot_read)
    normed_read = slot_read * scale_read * head_gain[0]
    gate_sig = jax.nn.sigmoid(gate_act)
    gate_silu = gate_act * gate_sig
    mixed_heads = (normed_read * gate_silu).astype(jnp.bfloat16)
    branch = lax.psum(plain_dot(mixed_heads, w_out), "head")
    hidden = stream_f + branch
    scale_mid = rms_scale(hidden)
    normed_mid = (hidden * scale_mid * mlp_gain).astype(jnp.bfloat16)
    gate_pre = plain_dot(normed_mid, w_gate)
    up_pre = plain_dot(normed_mid, w_up)
    pre_sig = jax.nn.sigmoid(gate_pre)
    pre_silu = gate_pre * pre_sig
    ffn_act = (pre_silu * up_pre).astype(jnp.bfloat16)
    ffn_out = lax.psum(plain_dot(ffn_act, w_down), "head")
    result = hidden + ffn_out
    square_sums = lax.psum(
        jnp.stack(
            [jnp.sum(stream_f * stream_f), jnp.sum(hidden * hidden), jnp.sum(result * result)]
        ),
        "seq",
    )
    stream_rms = jnp.sqrt(square_sums / (tok_rows * lax.axis_size("seq") * width))
    upstream = cotangent.astype(jnp.float32)
    d_act = dot_right_t(cotangent, w_down)
    grad_down = dot_left_t(ffn_act, cotangent)
    d_gate = (d_act * up_pre * pre_sig * (1.0 + gate_pre * (1.0 - pre_sig))).astype(jnp.bfloat16)
    d_up = (d_act * pre_silu).astype(jnp.bfloat16)
    d_mid = lax.psum(dot_right_t(d_gate, w_gate) + dot_right_t(d_up, w_up), "head")
    grad_gate = dot_left_t(normed_mid, d_gate)
    grad_up = dot_left_t(normed_mid, d_up)
    grad_mlp_gain = jnp.sum(d_mid * hidden * scale_mid, axis=0)
    scaled_mid = d_mid * mlp_gain
    d_hidden = (
        upstream
        + scale_mid * scaled_mid
        - hidden * scale_mid**3 * jnp.mean(scaled_mid * hidden, axis=1, keepdims=True)
    )
    d_branch = d_hidden.astype(jnp.bfloat16)
    d_mixed = dot_right_t(d_branch, w_out)
    grad_out = dot_left_t(mixed_heads, d_branch)
    d_gate_act = (d_mixed * normed_read * gate_sig * (1.0 + gate_act * (1.0 - gate_sig))).astype(
        jnp.bfloat16
    )
    d_normed = d_mixed * gate_silu
    grad_head_gain = jnp.sum(d_normed * slot_read * scale_read, axis=0)[None, :]
    scaled_read = d_normed * head_gain[0]
    d_read = scale_read * scaled_read - slot_read * scale_read**3 * jnp.mean(
        scaled_read * slot_read, axis=1, keepdims=True
    )
    d_query, d_key, d_value, d_logs, back_key, back_value = attend_pull(d_read)
    suffix = entering((decay_all, back_key, back_value), "seq", compose, identity, True)
    finish_out, finish_pull = jax.vjp(finish, key_f, value_f, log_decay, key_in, value_in)
    more_key, more_value, more_logs, unused_key, unused_value = finish_pull((suffix[1], suffix[2]))
    query_back = d_query.astype(jnp.bfloat16)
    key_back = (d_key + more_key).astype(jnp.bfloat16)
    value_back = (d_value + more_value).astype(jnp.bfloat16)
    d_ranked, grad_slot, grad_bias = gate_pull(d_logs + more_logs)
    normed_f = normed_in.astype(jnp.float32)
    grad_low = precise_left_t(normed_f, d_ranked)
    grad_query = dot_left_t(normed_in, query_back)
    grad_key = dot_left_t(normed_in, key_back)
    grad_value = dot_left_t(normed_in, value_back)
    grad_outgate = dot_left_t(normed_in, d_gate_act)
    d_normed_in = (
        dot_right_t(query_back, w_query)
        + dot_right_t(key_back, w_key)
        + dot_right_t(value_back, w_value)
        + dot_right_t(d_gate_act, w_outgate)
        + precise_right_t(d_ranked, w_low.astype(jnp.float32))
    )
    d_in = lax.psum(d_normed_in, "head")
    grad_attn_gain = jnp.sum(d_in * stream_f * scale_in, axis=0)
    scaled_in = d_in * attn_gain
    grad_stream = (
        d_hidden
        + scale_in * scaled_in
        - stream_f * scale_in**3 * jnp.mean(scaled_in * stream_f, axis=1, keepdims=True)
    ).astype(jnp.bfloat16)
    summed = (
        lax.psum_scatter(grad_attn_gain, "seq", scatter_dimension=0, tiled=True),
        lax.psum_scatter(grad_query, "seq", scatter_dimension=0, tiled=True),
        lax.psum_scatter(grad_key, "seq", scatter_dimension=0, tiled=True),
        lax.psum_scatter(grad_value, "seq", scatter_dimension=0, tiled=True),
        lax.psum_scatter(grad_outgate, "seq", scatter_dimension=0, tiled=True),
        lax.psum_scatter(grad_low, "seq", scatter_dimension=0, tiled=True),
        lax.psum_scatter(grad_slot, "seq", scatter_dimension=2, tiled=True),
        lax.psum_scatter(grad_bias, "seq", scatter_dimension=1, tiled=True),
        lax.psum_scatter(grad_head_gain, "seq", scatter_dimension=1, tiled=True),
        lax.psum_scatter(grad_out, "seq", scatter_dimension=1, tiled=True),
        lax.psum_scatter(grad_mlp_gain, "seq", scatter_dimension=0, tiled=True),
        lax.psum_scatter(grad_gate, "seq", scatter_dimension=0, tiled=True),
        lax.psum_scatter(grad_up, "seq", scatter_dimension=0, tiled=True),
        lax.psum_scatter(grad_down, "seq", scatter_dimension=1, tiled=True),
    )
    mixer_parts = summed[:10]
    ffn_parts = summed[10:]
    return (
        result.astype(jnp.bfloat16),
        grad_stream,
        mixer_parts[0],
        mixer_parts[1],
        mixer_parts[2],
        mixer_parts[3],
        mixer_parts[4],
        mixer_parts[5],
        mixer_parts[6],
        mixer_parts[7],
        mixer_parts[8],
        mixer_parts[9],
        ffn_parts[0],
        ffn_parts[1],
        ffn_parts[2],
        ffn_parts[3],
        stream_rms,
    )


def solution(mesh):
    in_specs = (
        P("seq", None),
        P("seq"),
        P(),
        P(None, "head"),
        P(None, "head"),
        P(None, "head"),
        P(None, "head"),
        P(None, "head"),
        P("head", None, None),
        P("head", None),
        P("head", None),
        P("head", None),
        P(),
        P(None, "head"),
        P(None, "head"),
        P("head", None),
        P("seq", None),
    )
    out_specs = (
        P("seq", None),
        P("seq", None),
        P("seq"),
        P("seq", "head"),
        P("seq", "head"),
        P("seq", "head"),
        P("seq", "head"),
        P("seq", "head"),
        P("head", None, "seq"),
        P("head", "seq"),
        P("head", "seq"),
        P("head", "seq"),
        P("seq"),
        P("seq", "head"),
        P("seq", "head"),
        P("head", "seq"),
        P(),
    )
    return jax.shard_map(body, mesh=mesh, in_specs=in_specs, out_specs=out_specs, check_vma=False)
```

profile of v0, /device:TPU:0, one launch (start us, length us, event | category | flops | bytes accessed | tf_op | source)
XLA Modules:
  0.0 2097.2 jit_solution(14405409629611684245)
XLA Ops:
  41.3 19.2 all-reduce.3
  68.0 41.7 %all-gather.10.cloned.1.call-done = f32[512,512]{1,0:T(8,128)} async-done(((f32[64,512]{1,0:T(8,128)}), f32[512,512]{1,0:T(8,128)}) %all-gather.10.cloned.1.call-update) | async-done | bytes 1048592 | tf_op jit(solution)/shard_map/all_gather | solution.py:24
  116.1 190.1 %while.121 = (s32[]{:T(128)}, f32[64,512]{1,0:T(8,128)S(1)}, f32[64,512]{1,0:T(8,128)S(1)}, s32[]{:T(128)}, f32[6,64,512]{2,1,0:T(8,128)}, /*index=5*/pred[6,64,...) while((s32[]{:T(128)}, f32[64,512]{1,0:T(8,128)S(1)}, ...), condition=%wide.region_10.11_spmd.clone, body=%wide.region_6.10_spmd.clone.sunk | while | flops 162037824 | bytes 11836321 | solution.py:155
  315.5 75.0 %all-reduce.14.cloned.1.call-done = f32[384,2048]{1,0:T(8,128)} async-done(((f32[384,2048]{1,0:T(8,128)}), f32[384,2048]{1,0:T(8,128)}) %all-reduce.14.cloned.1.call-update) | async-done | bytes 3145744 | tf_op jit(solution)/shard_map/psum | solution.py:194
  395.0 7.9 fusion.218
  425.5 119.0 %all-reduce.18.cloned.1.call-done = (f32[384,2048]{1,0:T(8,128)}, f32[384,2048]{1,0:T(8,128)}) async-done(((f32[384,2048]{1,0:T(8,128)}, f32[384,2048]{1,0:T(8,128)}), (f32[384,2048]{1,0:T(8,128)}, f32[384,2048]{1,0:T(8,128)})) %all-reduce.18.cloned.1.call-update) | async-done | bytes 6291472 | tf_op jit(solution)/shard_map/psum | solution.py:203
  557.0 203.1 %while.122 = (s32[]{:T(128)}, f32[64,512]{1,0:T(8,128)S(1)}, f32[64,512]{1,0:T(8,128)S(1)}, bf16[6,64,512]{2,1,0:T(8,128)(2,1)S(1)}, f32[6,64,512]{2,1,0:T(8,128...) while((s32[]{:T(128)}, f32[64,512]{1,0:T(8,128)S(1)}, ...), condition=%wide.region_26.27_spmd.clone, body=%wide.region_18.26_spmd.clone.sunk | while | flops 312401856 | bytes 12292755 | solution.py:155
  767.1 34.2 %all-gather.14.cloned.1.call-done = f32[512,512]{1,0:T(8,128)} async-done(((f32[64,512]{1,0:T(8,128)}), f32[512,512]{1,0:T(8,128)}) %all-gather.14.cloned.1.call-update) | async-done | bytes 1048592 | tf_op jit(solution)/shard_map/all_gather | solution.py:24
  801.3 40.9 %all-gather.16.cloned.1.call-done = f32[512,512]{1,0:T(8,128)} async-done(((f32[64,512]{1,0:T(8,128)}), f32[512,512]{1,0:T(8,128)}) %all-gather.16.cloned.1.call-update) | async-done | bytes 1048592 | tf_op jit(solution)/shard_map/all_gather | solution.py:24
  842.3 12.7 while.120
  901.9 7.5 fusion.228
  910.6 7.5 fusion.227
  919.4 8.8 fusion.229
  931.5 44.0 %all-reduce.16.cloned.1.call-done = f32[384,2048]{1,0:T(8,128)} async-done(((f32[384,2048]{1,0:T(8,128)}), f32[384,2048]{1,0:T(8,128)}) %all-reduce.16.cloned.1.call-update) | async-done | bytes 3145744 | tf_op jit(solution)/shard_map/psum | solution.py:260
  981.5 37.6 %all-reduce.8 = (f32[2048]{0:T(1024)S(1)}, f32[1,16,64]{1,0,2:T(1,128)S(1)}, f32[1,64]{1,0:T(1,128)S(1)}, f32[2048]{0:T(1024)S(1)}, f32[3]{0:T(128)S(1)}) all-reduce(f32[2048]{0:T(1024)S(1)} %get-tuple-element.1846, f32[1,16,64]{1,0,2:T(1,128)S(1)} %bitcast.628, ...), channel_id=7, replica_groups=mesh['seq'=8,'head'=4] {'seq'}, use_global_device_ids=true, to_apply=%region_37.38.clone | all-reduce | flops 5187 | bytes 41496
  1027.5 13.2 reduce-scatter.22.cloned.1.call-done
  1040.7 91.6 %reduce-scatter.24.cloned.1.call-done = f32[512,256]{1,0:T(8,128)} async-done(((f32[512,2048]{1,0:T(8,128)}), f32[512,256]{1,0:T(8,128)}) %reduce-scatter.24.cloned.1.call-update) | async-done | bytes 524304 | tf_op jit(solution)/shard_map/reduce_scatter | solution.py:278
  1132.3 92.3 %reduce-scatter.14.cloned.1.call-done = f32[256,512]{1,0:T(8,128)} async-done(((f32[2048,512]{1,0:T(8,128)}), f32[256,512]{1,0:T(8,128)}) %reduce-scatter.14.cloned.1.call-update) | async-done | bytes 524304 | tf_op jit(solution)/shard_map/reduce_scatter | solution.py:270
  1224.7 91.9 %reduce-scatter.20.cloned.1.call-done = f32[256,512]{1,0:T(8,128)} async-done(((f32[2048,512]{1,0:T(8,128)}), f32[256,512]{1,0:T(8,128)}) %reduce-scatter.20.cloned.1.call-update) | async-done | bytes 524304 | tf_op jit(solution)/shard_map/reduce_scatter | solution.py:273
  1316.6 92.4 %reduce-scatter.16.cloned.1.call-done = f32[256,512]{1,0:T(8,128)} async-done(((f32[2048,512]{1,0:T(8,128)}), f32[256,512]{1,0:T(8,128)}) %reduce-scatter.16.cloned.1.call-update) | async-done | bytes 524304 | tf_op jit(solution)/shard_map/reduce_scatter | solution.py:271
  1408.9 91.7 %reduce-scatter.18.cloned.1.call-done = f32[256,512]{1,0:T(8,128)} async-done(((f32[2048,512]{1,0:T(8,128)}), f32[256,512]{1,0:T(8,128)}) %reduce-scatter.18.cloned.1.call-update) | async-done | bytes 524304 | tf_op jit(solution)/shard_map/reduce_scatter | solution.py:272
  1500.7 196.9 %reduce-scatter.28.cloned.1.call-done = f32[256,1408]{1,0:T(8,128)} async-done(((f32[2048,1408]{1,0:T(8,128)}), f32[256,1408]{1,0:T(8,128)}) %reduce-scatter.28.cloned.1.call-update) | async-done | bytes 1441808 | tf_op jit(solution)/shard_map/reduce_scatter | solution.py:281
  1697.6 196.1 %reduce-scatter.26.cloned.1.call-done = f32[256,1408]{1,0:T(8,128)} async-done(((f32[2048,1408]{1,0:T(8,128)}), f32[256,1408]{1,0:T(8,128)}) %reduce-scatter.26.cloned.1.call-update) | async-done | bytes 1441808 | tf_op jit(solution)/shard_map/reduce_scatter | solution.py:280
  1893.7 196.7 %reduce-scatter.30.cloned.1.call-done = f32[1408,256]{1,0:T(8,128)} async-done(((f32[1408,2048]{1,0:T(8,128)}), f32[1408,256]{1,0:T(8,128)}) %reduce-scatter.30.cloned.1.call-update) | async-done | bytes 1441808 | tf_op jit(solution)/shard_map/reduce_scatter | solution.py:282
  (862 shorter events, 570.8 us)
Async XLA Ops:
  7.2 305.3 %copy-start = (bf16[512,2048]{1,0:T(8,128)(2,1)S(1)}, bf16[512,2048]{1,0:T(8,128)(2,1)}, u32[]{:S(2)}) copy-start(bf16[512,2048]{1,0:T(8,128)(2,1)} %param.36) | copy-start | bytes 6291460
  7.2 60.8 %all-gather.12.cloned.1.call-start = ((), (), s32[]{:S(2)}) async-start(), calls=%async_computation.22 | async-start | bytes 1179648 | tf_op jit(solution)/shard_map/all_gather | solution.py:24
  8.7 16.8 collective-permute-start
  16.5 19.8 copy-start.52
  27.8 81.9 %all-gather.10.cloned.1.call-start = ((), (), s32[]{:S(2)}) async-start(), calls=%async_computation.21 | async-start | bytes 1179648 | tf_op jit(solution)/shard_map/all_gather | solution.py:24
  32.8 357.7 %all-reduce.14.cloned.1.call-start = ((), (), s32[]{:S(2)}) async-start(), calls=%async_computation.10 | async-start | bytes 6291456 | tf_op jit(solution)/shard_map/psum | solution.py:194
  315.3 78.1 %copy-start.58 = (f32[2048]{0:T(1024)S(1)}, f32[2048]{0:T(1024)}, u32[]{:S(2)}) copy-start(f32[2048]{0:T(1024)} %param.37) | copy-start | bytes 24580
  315.3 229.2 %all-reduce.18.cloned.1.call-start = ((), (), s32[]{:S(2)}) async-start(), calls=%async_computation.26 | async-start | bytes 12582912 | tf_op jit(solution)/shard_map/psum | solution.py:203
  424.4 376.9 %all-gather.14.cloned.1.call-start = ((), (), s32[]{:S(2)}) async-start(), calls=%async_computation.23 | async-start | bytes 1179648 | tf_op jit(solution)/shard_map/all_gather | solution.py:24
  760.8 81.4 %all-gather.16.cloned.1.call-start = ((), (), s32[]{:S(2)}) async-start(), calls=%async_computation.24 | async-start | bytes 1179648 | tf_op jit(solution)/shard_map/all_gather | solution.py:24
  761.4 168.2 %reduce-scatter.32.cloned.1.call-start = ((), (), s32[]{:S(2)}) async-start(), calls=%async_computation.25 | async-start | bytes 294912
  767.0 208.4 %all-reduce.16.cloned.1.call-start = ((), (), s32[]{:S(2)}) async-start(), calls=%async_computation.11 | async-start | bytes 6291456 | tf_op jit(solution)/shard_map/psum | solution.py:260
  842.3 13.4 copy-start.17
  877.7 163.1 %reduce-scatter.22.cloned.1.call-start = ((), (), s32[]{:S(2)}) async-start(), calls=%async_computation.16 | async-start | bytes 147456 | tf_op jit(solution)/shard_map/reduce_scatter | solution.py:274
  880.7 251.6 %reduce-scatter.24.cloned.1.call-start = ((), (), s32[]{:S(2)}) async-start(), calls=%async_computation.17 | async-start | bytes 4718592 | tf_op jit(solution)/shard_map/reduce_scatter | solution.py:278
  885.9 338.7 %reduce-scatter.14.cloned.1.call-start = ((), (), s32[]{:S(2)}) async-start(), calls=%async_computation.12 | async-start | bytes 4718592 | tf_op jit(solution)/shard_map/reduce_scatter | solution.py:270
  889.4 427.2 %reduce-scatter.20.cloned.1.call-start = ((), (), s32[]{:S(2)}) async-start(), calls=%async_computation.15 | async-start | bytes 4718592 | tf_op jit(solution)/shard_map/reduce_scatter | solution.py:273
  893.7 515.2 %reduce-scatter.16.cloned.1.call-start = ((), (), s32[]{:S(2)}) async-start(), calls=%async_computation.13 | async-start | bytes 4718592 | tf_op jit(solution)/shard_map/reduce_scatter | solution.py:271
  897.1 603.6 %reduce-scatter.18.cloned.1.call-start = ((), (), s32[]{:S(2)}) async-start(), calls=%async_computation.14 | async-start | bytes 4718592 | tf_op jit(solution)/shard_map/reduce_scatter | solution.py:272
  900.7 797.0 %reduce-scatter.28.cloned.1.call-start = ((), (), s32[]{:S(2)}) async-start(), calls=%async_computation.19 | async-start | bytes 12976128 | tf_op jit(solution)/shard_map/reduce_scatter | solution.py:281
  909.4 984.3 %reduce-scatter.26.cloned.1.call-start = ((), (), s32[]{:S(2)}) async-start(), calls=%async_computation.18 | async-start | bytes 12976128 | tf_op jit(solution)/shard_map/reduce_scatter | solution.py:280
  918.2 1172.3 %reduce-scatter.30.cloned.1.call-start = ((), (), s32[]{:S(2)}) async-start(), calls=%async_computation.20 | async-start | bytes 12976128 | tf_op jit(solution)/shard_map/reduce_scatter | solution.py:282
  931.5 90.6 %copy-start.69 = (f32[384]{0:T(512)S(1)}, f32[384]{0:T(512)}, u32[]{:S(2)}) copy-start(f32[384]{0:T(512)} %get-tuple-element.2067) | copy-start | bytes 4612
  1022.0 1068.5 %copy-start.1 = (bf16[512,2048]{1,0:T(8,128)(2,1)S(1)}, bf16[512,2048]{1,0:T(8,128)(2,1)}, u32[]{:S(2)}) copy-start(bf16[512,2048]{1,0:T(8,128)(2,1)} %param.36) | copy-start | bytes 6291460
  (141 other events, 609.7 us)
Sparse Core Ops, SparseCore 0:
  28.0 40.0 all-gather.11
  70.7 38.9 all-gather.9
  315.4 75.0 all-reduce.13
  424.5 119.8 all-reduce.17
  760.9 40.3 all-gather.13
  803.3 38.8 all-gather.15
  845.5 59.9 reduce-scatter.31
  907.9 67.4 all-reduce.15
  979.3 61.3 reduce-scatter.21
  1044.8 87.4 reduce-scatter.23
  1137.0 87.6 reduce-scatter.13
  1228.7 87.8 reduce-scatter.19
  1321.2 87.6 reduce-scatter.15
  1413.0 87.6 reduce-scatter.17
  1505.1 192.4 reduce-scatter.27
  1702.1 191.6 reduce-scatter.25
  1898.2 192.2 reduce-scatter.29
where the time goes:
time: 2110 us; the launch traced here: 2100 us
  waiting for transfers between devices  1430 us (68%)
  matrix products  329 us (16%)
  other arithmetic  155 us (7%)
  local copies, waits for them, and re-layouts  103 us (5%)
  blocking collectives  56.7 us (3%)
    reduce_scatter x1, waiting for transfers between devices, body(): lax.psum_scatter(grad_up, 'seq', scatter_dimension=0, tiled=True)  197 us
    reduce_scatter x1, waiting for transfers between devices, body(): lax.psum_scatter(grad_down, 'seq', scatter_dimension=1, tiled=True)  197 us
    reduce_scatter x1, waiting for transfers between devices, body(): lax.psum_scatter(grad_gate, 'seq', scatter_dimension=0, tiled=True)  196 us
    all_gather x4, waiting for transfers between devices, entering(): gathered = jax.tree.map(lambda a: lax.all_gather(a, axis), part)  124 us
    psum x1, waiting for transfers between devices, body(): ffn_out = lax.psum(plain_dot(ffn_act, w_down), 'head')  119 us
    reduce_scatter x1, waiting for transfers between devices, body(): lax.psum_scatter(grad_key, 'seq', scatter_dimension=0, tiled=True)  92.4 us
    reduce_scatter x1, waiting for transfers between devices, body(): lax.psum_scatter(grad_query, 'seq', scatter_dimension=0, tiled=True)  92.3 us
    reduce_scatter x1, waiting for transfers between devices, body(): lax.psum_scatter(grad_outgate, 'seq', scatter_dimension=0, tiled=True)  91.9 us
  transfers between devices with their start and end apart: 18, of which 16 were waited for; matrix products, arithmetic and copies ran while one was open for 6% of the time, Pallas kernels for 0%

commit v1 on v0

v1 whole, which is shorter than its diff:
```python
import jax
import jax.numpy as jnp
from jax import lax
from jax.experimental import pallas as pl
from jax.experimental.pallas import tpu as pltpu
from jax.sharding import PartitionSpec as P

CHUNK = 32
CHUNKS = 2
VMEM = 48 << 20
READ_COST = 17 << 30
BACK_COST = 34 << 30


EPSILON = 1e-06
GATE_NORM = 8.0
PRECISE = lax.Precision.HIGHEST


def passed_along(array, axis, by):
    devices = lax.axis_size(axis)
    pairs = [(i, i + by) for i in range(devices) if 0 <= i + by < devices]
    return lax.ppermute(array, axis, pairs)


def swapped(array, axis, by):
    return lax.ppermute(array, axis, [(i, i ^ by) for i in range(lax.axis_size(axis))])


def entering(part, axis, combine, identity, reverse):
    count = lax.axis_size(axis)
    place = lax.axis_index(axis)
    ahead = count - 1 - place if reverse else place
    sign = -1 if reverse else 1

    def from_before(state, by):
        moved = jax.tree.map(lambda a: passed_along(a, axis, sign * by), state)
        return jax.tree.map(lambda m, e: jnp.where(ahead >= by, m, e), moved, identity)

    state = from_before(part, 1)
    by = 1
    while by < count:
        state = combine(from_before(state, by), state)
        by *= 2
    return state


def head_sum(parts):
    count = lax.axis_size("head")
    low = lax.axis_index("head") % 2
    out = []
    for part in parts:
        rows = part.shape[0] // 2
        mine = lax.dynamic_slice_in_dim(part, low * rows, rows, 0)
        other = lax.dynamic_slice_in_dim(part, (1 - low) * rows, rows, 0)
        half = mine + swapped(other, "head", 1)
        by = 2
        while by < count:
            half = half + swapped(half, "head", by)
            by *= 2
        back = swapped(half, "head", 1)
        out.append(jnp.where(low == 0, half, back))
        out.append(jnp.where(low == 0, back, half))
    return jnp.concatenate(out, axis=0)


def sent(array):
    moved = swapped(array.astype(jnp.float32), "seq", 1)
    unit = jnp.minimum(lax.axis_index("seq").astype(jnp.float32) + 1.0, 1.0)
    return (moved * unit).astype(jnp.bfloat16)


def width_blocks(array):
    count = lax.axis_size("seq")
    lines = count // 2
    place = lax.axis_index("seq")
    line, odd = place // 2, place % 2
    wide = array.shape[1] // count
    roles = list(range(lines))
    if lines == 4:
        left = line < 2
        roles = [jnp.where(left, a, b) for a, b in ((2, 1), (3, 0), (1, 2), (0, 3))]

    def blocks(parity):
        return jnp.stack(
            [lax.dynamic_slice_in_dim(array, (2 * r + parity) * wide, wide, 1) for r in roles]
        )

    mine, theirs = blocks(odd), blocks(1 - odd)
    return mine, sent(theirs)


def seq_sum(wide, narrow, wide_first):
    count = lax.axis_size("seq")
    lines = count // 2
    place = lax.axis_index("seq") // 2
    mine, theirs = wide
    pair = (narrow, sent(narrow))
    rule = "ztd,tf->zdf" if wide_first else "ztd,tf->zfd"

    def product(lo, hi):
        return sum(
            jnp.einsum(rule, w[lo:hi], n, preferred_element_type=jnp.float32)
            for w, n in zip((mine, theirs), pair)
        )

    if lines != 4:
        groups = [[line * 2 + x for line in range(lines)] for x in range(2)]
        return lax.psum_scatter(
            product(0, lines), "seq", scatter_dimension=0, axis_index_groups=groups, tiled=True
        )[0]

    def moved(array, pairs):
        return lax.ppermute(
            array, "seq", [(2 * a + x, 2 * b + x) for a, b in pairs for x in range(2)]
        )

    far = product(0, 3)
    near = product(3, 4)
    from_end = moved(far, ((0, 1), (3, 2)))
    from_middle = moved(far[:2] + from_end[:2], ((1, 2), (2, 1)))
    to_end = moved(near + from_middle[1:], ((1, 0), (2, 3)))
    at_end = (place == 0) | (place == 3)
    return jnp.where(at_end, near[0] + to_end[0], far[2] + from_end[2] + from_middle[0])


def precise_dot(left, right):
    return jnp.dot(left, right, precision=PRECISE, preferred_element_type=jnp.float32)


def plain_dot(left, right):
    return jnp.dot(left, right, preferred_element_type=jnp.float32)


def dot_right_t(left, right):
    return lax.dot_general(
        left, right, (((1,), (1,)), ((), ())), preferred_element_type=jnp.float32
    )


def dot_left_t(left, right):
    return lax.dot_general(
        left, right, (((0,), (0,)), ((), ())), preferred_element_type=jnp.float32
    )


def precise_left_t(left, right):
    return lax.dot_general(
        left, right, (((0,), (0,)), ((), ())), precision=PRECISE, preferred_element_type=jnp.float32
    )


def precise_right_t(left, right):
    return lax.dot_general(
        left, right, (((1,), (1,)), ((), ())), precision=PRECISE, preferred_element_type=jnp.float32
    )


def rms_scale(value):
    return lax.rsqrt(jnp.mean(value * value, axis=-1, keepdims=True) + EPSILON)


def split(value):
    high = value.astype(jnp.bfloat16)
    return high, (value - high.astype(jnp.float32)).astype(jnp.bfloat16)


def nn(left, right):
    return jnp.dot(left, right, preferred_element_type=jnp.float32)


def nt(left, right):
    return lax.dot_general(
        left, right, (((1,), (1,)), ((), ())), preferred_element_type=jnp.float32
    )


def two(product, left, right):
    high, low = split(right)
    return product(left, high) + product(left, low)


def three(product, left, right):
    left_high, left_low = split(left)
    right_high, right_low = split(right)
    return product(left_high, right_high) + (
        product(left_low, right_high) + product(left_high, right_low)
    )


def row_blocks(value):
    return [value[r : r + 8] for r in range(0, value.shape[0], 8)]


def exact_dot(left, right):
    return jnp.dot(left, right, precision=PRECISE, preferred_element_type=jnp.float32)


def triangle(size, upper):
    row = lax.broadcasted_iota(jnp.int32, (size, size), 0)
    column = lax.broadcasted_iota(jnp.int32, (size, size), 1)
    keep = row <= column if upper else row >= column
    return jnp.where(keep, 1.0, 0.0)


def spans(running, docs, span_s):
    size = running.shape[0]
    run, doc = row_blocks(running), row_blocks(docs)
    place = lax.broadcasted_iota(jnp.int32, (8, running.shape[1]), 0)
    for j in range(size):
        for r in range(j // 8, size // 8):
            ok = doc[r] == docs[j : j + 1]
            if r == j // 8 and j % 8:
                ok = ok & (place >= j % 8)
            span_s[j, 8 * r : 8 * r + 8] = jnp.where(ok, jnp.exp(run[r] - running[j : j + 1]), 0.0)


def to_end(running, docs):
    last = running.shape[0] - 1
    return jnp.where(
        docs == docs[last : last + 1], jnp.exp(running[last : last + 1] - running), 0.0
    )


def turned(to_end_weights, kept):
    size, slots = to_end_weights.shape
    fill = jnp.broadcast_to(kept, (128 - size, slots))
    both = jnp.concatenate([to_end_weights, fill], axis=0).T
    return both[:, :size], both[:, size : size + 1]


def read_kernel(
    q_ref, k_ref, v_ref, log_ref, new_ref, doc_ref, prev_ref, kin_ref, vin_ref,
    read_ref, score_ref, prob_ref, ks_ref, vs_ref, span_s,
):
    size = span_s.shape[0]
    lower = triangle(size, False)
    scaling = q_ref.shape[1] ** (-0.5)
    ks_ref[0] = kin_ref[...]
    vs_ref[0] = vin_ref[...]
    lane = lax.broadcasted_iota(jnp.int32, (8, size), 1)

    def chunk(i, carry):
        rows = pl.ds(pl.multiple_of(i * size, size), size)
        queries, keys, values = q_ref[rows, :], k_ref[rows, :], v_ref[rows, :]
        new, docs = new_ref[rows, :], doc_ref[rows, :]
        running = exact_dot(lower, log_ref[rows, :])
        carried = jnp.where(docs == prev_ref[rows, :], jnp.exp(running), 0.0)
        key_state, value_state = ks_ref[i], vs_ref[i]
        spans(running, docs, span_s)
        affinity = row_blocks(nt(queries, keys))
        scores = row_blocks(carried * two(nt, queries, key_state))
        for j in range(size):
            for r in range(j // 8, size // 8):
                weight = span_s[j, 8 * r : 8 * r + 8] * new[j : j + 1]
                scores[r] = scores[r] + weight * affinity[r][:, j : j + 1]
        scores = scaling * jnp.concatenate(scores, axis=0)
        probs = jnp.exp(scores - jnp.max(scores, axis=1, keepdims=True))
        probs = probs / jnp.sum(probs, axis=1, keepdims=True)
        score_ref[rows, :] = scores
        prob_ref[rows, :] = probs
        used = probs.astype(jnp.bfloat16).astype(jnp.float32)
        part = row_blocks(used)
        mixing = [jnp.zeros((8, size), jnp.float32) for _ in part]
        for j in range(size):
            for r in range(j // 8, size // 8):
                weight = span_s[j, 8 * r : 8 * r + 8] * new[j : j + 1]
                total = jnp.sum(part[r] * weight, axis=1, keepdims=True)
                mixing[r] = jnp.where(lane == j, total, mixing[r])
        high, low = split(jnp.concatenate(mixing, axis=0))
        read_ref[rows, :] = (
            three(nn, used * carried, value_state) + nn(high, values) + nn(low, values)
        )
        end, kept = turned(to_end(running, docs) * new, carried[size - 1 : size])
        high, low = split(end)
        ks_ref[i + 1] = kept * key_state + (nn(high, keys) + nn(low, keys))
        vs_ref[i + 1] = kept * value_state + (nn(high, values) + nn(low, values))
        return carry

    lax.fori_loop(0, q_ref.shape[0] // size, chunk, 0)


def back_query_kernel(
    q_ref, k_ref, v_ref, log_ref, new_ref, doc_ref, prev_ref, score_ref, prob_ref, ks_ref, vs_ref, g_ref,
    dq_ref, dk_ref, dv_ref, held_ref, gained_ref, xk_ref, xv_ref, dkin_ref, dvin_ref, span_s,
):
    size = span_s.shape[0]
    count = q_ref.shape[0] // size
    lower = triangle(size, False)
    scaling = q_ref.shape[1] ** (-0.5)
    dkin_ref[...] = jnp.zeros_like(dkin_ref)
    dvin_ref[...] = jnp.zeros_like(dvin_ref)
    lane = lax.broadcasted_iota(jnp.int32, (8, size), 1)

    def chunk(turn, carry):
        i = count - 1 - turn
        start = pl.multiple_of(i * size, size)
        rows = pl.ds(start, size)
        queries, keys, values, grads = q_ref[rows, :], k_ref[rows, :], v_ref[rows, :], g_ref[rows, :]
        new, docs = new_ref[rows, :], doc_ref[rows, :]
        running = exact_dot(lower, log_ref[rows, :])
        carried = jnp.where(docs == prev_ref[rows, :], jnp.exp(running), 0.0)
        spans(running, docs, span_s)
        affinity = row_blocks(nt(queries, keys))
        grad_high, grad_low = split(grads)
        pull = row_blocks(nt(grad_high, values) + nt(grad_low, values))
        back = row_blocks(carried * three(nt, grads, vs_ref[i]))
        for j in range(size):
            for r in range(j // 8, size // 8):
                weight = span_s[j, 8 * r : 8 * r + 8] * new[j : j + 1]
                back[r] = back[r] + weight * pull[r][:, j : j + 1]
        back = jnp.concatenate(back, axis=0)
        probs = prob_ref[rows, :]
        used = probs.astype(jnp.bfloat16).astype(jnp.float32)
        inner = probs * (back - jnp.sum(probs * back, axis=1, keepdims=True))
        gained_ref[rows, :] = inner * score_ref[rows, :] + used * back
        outer = scaling * inner
        part, used_part = row_blocks(outer), row_blocks(used)
        key_mix = [jnp.zeros((8, size), jnp.float32) for _ in part]
        value_mix = [jnp.zeros((8, size), jnp.float32) for _ in part]
        for j in range(size):
            held = None
            for r in range(j // 8, size // 8):
                span = span_s[j, 8 * r : 8 * r + 8]
                key_side, value_side = part[r] * span, used_part[r] * span
                own = key_side * affinity[r][:, j : j + 1] + value_side * pull[r][:, j : j + 1]
                held = own if held is None else held + own
                fresh = new[j : j + 1]
                key_mix[r] = jnp.where(
                    lane == j, jnp.sum(key_side * fresh, axis=1, keepdims=True), key_mix[r]
                )
                value_mix[r] = jnp.where(
                    lane == j, jnp.sum(value_side * fresh, axis=1, keepdims=True), value_mix[r]
                )
            held_ref[pl.ds(start + j, 1), :] = jnp.sum(held, axis=0, keepdims=True)
        key_mix = jnp.concatenate(key_mix, axis=0)
        value_mix = jnp.concatenate(value_mix, axis=0)
        outer_in, used_in = outer * carried, used * carried
        high, low = split(key_mix)
        dq_ref[rows, :] = three(nn, outer_in, ks_ref[i]) + (nn(high, keys) + nn(low, keys))
        fill = jnp.zeros((128 - size, size), jnp.float32)
        high, low = split(jnp.concatenate([key_mix, fill], axis=0).T[:, :size])
        dk_ref[rows, :] = nn(high, queries) + nn(low, queries)
        mixed = jnp.concatenate([value_mix, fill], axis=0).T[:, :size]
        dv_ref[rows, :] = three(nn, mixed, grads)
        outer_t, kept = turned(outer_in, carried[size - 1 : size])
        used_t, kept = turned(used_in, carried[size - 1 : size])
        high, low = split(outer_t)
        to_key = nn(high, queries) + nn(low, queries)
        to_value = three(nn, used_t, grads)
        xk_ref[i] = to_key
        xv_ref[i] = to_value
        dkin_ref[...] = kept * dkin_ref[...] + to_key
        dvin_ref[...] = kept * dvin_ref[...] + to_value
        return carry

    lax.fori_loop(0, count, chunk, 0)


def back_key_kernel(
    k_ref, v_ref, log_ref, new_ref, doc_ref, prev_ref, dk_in_ref, dv_in_ref, held_ref, gained_ref,
    xk_ref, xv_ref, dkend_ref, dvend_ref, total_ref,
    dk_ref, dv_ref, dlog_ref, ks, vs, total,
):
    size = CHUNK
    count = k_ref.shape[0] // size
    lower, upper = triangle(size, False), triangle(size, True)
    ks[...] = dkend_ref[...]
    vs[...] = dvend_ref[...]
    total[...] = total_ref[...]

    def chunk(turn, carry):
        i = count - 1 - turn
        rows = pl.ds(pl.multiple_of(i * size, size), size)
        keys, values = k_ref[rows, :], v_ref[rows, :]
        logs, new, docs = log_ref[rows, :], new_ref[rows, :], doc_ref[rows, :]
        running = exact_dot(lower, logs)
        carried = jnp.where(docs == prev_ref[rows, :], jnp.exp(running), 0.0)
        end = to_end(running, docs)
        weight = end * new
        dk_ref[rows, :] = (dk_in_ref[rows, :] + three(nn, weight, ks[...])).astype(dk_ref.dtype)
        dv_ref[rows, :] = (dv_in_ref[rows, :] + three(nn, weight, vs[...])).astype(dv_ref.dtype)
        held = held_ref[rows, :] + end * (two(nt, keys, ks[...]) + two(nt, values, vs[...]))
        change = gained_ref[rows, :] - new * held
        after = exact_dot(upper, change) + total[...]
        dlog_ref[rows, :] = after - jnp.exp(logs) * held
        total[...] = after[:1]
        unused, kept = turned(carried, carried[size - 1 : size])
        ks[...] = kept * ks[...] + xk_ref[i]
        vs[...] = kept * vs[...] + xv_ref[i]
        return carry

    lax.fori_loop(0, count, chunk, 0)


def cost(flops, moved):
    return pl.CostEstimate(flops=flops, bytes_accessed=moved, transcendentals=0)


def read_slots(queries, keys, values, logs, new, docs, prev, key_in, value_in):
    rows, width = queries.shape
    slots = logs.shape[1]
    count = rows // CHUNK
    f32 = jnp.float32
    return pl.pallas_call(
        read_kernel,
        out_shape=(
            jax.ShapeDtypeStruct((rows, width), f32),
            jax.ShapeDtypeStruct((rows, slots), f32),
            jax.ShapeDtypeStruct((rows, slots), f32),
            jax.ShapeDtypeStruct((count + 1, slots, width), f32),
            jax.ShapeDtypeStruct((count + 1, slots, width), f32),
        ),
        scratch_shapes=[pltpu.VMEM((CHUNK, CHUNK, slots), f32)],
        compiler_params=pltpu.CompilerParams(vmem_limit_bytes=VMEM),
        cost_estimate=cost(READ_COST, 5 << 20),
    )(queries, keys, values, logs, new, docs, prev, key_in, value_in)


def back_query(queries, keys, values, logs, new, docs, prev, scores, probs, key_states, value_states, grads):
    rows, width = queries.shape
    slots = logs.shape[1]
    count = rows // CHUNK
    f32 = jnp.float32
    narrow = jax.ShapeDtypeStruct((rows, slots), f32)
    wide = jax.ShapeDtypeStruct((rows, width), f32)
    states = jax.ShapeDtypeStruct((count, slots, width), f32)
    state = jax.ShapeDtypeStruct((slots, width), f32)
    return pl.pallas_call(
        back_query_kernel,
        out_shape=(wide, wide, wide, narrow, narrow, states, states, state, state),
        scratch_shapes=[pltpu.VMEM((CHUNK, CHUNK, slots), f32)],
        compiler_params=pltpu.CompilerParams(vmem_limit_bytes=VMEM),
        cost_estimate=cost(BACK_COST, 10 << 20),
    )(queries, keys, values, logs, new, docs, prev, scores, probs, key_states, value_states, grads)


def back_key(keys, values, logs, new, docs, prev, dk, dv, held, gained, xk, xv, dk_end, dv_end, total):
    rows, width = keys.shape
    slots = logs.shape[1]
    f32 = jnp.float32
    wide = jax.ShapeDtypeStruct((rows, width), jnp.bfloat16)
    return pl.pallas_call(
        back_key_kernel,
        out_shape=(wide, wide, jax.ShapeDtypeStruct((rows, slots), f32)),
        scratch_shapes=[
            pltpu.VMEM((slots, width), f32),
            pltpu.VMEM((slots, width), f32),
            pltpu.VMEM((1, slots), f32),
        ],
        compiler_params=pltpu.CompilerParams(vmem_limit_bytes=VMEM),
        cost_estimate=cost(READ_COST, 8 << 20),
    )(keys, values, logs, new, docs, prev, dk, dv, held, gained, xk, xv, dk_end, dv_end, total)


def compose(earlier, later):
    factor = later[0][:, None]
    return (earlier[0] * later[0], factor * earlier[1] + later[1], factor * earlier[2] + later[2])


def body(
    stream,
    seg_ids,
    attn_gain,
    w_query,
    w_key,
    w_value,
    w_outgate,
    w_low,
    w_slot,
    forget_bias,
    head_gain,
    w_out,
    mlp_gain,
    w_gate,
    w_up,
    w_down,
    cotangent,
):
    tok_rows = stream.shape[0]
    width = stream.shape[1]
    slots = w_slot.shape[2]
    head_width = w_query.shape[1]
    prior = passed_along(seg_ids[tok_rows - 1 :], "seq", 1)[0]
    stream_f = stream.astype(jnp.float32)
    scale_in = rms_scale(stream_f)
    normed_in = (stream_f * scale_in * attn_gain).astype(jnp.bfloat16)
    query_rows = plain_dot(normed_in, w_query).astype(jnp.bfloat16)
    key_rows = plain_dot(normed_in, w_key).astype(jnp.bfloat16)
    value_rows = plain_dot(normed_in, w_value).astype(jnp.bfloat16)
    gate_act = plain_dot(normed_in, w_outgate)
    ranked = plain_dot(normed_in, w_low)

    def decay_logs(ranked_in, slot_map, bias_row):
        return jax.nn.log_sigmoid(precise_dot(ranked_in, slot_map[0]) + bias_row[0]) / GATE_NORM

    log_decay, gate_pull = jax.vjp(decay_logs, ranked, w_slot, forget_bias)

    new = -jnp.expm1(log_decay)
    last_doc = seg_ids[tok_rows - 1]
    running = precise_dot(jnp.tril(jnp.ones((tok_rows, tok_rows), jnp.float32)), log_decay)
    total = running[tok_rows - 1]
    in_last = (seg_ids == last_doc)[:, None]
    factor = jnp.where(in_last, jnp.exp(jnp.where(in_last, total - running, 0.0)) * new, 0.0)
    docs = seg_ids.astype(jnp.float32)
    before = jnp.concatenate([prior.astype(jnp.float32)[None], docs[CHUNK - 1 : -1 : CHUNK]])
    docs = jnp.broadcast_to(docs[:, None], (tok_rows, slots))
    before = jnp.broadcast_to(jnp.repeat(before, CHUNK)[:, None], (tok_rows, slots))

    chunk = tok_rows // CHUNKS

    def over_heads(product):
        return head_sum(
            [product(lambda a, i=i: a[i * chunk : (i + 1) * chunk]) for i in range(CHUNKS)]
        )

    zero_state = jnp.zeros((slots, head_width), jnp.float32)
    local_key = precise_left_t(factor, key_rows.astype(jnp.float32))
    local_value = precise_left_t(factor, value_rows.astype(jnp.float32))
    decay_all = jnp.where(last_doc == prior, jnp.exp(total), 0.0)
    identity = (jnp.ones((slots,), jnp.float32), zero_state, zero_state)
    prefix = entering((decay_all, local_key, local_value), "seq", compose, identity, False)
    slot_read, scores, probs, key_states, value_states = read_slots(
        query_rows, key_rows, value_rows, log_decay, new, docs, before, prefix[1], prefix[2]
    )
    scale_read = rms_scale(slot_read)
    normed_read = slot_read * scale_read * head_gain[0]
    gate_sig = jax.nn.sigmoid(gate_act)
    gate_silu = gate_act * gate_sig
    mixed_heads = (normed_read * gate_silu).astype(jnp.bfloat16)
    branch = over_heads(lambda rows: plain_dot(rows(mixed_heads), w_out))
    hidden = stream_f + branch
    scale_mid = rms_scale(hidden)
    normed_mid = (hidden * scale_mid * mlp_gain).astype(jnp.bfloat16)
    gate_pre = plain_dot(normed_mid, w_gate)
    up_pre = plain_dot(normed_mid, w_up)
    pre_sig = jax.nn.sigmoid(gate_pre)
    pre_silu = gate_pre * pre_sig
    ffn_act = (pre_silu * up_pre).astype(jnp.bfloat16)
    ffn_out = over_heads(lambda rows: plain_dot(rows(ffn_act), w_down))
    result = hidden + ffn_out
    square_sums = lax.psum(
        jnp.stack(
            [jnp.sum(stream_f * stream_f), jnp.sum(hidden * hidden), jnp.sum(result * result)]
        ),
        "seq",
    )
    stream_rms = jnp.sqrt(square_sums / (tok_rows * lax.axis_size("seq") * width))
    upstream = cotangent.astype(jnp.float32)
    d_act = dot_right_t(cotangent, w_down)
    grad_down = seq_sum(width_blocks(cotangent), ffn_act, False)
    d_gate = (d_act * up_pre * pre_sig * (1.0 + gate_pre * (1.0 - pre_sig))).astype(jnp.bfloat16)
    d_up = (d_act * pre_silu).astype(jnp.bfloat16)
    d_mid = over_heads(
        lambda rows: dot_right_t(rows(d_gate), w_gate) + dot_right_t(rows(d_up), w_up)
    )
    wide_mid = width_blocks(normed_mid)
    grad_gate = seq_sum(wide_mid, d_gate, True)
    grad_up = seq_sum(wide_mid, d_up, True)
    grad_mlp_gain = jnp.sum(d_mid * hidden * scale_mid, axis=0)
    scaled_mid = d_mid * mlp_gain
    d_hidden = (
        upstream
        + scale_mid * scaled_mid
        - hidden * scale_mid**3 * jnp.mean(scaled_mid * hidden, axis=1, keepdims=True)
    )
    d_branch = d_hidden.astype(jnp.bfloat16)
    d_mixed = dot_right_t(d_branch, w_out)
    grad_out = seq_sum(width_blocks(d_branch), mixed_heads, False)
    d_gate_act = (d_mixed * normed_read * gate_sig * (1.0 + gate_act * (1.0 - gate_sig))).astype(
        jnp.bfloat16
    )
    d_normed = d_mixed * gate_silu
    grad_head_gain = jnp.sum(d_normed * slot_read * scale_read, axis=0)[None, :]
    scaled_read = d_normed * head_gain[0]
    d_read = scale_read * scaled_read - slot_read * scale_read**3 * jnp.mean(
        scaled_read * slot_read, axis=1, keepdims=True
    )
    d_query, d_key, d_value, held, gained, to_keys, to_values, key_back, value_back = back_query(
        query_rows, key_rows, value_rows, log_decay, new, docs, before, scores, probs, key_states, value_states, d_read
    )
    query_back = d_query.astype(jnp.bfloat16)
    suffix = entering((decay_all, key_back, value_back), "seq", compose, identity, True)
    end_total = jnp.sum(key_states[-1] * suffix[1] + value_states[-1] * suffix[2], axis=1)[None, :]
    key_back, value_back, d_logs = back_key(
        key_rows, value_rows, log_decay, new, docs, before, d_key, d_value, held, gained,
        to_keys, to_values, suffix[1], suffix[2], end_total,
    )
    d_ranked, grad_slot, grad_bias = gate_pull(d_logs)
    normed_f = normed_in.astype(jnp.float32)
    grad_low = precise_left_t(normed_f, d_ranked)
    wide_in = width_blocks(normed_in)
    grad_outgate = seq_sum(wide_in, d_gate_act, True)
    grad_query = seq_sum(wide_in, query_back, True)
    grad_key = seq_sum(wide_in, key_back, True)
    grad_value = seq_sum(wide_in, value_back, True)
    d_in = over_heads(
        lambda rows: dot_right_t(rows(query_back), w_query)
        + dot_right_t(rows(key_back), w_key)
        + dot_right_t(rows(value_back), w_value)
        + dot_right_t(rows(d_gate_act), w_outgate)
        + precise_right_t(rows(d_ranked), w_low.astype(jnp.float32))
    )
    grad_attn_gain = jnp.sum(d_in * stream_f * scale_in, axis=0)
    scaled_in = d_in * attn_gain
    grad_stream = (
        d_hidden
        + scale_in * scaled_in
        - stream_f * scale_in**3 * jnp.mean(scaled_in * stream_f, axis=1, keepdims=True)
    ).astype(jnp.bfloat16)
    count = lax.axis_size("seq")
    small = [
        grad_attn_gain.reshape(count, -1),
        grad_mlp_gain.reshape(count, -1),
        grad_low.reshape(count, -1),
        jnp.moveaxis(grad_slot[0].reshape(-1, count, slots // count), 1, 0).reshape(count, -1),
        grad_bias.reshape(count, -1),
        grad_head_gain.reshape(count, -1),
    ]
    sizes = [a.shape[1] for a in small]
    packed = jnp.concatenate(small, axis=1)
    packed = jnp.pad(packed, ((0, 0), (0, -packed.shape[1] % 128)))
    packed = lax.psum_scatter(packed, "seq", scatter_dimension=0, tiled=True)[0]
    ends = [sum(sizes[: i + 1]) for i in range(len(sizes))]
    small = [packed[end - size : end] for end, size in zip(ends, sizes)]
    summed = (
        small[0],
        grad_query,
        grad_key,
        grad_value,
        grad_outgate,
        small[2].reshape(width // count, -1),
        small[3].reshape(1, -1, slots // count),
        small[4][None, :],
        small[5][None, :],
        grad_out,
        small[1],
        grad_gate,
        grad_up,
        grad_down,
    )
    mixer_parts = summed[:10]
    ffn_parts = summed[10:]
    return (
        result.astype(jnp.bfloat16),
        grad_stream,
        mixer_parts[0],
        mixer_parts[1],
        mixer_parts[2],
        mixer_parts[3],
        mixer_parts[4],
        mixer_parts[5],
        mixer_parts[6],
        mixer_parts[7],
        mixer_parts[8],
        mixer_parts[9],
        ffn_parts[0],
        ffn_parts[1],
        ffn_parts[2],
        ffn_parts[3],
        stream_rms,
    )


def solution(mesh):
    in_specs = (
        P("seq", None),
        P("seq"),
        P(),
        P(None, "head"),
        P(None, "head"),
        P(None, "head"),
        P(None, "head"),
        P(None, "head"),
        P("head", None, None),
        P("head", None),
        P("head", None),
        P("head", None),
        P(),
        P(None, "head"),
        P(None, "head"),
        P("head", None),
        P("seq", None),
    )
    out_specs = (
        P("seq", None),
        P("seq", None),
        P("seq"),
        P("seq", "head"),
        P("seq", "head"),
        P("seq", "head"),
        P("seq", "head"),
        P("seq", "head"),
        P("head", None, "seq"),
        P("head", "seq"),
        P("head", "seq"),
        P("head", "seq"),
        P("seq"),
        P("seq", "head"),
        P("seq", "head"),
        P("head", "seq"),
        P(),
    )
    return jax.shard_map(body, mesh=mesh, in_specs=in_specs, out_specs=out_specs, check_vma=False)
```

time: 2110 us -> 1390 us (0.66)
  waiting for transfers between devices: 1430 us -> 858 us
  matrix products: 329 us -> 117 us
  starting transfers between devices: 7.23 us -> 143 us
  other arithmetic: 155 us -> 98.3 us
  Pallas kernels: 0 us -> 47.5 us
  blocking collectives: 56.7 us -> 20.7 us
  local copies, waits for them, and re-layouts: 103 us -> 79.5 us
    reduce_scatter x9 -> x0, waiting for transfers between devices: 1060 us -> none  [the longest x1 197 us: body(): lax.psum_scatter(grad_up, 'seq', scatter_dimension=0, tiled=True)]
    ppermute x0 -> x60, waiting for transfers between devices: none -> 763 us  [the longest x24 603 us: moved(): lax.ppermute(array, 'seq', [(2 * a + x, 2 * b + x) for a, b in pairs for...]
    psum x3 -> x0, waiting for transfers between devices: 238 us -> none  [the longest x1 119 us: body(): ffn_out = lax.psum(plain_dot(ffn_act, w_down), 'head')]
    all_gather x4 -> x0, waiting for transfers between devices: 124 us -> none  [entering(): gathered = jax.tree.map(lambda a: lax.all_gather(a, axis), part)]
    ppermute x1 -> x23, waiting for transfers between devices: 0.01 us -> 95.3 us  [passed_along(): return lax.ppermute(array, axis, pairs)]
    dot_general x32, matrix products: 139 us -> 55.4 us  [product(): jnp.einsum(rule, w[lo:hi], n, preferred_element_type=jnp.float32)]
    ppermute x0 -> x60, starting transfers between devices: none -> 83.8 us  [the longest x24 47.7 us: moved(): lax.ppermute(array, 'seq', [(2 * a + x, 2 * b + x) for a, b in pairs for...]
    unnamed x2 -> x0, blocking collectives: 56.7 us -> none
  transfers between devices with their start and end apart: 18 -> 84, of which waited for: 16 -> 33; matrix products, arithmetic and copies ran while one was open for 6% -> 18% of each run, Pallas kernels for 0% -> 3%
where the time goes in v1:
time: 1390 us; the launch traced here: 1380 us
  waiting for transfers between devices  858 us (62%)
  starting transfers between devices  143 us (10%)
  matrix products  117 us (8%)
  other arithmetic  98.3 us (7%)
  local copies, waits for them, and re-layouts  79.5 us (6%)
  Pallas kernels  47.5 us (3%)
  blocking collectives  20.7 us (1%)
  between operations  18.9 us (1%)
    ppermute x24, waiting for transfers between devices, moved(): lax.ppermute(array, 'seq', [(2 * a + x, 2 * b + x) for a, b in pairs for...  603 us
    ppermute x36, waiting for transfers between devices, swapped(): lax.ppermute(array, axis, [(i, i ^ by) for i in range(lax.axis_size(axis))])  160 us
    ppermute x23, waiting for transfers between devices, passed_along(): return lax.ppermute(array, axis, pairs)  95.3 us
    ppermute x23, starting transfers between devices, passed_along(): return lax.ppermute(array, axis, pairs)  59.5 us
    dot_general x32, matrix products, product(): jnp.einsum(rule, w[lo:hi], n, preferred_element_type=jnp.float32)  55.4 us
    ppermute x24, starting transfers between devices, moved(): lax.ppermute(array, 'seq', [(2 * a + x, 2 * b + x) for a, b in pairs for...  47.7 us
    ppermute x36, starting transfers between devices, swapped(): lax.ppermute(array, axis, [(i, i ^ by) for i in range(lax.axis_size(axis))])  36.1 us
    another operation x21, local copies, waits for them, and re-layouts, blocks(): jnp.stack([lax.dynamic_slice_in_dim(array, (2 * r + parity) * wide, wide,...  32.1 us
  transfers between devices with their start and end apart: 84, of which 33 were waited for; matrix products, arithmetic and copies ran while one was open for 18% of the time, Pallas kernels for 3%

profile of v1, /device:TPU:0, one launch (start us, length us, event | category | flops | bytes accessed | tf_op | source)
XLA Modules:
  0.0 1382.6 jit_solution(5551106670123273763)
XLA Ops:
  76.8 12.2 shard_map.296
  123.2 45.0 %collective-permute-done.30 = f32[64]{0:T(128)S(1)} collective-permute-done((f32[64]{0:T(128)S(1)}, f32[64]{0:T(128)S(1)}, u32[]{:S(2)}, u32[]{:S(2)}) %collective-permute-start.30) | collective-permute-done | bytes 288 | tf_op jit(solution)/shard_map/ppermute | solution.py:23
  255.1 14.3 %collective-permute-done.22 = f32[96,2048]{1,0:T(8,128)S(1)} collective-permute-done((f32[96,2048]{1,0:T(8,128)S(1)}, f32[96,2048]{1,0:T(8,128)S(1)}, u32[]{:S(2)}, u32[]{:S(2)}) %collective-permute-start.22) | collective-permute-done | bytes 786464 | tf_op jit(solution)/shard_map/ppermute | solution.py:27
  272.2 14.1 %collective-permute-done.19 = f32[96,2048]{1,0:T(8,128)S(1)} collective-permute-done((f32[96,2048]{1,0:T(8,128)S(1)}, f32[96,2048]{1,0:T(8,128)S(1)}, u32[]{:S(2)}, u32[]{:S(2)}) %collective-permute-start.19) | collective-permute-done | bytes 786464 | tf_op jit(solution)/shard_map/ppermute | solution.py:27
  289.2 14.0 %collective-permute-done.28 = f32[96,2048]{1,0:T(8,128)S(1)} collective-permute-done((f32[96,2048]{1,0:T(8,128)S(1)}, f32[96,2048]{1,0:T(8,128)S(1)}, u32[]{:S(2)}, u32[]{:S(2)}) %collective-permute-start.28) | collective-permute-done | bytes 786464 | tf_op jit(solution)/shard_map/ppermute | solution.py:27
  332.7 41.4 %collective-permute-done.74 = f32[384,1408]{1,0:T(8,128)S(1)} collective-permute-done((f32[384,1408]{1,0:T(8,128)S(1)}, f32[384,1408]{1,0:T(8,128)S(1)}, u32[]{:S(2)}, u32[]{:S(2)}) %collective-permute-start.74) | collective-permute-done | bytes 2162720 | tf_op jit(solution)/shard_map/ppermute | solution.py:27
  377.4 43.0 %collective-permute-done.78 = f32[384,1408]{1,0:T(8,128)S(1)} collective-permute-done((f32[384,1408]{1,0:T(8,128)S(1)}, f32[384,1408]{1,0:T(8,128)S(1)}, u32[]{:S(2)}, u32[]{:S(2)}) %collective-permute-start.78) | collective-permute-done | bytes 2162720 | tf_op jit(solution)/shard_map/ppermute | solution.py:27
  438.7 25.8 %shard_map.297 = (f32[384,512]{1,0:T(8,128)S(1)}, f32[384,512]{1,0:T(8,128)S(1)}, f32[384,512]{1,0:T(8,128)S(1)}, f32[384,64]{1,0:T(8,128)S(1)}, f32[384,64]{1,0...) custom-call(bf16[384,512]{1,0:T(8,128)(2,1)S(1)} %copy-done.12, ...), custom_call_target="tpu_custom_call" | custom-call | flops 36507222016 | bytes 10485760 | tf_op jit(solution)/shard_map/pallas_call | solution.py:429
  498.6 19.7 %collective-permute-done.34 = f32[64,512]{1,0:T(8,128)S(1)} collective-permute-done((f32[64,512]{1,0:T(8,128)S(1)}, f32[64,512]{1,0:T(8,128)S(1)}, u32[]{:S(2)}, u32[]{:S(2)}) %collective-permute-start.34) | collective-permute-done | bytes 131104 | tf_op jit(solution)/shard_map/ppermute | solution.py:23
  540.5 10.4 collective-permute-done.40
  553.9 9.4 shard_map.298
  595.0 10.5 collective-permute-done.52
  608.5 12.0 collective-permute-done.56
  649.4 10.8 collective-permute-done.61
  662.9 30.9 %collective-permute-done.53 = f32[3,256,512]{2,1,0:T(8,128)} collective-permute-done((f32[3,256,512]{2,1,0:T(8,128)S(1)}, f32[3,256,512]{2,1,0:T(8,128)}, u32[]{:S(2)}, u32[]{:S(2)}) %collective-permute-start.53) | collective-permute-done | bytes 1572896 | tf_op jit(solution)/shard_map/ppermute | solution.py:114
  702.7 24.9 %collective-permute-done.57 = f32[3,256,512]{2,1,0:T(8,128)} collective-permute-done((f32[3,256,512]{2,1,0:T(8,128)}, f32[3,256,512]{2,1,0:T(8,128)}, u32[]{:S(2)}, u32[]{:S(2)}) %collective-permute-start.57) | collective-permute-done | bytes 1572896 | tf_op jit(solution)/shard_map/ppermute | solution.py:114
  743.3 298.8 %collective-permute-done.66 = f32[3,512,256]{2,1,0:T(8,128)} collective-permute-done((f32[3,512,256]{2,1,0:T(8,128)}, f32[3,512,256]{2,1,0:T(8,128)}, u32[]{:S(2)}, u32[]{:S(2)}) %collective-permute-start.66) | collective-permute-done | bytes 1572896 | tf_op jit(solution)/shard_map/ppermute | solution.py:114
  1048.5 20.7 %psum.7 = f32[3]{0:T(128)S(1)} all-reduce(f32[3]{0:T(128)S(1)} %pad_maximum_fusion.7), channel_id=1, replica_groups=mesh['seq'=8,'head'=4] {'seq'}, use_global_device_ids=true, to_apply=%region_15.16 | all-reduce | flops 3 | bytes 24 | tf_op jit(solution)/shard_map/psum | solution.py:542
  1099.6 33.6 %collective-permute-done.51 = f32[1,256,512]{2,1,0:T(8,128)S(1)} collective-permute-done((f32[1,256,512]{2,1,0:T(8,128)S(1)}, f32[1,256,512]{2,1,0:T(8,128)S(1)}, u32[]{:S(2)}, u32[]{:S(2)}) %collective-permute-start.51) | collective-permute-done | bytes 524320 | tf_op jit(solution)/shard_map/ppermute | solution.py:114
  1138.2 10.1 collective-permute-done.63
  1178.7 62.0 %collective-permute-done.68 = f32[1,512,256]{2,1,0:T(8,128)S(1)} collective-permute-done((f32[1,512,256]{2,1,0:T(8,128)S(1)}, f32[1,512,256]{2,1,0:T(8,128)S(1)}, u32[]{:S(2)}, u32[]{:S(2)}) %collective-permute-start.68) | collective-permute-done | bytes 524320 | tf_op jit(solution)/shard_map/ppermute | solution.py:114
  1246.0 12.2 collective-permute-done.73
  1261.3 49.0 %collective-permute-done.77 = f32[1,256,1408]{2,1,0:T(8,128)S(1)} collective-permute-done((f32[1,256,1408]{2,1,0:T(8,128)S(1)}, f32[1,256,1408]{2,1,0:T(8,128)S(1)}, u32[]{:S(2)}, u32[]{:S(2)}) %collective-permute-start.77) | collective-permute-done | bytes 1441824 | tf_op jit(solution)/shard_map/ppermute | solution.py:114
  1313.1 58.9 %collective-permute-done.82 = f32[1,1408,256]{2,1,0:T(8,128)S(1)} collective-permute-done((f32[1,1408,256]{2,1,0:T(8,128)S(1)}, f32[1,1408,256]{2,1,0:T(8,128)S(1)}, u32[]{:S(2)}, u32[]{:S(2)}) %collective-permute-start.82) | collective-permute-done | bytes 1441824 | tf_op jit(solution)/shard_map/ppermute | solution.py:114
  (669 shorter events, 480.1 us)
Async XLA Ops:
  7.2 1062.5 %all-reduce.4.cloned.1.call-start = ((), (), s32[]{:S(2)}) async-start(), calls=%async_computation | async-start | bytes 311296
  97.4 86.4 %collective-permute-start.47 = (f32[4,384,256]{1,2,0:T(8,128)}, f32[4,384,256]{1,2,0:T(8,128)}, u32[]{:S(2)}, u32[]{:S(2)}) collective-permute-start(f32[4,384,256]{1,2,0:T(8,128)} %maximum_convert_fusion), channel_id=1, source_target_pairs={{0,4},{4,0},{8,12},{12,8},{16,20},{20,16},{24,28},{28,24},{1,5},{5... | collective-permute-start | bytes 4718600 | tf_op jit(solution)/shard_map/ppermute | solution.py:27
  108.5 79.3 %collective-permute-start.79 = (f32[4,384,256]{1,2,0:T(8,128)}, f32[4,384,256]{1,2,0:T(8,128)}, u32[]{:S(2)}, u32[]{:S(2)}) collective-permute-start(f32[4,384,256]{1,2,0:T(8,128)} %maximum_convert_fusion.3), channel_id=1, source_target_pairs={{0,4},{4,0},{8,12},{12,8},{16,20},{20,16},{24,28},{28,24},{1,5},{5... | collective-permute-start | bytes 4718600 | tf_op jit(solution)/shard_map/ppermute | solution.py:27
  244.0 80.2 %collective-permute-start.69 = (f32[4,384,256]{1,2,0:T(8,128)S(1)}, f32[4,384,256]{1,2,0:T(8,128)S(1)}, u32[]{:S(2)}, u32[]{:S(2)}) collective-permute-start(f32[4,384,256]{1,2,0:T(8,128)S(1)} %maximum_convert_fusion.2), channel_id=1, source_target_pairs={{0,4},{4,0},{8,12},{12,8},{16,20},{20,16},{24,28},{28,24},{1,5},{5... | collective-permute-start | bytes 4718600 | tf_op jit(solution)/shard_map/ppermute | solution.py:27
  247.0 80.7 %collective-permute-start.70 = (f32[384,1408]{1,0:T(8,128)S(1)}, f32[384,1408]{1,0:T(8,128)S(1)}, u32[]{:S(2)}, u32[]{:S(2)}) collective-permute-start(f32[384,1408]{1,0:T(8,128)S(1)} %copy-done.138), channel_id=1, source_target_pairs={{0,4},{4,0},{8,12},{12,8},{16,20},{20,16},{24,28},{28,24},{1,5},{5... | collective-permute-start | bytes 6488072 | tf_op jit(solution)/shard_map/ppermute | solution.py:27
  253.5 120.5 %collective-permute-start.74 = (f32[384,1408]{1,0:T(8,128)S(1)}, f32[384,1408]{1,0:T(8,128)S(1)}, u32[]{:S(2)}, u32[]{:S(2)}) collective-permute-start(f32[384,1408]{1,0:T(8,128)S(1)} %copy-done.137), channel_id=1, source_target_pairs={{0,4},{4,0},{8,12},{12,8},{16,20},{20,16},{24,28},{28,24},{1,5},{5... | collective-permute-start | bytes 6488072 | tf_op jit(solution)/shard_map/ppermute | solution.py:27
  303.1 117.3 %collective-permute-start.78 = (f32[384,1408]{1,0:T(8,128)S(1)}, f32[384,1408]{1,0:T(8,128)S(1)}, u32[]{:S(2)}, u32[]{:S(2)}) collective-permute-start(f32[384,1408]{1,0:T(8,128)S(1)} %copy-done.136), channel_id=1, source_target_pairs={{0,4},{4,0},{8,12},{12,8},{16,20},{20,16},{24,28},{28,24},{1,5},{5... | collective-permute-start | bytes 6488072 | tf_op jit(solution)/shard_map/ppermute | solution.py:27
  318.5 271.5 %collective-permute-start.64 = (f32[384,512]{1,0:T(8,128)}, f32[384,512]{1,0:T(8,128)}, u32[]{:S(2)}, u32[]{:S(2)}) collective-permute-start(f32[384,512]{1,0:T(8,128)} %get-tuple-element.119), channel_id=1, source_target_pairs={{0,4},{4,0},{8,12},{12,8},{16,20},{20,16},{24,28},{28,24},{1,5},{5... | collective-permute-start | bytes 2359304 | tf_op jit(solution)/shard_map/ppermute | solution.py:27
  324.3 101.2 %collective-permute-start.23 = (f32[96,2048]{1,0:T(8,128)S(1)}, f32[96,2048]{1,0:T(8,128)S(1)}, u32[]{:S(2)}, u32[]{:S(2)}) collective-permute-start(f32[96,2048]{1,0:T(8,128)S(1)} %add.595), channel_id=1, source_target_pairs={{0,1},{1,0},{2,3},{3,2},{4,5},{5,4},{6,7},{7,6},{8,9},{9,8},{10,11... | collective-permute-start | bytes 2359304 | tf_op jit(solution)/shard_map/ppermute | solution.py:27
  327.7 97.9 %collective-permute-start.20 = (f32[96,2048]{1,0:T(8,128)S(1)}, f32[96,2048]{1,0:T(8,128)S(1)}, u32[]{:S(2)}, u32[]{:S(2)}) collective-permute-start(f32[96,2048]{1,0:T(8,128)S(1)} %add.593), channel_id=1, source_target_pairs={{0,1},{1,0},{2,3},{3,2},{4,5},{5,4},{6,7},{7,6},{8,9},{9,8},{10,11... | collective-permute-start | bytes 2359304 | tf_op jit(solution)/shard_map/ppermute | solution.py:27
  474.5 106.1 %collective-permute-start.48 = (f32[384,512]{1,0:T(8,128)}, f32[384,512]{1,0:T(8,128)}, u32[]{:S(2)}, u32[]{:S(2)}) collective-permute-start(f32[384,512]{1,0:T(8,128)} %get-tuple-element.123), channel_id=1, source_target_pairs={{0,4},{4,0},{8,12},{12,8},{16,20},{20,16},{24,28},{28,24},{1,5},{5... | collective-permute-start | bytes 2359304 | tf_op jit(solution)/shard_map/ppermute | solution.py:27
  482.6 102.4 %collective-permute-start.60 = (f32[384,512]{1,0:T(8,128)}, f32[384,512]{1,0:T(8,128)}, u32[]{:S(2)}, u32[]{:S(2)}) collective-permute-start(f32[384,512]{1,0:T(8,128)} %get-tuple-element.121), channel_id=1, source_target_pairs={{0,4},{4,0},{8,12},{12,8},{16,20},{20,16},{24,28},{28,24},{1,5},{5... | collective-permute-start | bytes 2359304 | tf_op jit(solution)/shard_map/ppermute | solution.py:27
  627.2 100.4 %collective-permute-start.57 = (f32[3,256,512]{2,1,0:T(8,128)}, f32[3,256,512]{2,1,0:T(8,128)}, u32[]{:S(2)}, u32[]{:S(2)}) collective-permute-start(f32[3,256,512]{2,1,0:T(8,128)} %convolution_add_fusion.14), channel_id=1, source_target_pairs={{0,8},{4,12},{24,16},{28,20},{1,9},{5,13},{25,17},{29,21},{2,10},{... | collective-permute-start | bytes 4718600 | tf_op jit(solution)/shard_map/ppermute | solution.py:114
  638.6 448.4 %collective-permute-start.71 = (f32[3,256,1408]{2,1,0:T(8,128)}, f32[3,256,1408]{2,1,0:T(8,128)}, u32[]{:S(2)}, u32[]{:S(2)}) collective-permute-start(f32[3,256,1408]{2,1,0:T(8,128)} %convolution_add_fusion.1), channel_id=1, source_target_pairs={{0,8},{4,12},{24,16},{28,20},{1,9},{5,13},{25,17},{29,21},{2,10},{... | collective-permute-start | bytes 12976136 | tf_op jit(solution)/shard_map/ppermute | solution.py:114
  643.3 448.7 %collective-permute-start.75 = (f32[3,256,1408]{2,1,0:T(8,128)}, f32[3,256,1408]{2,1,0:T(8,128)}, u32[]{:S(2)}, u32[]{:S(2)}) collective-permute-start(f32[3,256,1408]{2,1,0:T(8,128)} %convolution_add_fusion), channel_id=1, source_target_pairs={{0,8},{4,12},{24,16},{28,20},{1,9},{5,13},{25,17},{29,21},{2,10},{... | collective-permute-start | bytes 12976136 | tf_op jit(solution)/shard_map/ppermute | solution.py:114
  693.8 401.8 %collective-permute-start.80 = (f32[3,1408,256]{2,1,0:T(8,128)}, f32[3,1408,256]{2,1,0:T(8,128)}, u32[]{:S(2)}, u32[]{:S(2)}) collective-permute-start(f32[3,1408,256]{2,1,0:T(8,128)} %add_bitcast_fusion), channel_id=1, source_target_pairs={{0,8},{4,12},{24,16},{28,20},{1,9},{5,13},{25,17},{29,21},{2,10},{... | collective-permute-start | bytes 12976136 | tf_op jit(solution)/shard_map/ppermute | solution.py:114
  730.3 311.7 %collective-permute-start.66 = (f32[3,512,256]{2,1,0:T(8,128)}, f32[3,512,256]{2,1,0:T(8,128)}, u32[]{:S(2)}, u32[]{:S(2)}) collective-permute-start(f32[3,512,256]{2,1,0:T(8,128)} %add_bitcast_fusion.1), channel_id=1, source_target_pairs={{0,8},{4,12},{24,16},{28,20},{1,9},{5,13},{25,17},{29,21},{2,10},{... | collective-permute-start | bytes 4718600 | tf_op jit(solution)/shard_map/ppermute | solution.py:114
  736.0 346.0 %collective-permute-start.50 = (f32[2,256,512]{2,1,0:T(8,128)}, f32[2,256,512]{2,1,0:T(8,128)}, u32[]{:S(2)}, u32[]{:S(2)}) collective-permute-start(f32[2,256,512]{2,1,0:T(8,128)} %slice_add_fusion.16), channel_id=1, source_target_pairs={{8,16},{12,20},{16,8},{20,12},{9,17},{13,21},{17,9},{21,13},{10,18... | collective-permute-start | bytes 3145736 | tf_op jit(solution)/shard_map/ppermute | solution.py:114
  1095.5 80.2 %collective-permute-start.76 = (f32[2,256,1408]{2,1,0:T(8,128)S(1)}, f32[2,256,1408]{2,1,0:T(8,128)S(1)}, u32[]{:S(2)}, u32[]{:S(2)}) collective-permute-start(f32[2,256,1408]{2,1,0:T(8,128)S(1)} %slice_add_fusion.1), channel_id=1, source_target_pairs={{8,16},{12,20},{16,8},{20,12},{9,17},{13,21},{17,9},{21,13},{10,18... | collective-permute-start | bytes 8650760 | tf_op jit(solution)/shard_map/ppermute | solution.py:114
  1134.6 108.6 %collective-permute-start.81 = (f32[2,1408,256]{2,1,0:T(8,128)S(1)}, f32[2,1408,256]{2,1,0:T(8,128)S(1)}, u32[]{:S(2)}, u32[]{:S(2)}) collective-permute-start(f32[2,1408,256]{2,1,0:T(8,128)S(1)} %slice_add_fusion), channel_id=1, source_target_pairs={{8,16},{12,20},{16,8},{20,12},{9,17},{13,21},{17,9},{21,13},{10,18... | collective-permute-start | bytes 8650760 | tf_op jit(solution)/shard_map/ppermute | solution.py:114
  1155.0 85.8 %collective-permute-start.68 = (f32[1,512,256]{2,1,0:T(8,128)S(1)}, f32[1,512,256]{2,1,0:T(8,128)S(1)}, u32[]{:S(2)}, u32[]{:S(2)}) collective-permute-start(f32[1,512,256]{2,1,0:T(8,128)S(1)} %get-tuple-element.216), channel_id=1, source_target_pairs={{8,0},{12,4},{16,24},{20,28},{9,1},{13,5},{17,25},{21,29},{10,2},{... | collective-permute-start | bytes 1572872 | tf_op jit(solution)/shard_map/ppermute | solution.py:114
  1164.5 93.7 %collective-permute-start.73 = (f32[1,256,1408]{2,1,0:T(8,128)S(1)}, f32[1,256,1408]{2,1,0:T(8,128)S(1)}, u32[]{:S(2)}, u32[]{:S(2)}) collective-permute-start(f32[1,256,1408]{2,1,0:T(8,128)S(1)} %get-tuple-element.218), channel_id=1, source_target_pairs={{8,0},{12,4},{16,24},{20,28},{9,1},{13,5},{17,25},{21,29},{10,2},{... | collective-permute-start | bytes 4325384 | tf_op jit(solution)/shard_map/ppermute | solution.py:114
  1177.4 132.9 %collective-permute-start.77 = (f32[1,256,1408]{2,1,0:T(8,128)S(1)}, f32[1,256,1408]{2,1,0:T(8,128)S(1)}, u32[]{:S(2)}, u32[]{:S(2)}) collective-permute-start(f32[1,256,1408]{2,1,0:T(8,128)S(1)} %get-tuple-element.220), channel_id=1, source_target_pairs={{8,0},{12,4},{16,24},{20,28},{9,1},{13,5},{17,25},{21,29},{10,2},{... | collective-permute-start | bytes 4325384 | tf_op jit(solution)/shard_map/ppermute | solution.py:114
  1244.7 127.4 %collective-permute-start.82 = (f32[1,1408,256]{2,1,0:T(8,128)S(1)}, f32[1,1408,256]{2,1,0:T(8,128)S(1)}, u32[]{:S(2)}, u32[]{:S(2)}) collective-permute-start(f32[1,1408,256]{2,1,0:T(8,128)S(1)} %get-tuple-element.222), channel_id=1, source_target_pairs={{8,0},{12,4},{16,24},{20,28},{9,1},{13,5},{17,25},{21,29},{10,2},{... | collective-permute-start | bytes 4325384 | tf_op jit(solution)/shard_map/ppermute | solution.py:114
  (209 other events, 3549.9 us)
Sparse Core Ops, SparseCore 0:
  741.4 69.8 all-reduce.3

commit v2 on v1

--- a/solution.py
+++ b/solution.py
@@ -1,3 +1,5 @@
+import functools
+
 import jax
 import jax.numpy as jnp
 from jax import lax
@@ -6,7 +8,8 @@
 from jax.sharding import PartitionSpec as P
 
 CHUNK = 32
-CHUNKS = 2
+CHUNKS = 4
+MESH = pl.DeviceIdType.MESH
 VMEM = 48 << 20
 READ_COST = 17 << 30
 BACK_COST = 34 << 30
@@ -23,105 +26,40 @@
     return lax.ppermute(array, axis, pairs)
 
 
-def swapped(array, axis, by):
-    return lax.ppermute(array, axis, [(i, i ^ by) for i in range(lax.axis_size(axis))])
-
-
-def entering(part, axis, combine, identity, reverse):
-    count = lax.axis_size(axis)
-    place = lax.axis_index(axis)
-    ahead = count - 1 - place if reverse else place
-    sign = -1 if reverse else 1
-
-    def from_before(state, by):
-        moved = jax.tree.map(lambda a: passed_along(a, axis, sign * by), state)
-        return jax.tree.map(lambda m, e: jnp.where(ahead >= by, m, e), moved, identity)
-
-    state = from_before(part, 1)
-    by = 1
-    while by < count:
-        state = combine(from_before(state, by), state)
-        by *= 2
-    return state
-
-
-def head_sum(parts):
-    count = lax.axis_size("head")
-    low = lax.axis_index("head") % 2
-    out = []
-    for part in parts:
-        rows = part.shape[0] // 2
-        mine = lax.dynamic_slice_in_dim(part, low * rows, rows, 0)
-        other = lax.dynamic_slice_in_dim(part, (1 - low) * rows, rows, 0)
-        half = mine + swapped(other, "head", 1)
-        by = 2
-        while by < count:
-            half = half + swapped(half, "head", by)
-            by *= 2
-        back = swapped(half, "head", 1)
-        out.append(jnp.where(low == 0, half, back))
-        out.append(jnp.where(low == 0, back, half))
-    return jnp.concatenate(out, axis=0)
-
-
-def sent(array):
-    moved = swapped(array.astype(jnp.float32), "seq", 1)
-    unit = jnp.minimum(lax.axis_index("seq").astype(jnp.float32) + 1.0, 1.0)
-    return (moved * unit).astype(jnp.bfloat16)
-
-
 def width_blocks(array):
     count = lax.axis_size("seq")
     lines = count // 2
     place = lax.axis_index("seq")
-    line, odd = place // 2, place % 2
+    odd = place % 2
     wide = array.shape[1] // count
     roles = list(range(lines))
-    if lines == 4:
-        left = line < 2
-        roles = [jnp.where(left, a, b) for a, b in ((2, 1), (3, 0), (1, 2), (0, 3))]
 
     def blocks(parity):
         return jnp.stack(
             [lax.dynamic_slice_in_dim(array, (2 * r + parity) * wide, wide, 1) for r in roles]
         )
 
-    mine, theirs = blocks(odd), blocks(1 - odd)
-    return mine, sent(theirs)
-
-
-def seq_sum(wide, narrow, wide_first):
-    count = lax.axis_size("seq")
-    lines = count // 2
-    place = lax.axis_index("seq") // 2
-    mine, theirs = wide
-    pair = (narrow, sent(narrow))
+    return blocks(odd), blocks(1 - odd).astype(jnp.float32)
+
+
+def pair_product(wide, narrow, wide_first):
     rule = "ztd,tf->zdf" if wide_first else "ztd,tf->zfd"
-
-    def product(lo, hi):
-        return sum(
-            jnp.einsum(rule, w[lo:hi], n, preferred_element_type=jnp.float32)
-            for w, n in zip((mine, theirs), pair)
-        )
-
-    if lines != 4:
-        groups = [[line * 2 + x for line in range(lines)] for x in range(2)]
-        return lax.psum_scatter(
-            product(0, lines), "seq", scatter_dimension=0, axis_index_groups=groups, tiled=True
-        )[0]
-
-    def moved(array, pairs):
-        return lax.ppermute(
-            array, "seq", [(2 * a + x, 2 * b + x) for a, b in pairs for x in range(2)]
-        )
-
-    far = product(0, 3)
-    near = product(3, 4)
-    from_end = moved(far, ((0, 1), (3, 2)))
-    from_middle = moved(far[:2] + from_end[:2], ((1, 2), (2, 1)))
-    to_end = moved(near + from_middle[1:], ((1, 0), (2, 3)))
-    at_end = (place == 0) | (place == 3)
-    return jnp.where(at_end, near[0] + to_end[0], far[2] + from_end[2] + from_middle[0])
+    return sum(
+        jnp.einsum(rule, w, n, preferred_element_type=jnp.float32)
+        for w, n in zip(wide, narrow)
+    )
+
+
+def line_sum(product):
+    lines = product.shape[0]
+    groups = [[line * 2 + x for line in range(lines)] for x in range(2)]
+    return lax.psum_scatter(
+        product, "seq", scatter_dimension=0, axis_index_groups=groups, tiled=True
+    )[0]
+
+
+def together(*arrays):
+    return lax.optimization_barrier(arrays)
 
 
 def precise_dot(left, right):
@@ -453,9 +391,261 @@
     )(keys, values, logs, new, docs, prev, dk, dv, held, gained, xk, xv, dk_end, dv_end, total)
 
 
-def compose(earlier, later):
-    factor = later[0][:, None]
-    return (earlier[0] * later[0], factor * earlier[1] + later[1], factor * earlier[2] + later[2])
+def other_of(place, by):
+    return place + by * (1 - 2 * ((place // by) % 2))
+
+
+def exchange_kernel(names, count, heads, reverse, *refs):
+    refs = dict(zip(names, refs))
+    wides = [n for n in names if n.startswith("wide_in")]
+    narrows = [n for n in names if n.startswith("narrow_in")]
+    place, head = lax.axis_index("seq"), lax.axis_index("head")
+    partner, sibling = {"seq": other_of(place, 1)}, {"head": other_of(head, 1)}
+    line = -1 if reverse else 1
+    ahead = count - 1 - place if reverse else place
+    left = count - 1 - ahead
+    spans_of = [1 << k for k in range(count.bit_length() - 1)]
+    hops = [1 << k for k in range(1, heads.bit_length() - 1)]
+
+    greeted = []
+    if wides or narrows:
+        greeted.append((partner, None))
+    if wides or "part" in refs:
+        greeted.append((sibling, None))
+    if "part" in refs:
+        greeted += [({"head": other_of(head, by)}, None) for by in hops]
+    if "state" in refs:
+        greeted += [({"seq": place + line * by}, left >= by) for by in spans_of]
+        greeted += [({"seq": place - line * by}, ahead >= by) for by in spans_of]
+    barrier = pltpu.get_barrier_semaphore()
+    total = 0
+    for device, ok in greeted:
+        if ok is None:
+            pl.semaphore_signal(barrier, inc=1, device_id=device, device_id_type=MESH)
+            total = total + 1
+        else:
+
+            @pl.when(ok)
+            def _(device=device):
+                pl.semaphore_signal(barrier, inc=1, device_id=device, device_id_type=MESH)
+
+            total = total + ok.astype(jnp.int32)
+    pl.semaphore_wait(barrier, total)
+
+    def copy(source, target, sems, device):
+        return pltpu.make_async_remote_copy(
+            src_ref=source, dst_ref=target, send_sem=sems[0], recv_sem=sems[1],
+            device_id=device, device_id_type=MESH,
+        )
+
+    def sems(name, i):
+        return refs[name + "_send"].at[i], refs[name + "_recv"].at[i]
+
+    def half_of(ref):
+        size = ref.shape[0] // 2
+        return ref.at[pl.ds((head % 2) * size, size)]
+
+    waits, forwards, states = [], [], []
+    if "state" in refs:
+        inside, received, before = refs["inside"], refs["received"], refs["before"]
+        inside[0] = refs["state"][...]
+        states = [
+            copy(inside.at[k], received.at[k], sems("state", k), {"seq": place + line * by})
+            for k, by in enumerate(spans_of)
+        ]
+
+        @pl.when(left >= 1)
+        def _():
+            states[0].start()
+
+    if "part" in refs:
+        part, added = refs["part"], refs["sum"]
+        rows = part.shape[0] // CHUNKS
+        half = rows // 2
+        low = head % 2
+        for c in range(CHUNKS):
+            start = pl.multiple_of(c * rows + (1 - low) * half, 8)
+            moved = copy(part.at[pl.ds(start, half)], refs["near"].at[c], sems("near", c), sibling)
+            moved.start()
+            waits.append(moved)
+    for i, name in enumerate(wides):
+        moved = copy(
+            half_of(refs[name]), half_of(refs[name.replace("in", "out")]), sems("wide", i), partner
+        )
+        moved.start()
+        forwards.append((name.replace("in", "out"), moved))
+    for i, name in enumerate(narrows):
+        moved = copy(refs[name], refs[name.replace("in", "out")], sems("narrow", i), partner)
+        moved.start()
+        waits.append(moved)
+
+    if "state" in refs:
+        lane = lax.broadcasted_iota(jnp.int32, before.shape, 1)
+        before[...] = jnp.where(lane < 128, 1.0, 0.0)
+
+        def composed(earlier, later):
+            return later[:, :1] * earlier + jnp.where(lane >= 128, later, 0.0)
+
+        for k, by in enumerate(spans_of):
+            moved = states[k]
+            if k:
+
+                @pl.when(left >= by)
+                def _(moved=moved):
+                    moved.start()
+
+            if k + 1 < len(spans_of):
+                inside[k + 1] = inside[k]
+
+            @pl.when(ahead >= by)
+            def _(k=k, moved=moved):
+                moved.wait_recv()
+                before[...] = composed(received[k], before[...])
+                if k + 1 < len(spans_of):
+                    inside[k + 1] = composed(received[k], inside[k])
+
+            @pl.when(left >= by)
+            def _(moved=moved):
+                moved.wait_send()
+
+    if "part" in refs:
+        own, arrived = refs["own"], refs["arrived"]
+        across = []
+        for c in range(CHUNKS):
+            waits[c].wait_recv()
+            start = pl.multiple_of(c * rows + low * half, 8)
+            own[0, c] = part[pl.ds(start, half), :] + refs["near"][c]
+            moved = copy(
+                own.at[0, c], arrived.at[0, c], sems("across", c), {"head": other_of(head, 2)}
+            )
+            moved.start()
+            across.append(moved)
+        for k in range(1, len(hops)):
+            later = []
+            for c in range(CHUNKS):
+                across[c].wait()
+                own[k, c] = own[k - 1, c] + arrived[k - 1, c]
+                moved = copy(
+                    own.at[k, c], arrived.at[k, c], sems("across", k * CHUNKS + c),
+                    {"head": other_of(head, hops[k])},
+                )
+                moved.start()
+                later.append(moved)
+            across = later
+        back = []
+        k = len(hops) - 1
+        for c in range(CHUNKS):
+            across[c].wait()
+            start = pl.multiple_of(c * rows + low * half, 8)
+            mine = pl.ds(start, half)
+            added[mine, :] = own[k, c] + arrived[k, c]
+            moved = copy(added.at[mine], added.at[mine], sems("back", c), sibling)
+            moved.start()
+            back.append(moved)
+        for c in range(CHUNKS):
+            waits[c].wait_send()
+            back[c].wait()
+        waits = waits[CHUNKS:]
+    for i, (name, moved) in enumerate(forwards):
+        moved.wait()
+        onward = copy(half_of(refs[name]), half_of(refs[name]), sems("onward", i), sibling)
+        onward.start()
+        waits.append(onward)
+    for moved in waits:
+        moved.wait()
+
+
+def exchange(number, part=None, state=None, reverse=False, wides=(), narrows=()):
+    count, heads = lax.axis_size("seq"), lax.axis_size("head")
+    f32 = jnp.float32
+    vmem, hbm = pl.BlockSpec(memory_space=pltpu.VMEM), pl.BlockSpec(memory_space=pl.ANY)
+    ins, outs, scratch = [], [], []
+    if part is not None:
+        ins.append(("part", part, vmem))
+        outs.append(("sum", part, vmem))
+        half = (CHUNKS, part.shape[0] // CHUNKS // 2, part.shape[1])
+        steps = heads.bit_length() - 2
+        scratch += [
+            ("near", pltpu.VMEM(half, f32)),
+            ("own", pltpu.VMEM((steps,) + half, f32)),
+            ("arrived", pltpu.VMEM((steps,) + half, f32)),
+        ]
+        for name, size in (("near", CHUNKS), ("across", steps * CHUNKS), ("back", CHUNKS)):
+            scratch += [(name + end, pltpu.SemaphoreType.DMA((size,))) for end in ("_send", "_recv")]
+    if state is not None:
+        ins.append(("state", state, vmem))
+        outs.append(("before", state, vmem))
+        steps = count.bit_length() - 1
+        scratch += [(n, pltpu.VMEM((steps,) + state.shape, f32)) for n in ("inside", "received")]
+        scratch += [("state" + end, pltpu.SemaphoreType.DMA((steps,))) for end in ("_send", "_recv")]
+    for kind, arrays in (("wide", wides), ("narrow", narrows)):
+        ins += [(f"{kind}_in{i}", a, hbm) for i, a in enumerate(arrays)]
+        outs += [(f"{kind}_out{i}", a, hbm) for i, a in enumerate(arrays)]
+        for name in (kind, "onward") if kind == "wide" else (kind,):
+            if arrays:
+                scratch += [
+                    (name + end, pltpu.SemaphoreType.DMA((len(arrays),))) for end in ("_send", "_recv")
+                ]
+    names = [n for n, *_ in ins] + [n for n, *_ in outs] + [n for n, _ in scratch]
+    return pl.pallas_call(
+        functools.partial(exchange_kernel, names, count, heads, reverse),
+        out_shape=tuple(jax.ShapeDtypeStruct(a.shape, f32) for _, a, _ in outs),
+        in_specs=[spec for *_, spec in ins],
+        out_specs=tuple(spec for *_, spec in outs),
+        scratch_shapes=[s for _, s in scratch],
+        compiler_params=pltpu.CompilerParams(
+            collective_id=number, has_side_effects=True, vmem_limit_bytes=VMEM
+        ),
+        cost_estimate=cost(40 << 30, 16 << 20),
+    )(*[a for _, a, _ in ins])
+
+
+def scatter_kernel(count, in_ref, out_ref, slots, send, receive):
+    place = lax.axis_index("seq")
+    others = [{"seq": lax.rem(place + k, count)} for k in range(1, count)]
+    barrier = pltpu.get_barrier_semaphore()
+    for device in others:
+        pl.semaphore_signal(barrier, inc=1, device_id=device, device_id_type=MESH)
+    pl.semaphore_wait(barrier, count - 1)
+    copies = []
+    for k, device in enumerate(others):
+        moved = pltpu.make_async_remote_copy(
+            src_ref=in_ref.at[device["seq"]], dst_ref=slots.at[place],
+            send_sem=send.at[k], recv_sem=receive.at[k], device_id=device, device_id_type=MESH,
+        )
+        moved.start()
+        copies.append(moved)
+    slots[place] = in_ref[place]
+    for moved in copies:
+        moved.wait()
+    total = slots[0]
+    for i in range(1, count):
+        total = total + slots[i]
+    out_ref[...] = total
+
+
+def scatter_sum(number, array):
+    count = array.shape[0]
+    vmem = pl.BlockSpec(memory_space=pltpu.VMEM)
+    return pl.pallas_call(
+        functools.partial(scatter_kernel, count),
+        out_shape=jax.ShapeDtypeStruct(array.shape[1:], jnp.float32),
+        in_specs=[vmem],
+        out_specs=vmem,
+        scratch_shapes=[
+            pltpu.VMEM(array.shape, jnp.float32),
+            pltpu.SemaphoreType.DMA((count - 1,)),
+            pltpu.SemaphoreType.DMA((count - 1,)),
+        ],
+        compiler_params=pltpu.CompilerParams(
+            collective_id=number, has_side_effects=True, vmem_limit_bytes=VMEM
+        ),
+        cost_estimate=cost(4 << 30, 1 << 20),
+    )(array)
+
+
+def state_of(keep, keys, values):
+    return jnp.concatenate([jnp.broadcast_to(keep[:, None], (keep.shape[0], 128)), keys, values], axis=1)
 
 
 def body(
@@ -507,28 +697,34 @@
     docs = jnp.broadcast_to(docs[:, None], (tok_rows, slots))
     before = jnp.broadcast_to(jnp.repeat(before, CHUNK)[:, None], (tok_rows, slots))
 
-    chunk = tok_rows // CHUNKS
-
-    def over_heads(product):
-        return head_sum(
-            [product(lambda a, i=i: a[i * chunk : (i + 1) * chunk]) for i in range(CHUNKS)]
-        )
-
-    zero_state = jnp.zeros((slots, head_width), jnp.float32)
+    def with_partner(own, received):
+        return own, received.astype(jnp.bfloat16)
+
+    def wide_float(array):
+        return array.astype(jnp.float32)
+
     local_key = precise_left_t(factor, key_rows.astype(jnp.float32))
     local_value = precise_left_t(factor, value_rows.astype(jnp.float32))
     decay_all = jnp.where(last_doc == prior, jnp.exp(total), 0.0)
-    identity = (jnp.ones((slots,), jnp.float32), zero_state, zero_state)
-    prefix = entering((decay_all, local_key, local_value), "seq", compose, identity, False)
+    (prefix,) = exchange(0, state=state_of(decay_all, local_key, local_value))
+    key_in, value_in = prefix[:, 128 : 128 + head_width], prefix[:, 128 + head_width :]
+    d_act = dot_right_t(cotangent, w_down)
+    key_in, d_act = together(key_in, d_act)
+    own_dy, their_dy = width_blocks(cotangent)
+    own_in, their_in = width_blocks(normed_in)
     slot_read, scores, probs, key_states, value_states = read_slots(
-        query_rows, key_rows, value_rows, log_decay, new, docs, before, prefix[1], prefix[2]
+        query_rows, key_rows, value_rows, log_decay, new, docs, before, key_in, value_in
     )
     scale_read = rms_scale(slot_read)
     normed_read = slot_read * scale_read * head_gain[0]
     gate_sig = jax.nn.sigmoid(gate_act)
     gate_silu = gate_act * gate_sig
     mixed_heads = (normed_read * gate_silu).astype(jnp.bfloat16)
-    branch = over_heads(lambda rows: plain_dot(rows(mixed_heads), w_out))
+    branch, from_dy, from_in = exchange(
+        1, part=plain_dot(mixed_heads, w_out), wides=(their_dy, their_in)
+    )
+    wide_dy = with_partner(own_dy, from_dy)
+    wide_in = with_partner(own_in, from_in)
     hidden = stream_f + branch
     scale_mid = rms_scale(hidden)
     normed_mid = (hidden * scale_mid * mlp_gain).astype(jnp.bfloat16)
@@ -537,26 +733,25 @@
     pre_sig = jax.nn.sigmoid(gate_pre)
     pre_silu = gate_pre * pre_sig
     ffn_act = (pre_silu * up_pre).astype(jnp.bfloat16)
-    ffn_out = over_heads(lambda rows: plain_dot(rows(ffn_act), w_down))
-    result = hidden + ffn_out
-    square_sums = lax.psum(
-        jnp.stack(
-            [jnp.sum(stream_f * stream_f), jnp.sum(hidden * hidden), jnp.sum(result * result)]
-        ),
-        "seq",
-    )
-    stream_rms = jnp.sqrt(square_sums / (tok_rows * lax.axis_size("seq") * width))
     upstream = cotangent.astype(jnp.float32)
-    d_act = dot_right_t(cotangent, w_down)
-    grad_down = seq_sum(width_blocks(cotangent), ffn_act, False)
     d_gate = (d_act * up_pre * pre_sig * (1.0 + gate_pre * (1.0 - pre_sig))).astype(jnp.bfloat16)
     d_up = (d_act * pre_silu).astype(jnp.bfloat16)
-    d_mid = over_heads(
-        lambda rows: dot_right_t(rows(d_gate), w_gate) + dot_right_t(rows(d_up), w_up)
-    )
-    wide_mid = width_blocks(normed_mid)
-    grad_gate = seq_sum(wide_mid, d_gate, True)
-    grad_up = seq_sum(wide_mid, d_up, True)
+    d_mid, from_act = exchange(
+        2,
+        part=dot_right_t(d_gate, w_gate) + dot_right_t(d_up, w_up),
+        narrows=(wide_float(ffn_act),),
+    )
+    grad_down = pair_product(wide_dy, with_partner(ffn_act, from_act), False)
+    d_mid, grad_down = together(d_mid, grad_down)
+    grad_down = line_sum(grad_down)
+    own_mid, their_mid = width_blocks(normed_mid)
+    ffn_part, d_mid = together(plain_dot(ffn_act, w_down), d_mid)
+    ffn_out, from_mid, from_gate = exchange(
+        3, part=ffn_part, wides=(their_mid,), narrows=(wide_float(d_gate),)
+    )
+    wide_mid = with_partner(own_mid, from_mid)
+    grad_gate = pair_product(wide_mid, with_partner(d_gate, from_gate), True)
+    d_mid, grad_gate = together(d_mid, grad_gate)
     grad_mlp_gain = jnp.sum(d_mid * hidden * scale_mid, axis=0)
     scaled_mid = d_mid * mlp_gain
     d_hidden = (
@@ -566,7 +761,7 @@
     )
     d_branch = d_hidden.astype(jnp.bfloat16)
     d_mixed = dot_right_t(d_branch, w_out)
-    grad_out = seq_sum(width_blocks(d_branch), mixed_heads, False)
+    own_branch, their_branch = width_blocks(d_branch)
     d_gate_act = (d_mixed * normed_read * gate_sig * (1.0 + gate_act * (1.0 - gate_sig))).astype(
         jnp.bfloat16
     )
@@ -576,30 +771,58 @@
     d_read = scale_read * scaled_read - slot_read * scale_read**3 * jnp.mean(
         scaled_read * slot_read, axis=1, keepdims=True
     )
+    grad_gate, grad_down, unused_read = together(grad_gate, grad_down, d_read)
+    grad_gate = line_sum(grad_gate)
     d_query, d_key, d_value, held, gained, to_keys, to_values, key_back, value_back = back_query(
         query_rows, key_rows, value_rows, log_decay, new, docs, before, scores, probs, key_states, value_states, d_read
     )
     query_back = d_query.astype(jnp.bfloat16)
-    suffix = entering((decay_all, key_back, value_back), "seq", compose, identity, True)
-    end_total = jnp.sum(key_states[-1] * suffix[1] + value_states[-1] * suffix[2], axis=1)[None, :]
+    suffix, from_up, from_outgate = exchange(
+        4,
+        state=state_of(decay_all, key_back, value_back),
+        reverse=True,
+        narrows=(wide_float(d_up), wide_float(d_gate_act)),
+    )
+    grad_up = pair_product(wide_mid, with_partner(d_up, from_up), True)
+    key_end, value_end = suffix[:, 128 : 128 + head_width], suffix[:, 128 + head_width :]
+    end_total = jnp.sum(key_states[-1] * key_end + value_states[-1] * value_end, axis=1)[None, :]
+    d_key, grad_up = together(d_key, grad_up)
+    grad_up, grad_gate = together(grad_up, grad_gate)
+    grad_up = line_sum(grad_up)
     key_back, value_back, d_logs = back_key(
         key_rows, value_rows, log_decay, new, docs, before, d_key, d_value, held, gained,
-        to_keys, to_values, suffix[1], suffix[2], end_total,
+        to_keys, to_values, key_end, value_end, end_total,
     )
     d_ranked, grad_slot, grad_bias = gate_pull(d_logs)
     normed_f = normed_in.astype(jnp.float32)
     grad_low = precise_left_t(normed_f, d_ranked)
-    wide_in = width_blocks(normed_in)
-    grad_outgate = seq_sum(wide_in, d_gate_act, True)
-    grad_query = seq_sum(wide_in, query_back, True)
-    grad_key = seq_sum(wide_in, key_back, True)
-    grad_value = seq_sum(wide_in, value_back, True)
-    d_in = over_heads(
-        lambda rows: dot_right_t(rows(query_back), w_query)
-        + dot_right_t(rows(key_back), w_key)
-        + dot_right_t(rows(value_back), w_value)
-        + dot_right_t(rows(d_gate_act), w_outgate)
-        + precise_right_t(rows(d_ranked), w_low.astype(jnp.float32))
+    d_in_part = (
+        dot_right_t(query_back, w_query)
+        + dot_right_t(key_back, w_key)
+        + dot_right_t(value_back, w_value)
+        + dot_right_t(d_gate_act, w_outgate)
+        + precise_right_t(d_ranked, w_low.astype(jnp.float32))
+    )
+    d_in, from_branch, *from_mixer = exchange(
+        5,
+        part=d_in_part,
+        wides=(their_branch,),
+        narrows=[wide_float(a) for a in (query_back, key_back, value_back, mixed_heads)],
+    )
+    from_mixed = from_mixer.pop()
+    from_mixer = [from_outgate, *from_mixer]
+    wide_branch = with_partner(own_branch, from_branch)
+    grad_out = pair_product(wide_branch, with_partner(mixed_heads, from_mixed), False)
+    own_mixer = jnp.concatenate([d_gate_act, query_back, key_back, value_back], axis=1)
+    their_mixer = jnp.concatenate([a.astype(jnp.bfloat16) for a in from_mixer], axis=1)
+    grad_mixer = pair_product(wide_in, (own_mixer, their_mixer), True)
+    grad_out, grad_up, d_in = together(grad_out, grad_up, d_in)
+    grad_out = line_sum(grad_out)
+    grad_mixer = line_sum(grad_mixer)
+    grad_outgate, grad_query, grad_key, grad_value = jnp.split(grad_mixer, 4, axis=1)
+    result = hidden + ffn_out
+    squares = jnp.stack(
+        [jnp.sum(stream_f * stream_f), jnp.sum(hidden * hidden), jnp.sum(result * result)]
     )
     grad_attn_gain = jnp.sum(d_in * stream_f * scale_in, axis=0)
     scaled_in = d_in * attn_gain
@@ -616,13 +839,15 @@
         jnp.moveaxis(grad_slot[0].reshape(-1, count, slots // count), 1, 0).reshape(count, -1),
         grad_bias.reshape(count, -1),
         grad_head_gain.reshape(count, -1),
+        jnp.broadcast_to(squares, (count, 3)),
     ]
     sizes = [a.shape[1] for a in small]
     packed = jnp.concatenate(small, axis=1)
-    packed = jnp.pad(packed, ((0, 0), (0, -packed.shape[1] % 128)))
-    packed = lax.psum_scatter(packed, "seq", scatter_dimension=0, tiled=True)[0]
+    packed = jnp.pad(packed, ((0, 0), (0, -packed.shape[1] % 1024)))
+    packed = scatter_sum(6, packed.reshape(count, -1, 128)).reshape(-1)
     ends = [sum(sizes[: i + 1]) for i in range(len(sizes))]
     small = [packed[end - size : end] for end, size in zip(ends, sizes)]
+    stream_rms = jnp.sqrt(small[6] / (tok_rows * count * width))
     summed = (
         small[0],
         grad_query,

time: 1390 us -> 800 us (0.58)
  waiting for transfers between devices: 858 us -> 165 us
  Pallas kernels: 47.5 us -> 420 us
  starting transfers between devices: 143 us -> 17.4 us
  other arithmetic: 98.3 us -> 37.5 us
  local copies, waits for them, and re-layouts: 79.5 us -> 45.5 us
  matrix products: 117 us -> 89.1 us
  blocking collectives: 20.7 us -> 0 us
    ppermute x60 -> x0, waiting for transfers between devices: 763 us -> none  [the longest x24 603 us: moved(): lax.ppermute(array, 'seq', [(2 * a + x, 2 * b + x) for a, b in pairs for...]
    pallas_call x0 -> x7, Pallas kernels: none -> 372 us  [the longest x6 362 us: exchange(): pl.pallas_call(functools.partial(exchange_kernel, names, count, heads, re...]
    reduce_scatter x0 -> x5, waiting for transfers between devices: none -> 165 us  [line_sum(): lax.psum_scatter(product, 'seq', scatter_dimension=0, axis_index_groups=g...]
    ppermute x23 -> x1, waiting for transfers between devices: 95.3 us -> 0.01 us  [passed_along(): return lax.ppermute(array, axis, pairs)]
    ppermute x60 -> x0, starting transfers between devices: 83.8 us -> none  [the longest x24 47.7 us: moved(): lax.ppermute(array, 'seq', [(2 * a + x, 2 * b + x) for a, b in pairs for...]
    ppermute x23 -> x1, starting transfers between devices: 59.5 us -> 5.42 us  [passed_along(): return lax.ppermute(array, axis, pairs)]
    add x29 -> x0, other arithmetic: 37.3 us -> none  [the longest x8 20.6 us: seq_sum(): from_middle = moved(far[:2] + from_end[:2], ((1, 2), (2, 1)))]
    dot_general x32 -> x10, matrix products: 55.4 us -> 28.8 us  [pair_product(): jnp.einsum(rule, w, n, preferred_element_type=jnp.float32)]
  transfers between devices with their start and end apart: 84 -> 6, of which waited for: 33 -> 3; matrix products, arithmetic and copies ran while one was open for 18% -> 15% of each run, Pallas kernels for 3% -> 36%
where the time goes in v2:
time: 800 us; the launch traced here: 792 us
  Pallas kernels  420 us (52%)
  waiting for transfers between devices  165 us (21%)
  matrix products  89.1 us (11%)
  local copies, waits for them, and re-layouts  45.5 us (6%)
  other arithmetic  37.5 us (5%)
  between operations  17.5 us (2%)
  starting transfers between devices  17.4 us (2%)
    pallas_call x6, Pallas kernels, exchange(): pl.pallas_call(functools.partial(exchange_kernel, names, count, heads, re...  362 us
    reduce_scatter x5, waiting for transfers between devices, line_sum(): lax.psum_scatter(product, 'seq', scatter_dimension=0, axis_index_groups=g...  165 us
    dot_general x9, matrix products, plain_dot(): return jnp.dot(left, right, preferred_element_type=jnp.float32)  29.6 us
    dot_general x10, matrix products, pair_product(): jnp.einsum(rule, w, n, preferred_element_type=jnp.float32)  28.8 us
    pallas_call x1, Pallas kernels, back_query(): pl.pallas_call(back_query_kernel, out_shape=(wide, wide, wide, narrow, na...  25.7 us
    dot_general x8, matrix products, dot_right_t(): lax.dot_general(left, right, (((1,), (1,)), ((), ())), preferred_element_...  23 us
    unnamed x252, local copies, waits for them, and re-layouts  22.6 us
  transfers between devices with their start and end apart: 6, of which 3 were waited for; matrix products, arithmetic and copies ran while one was open for 15% of the time, Pallas kernels for 36%

profile of v2, /device:TPU:0, one launch (start us, length us, event | category | flops | bytes accessed | tf_op | source)
XLA Modules:
  0.0 792.1 jit_solution(12045321789448166803)
XLA Ops:
  8.7 5.4 collective-permute-start
  31.2 7.2 fusion.111
  46.1 19.9 %shard_map.296 = f32[64,1152]{1,0:T(8,128)S(1)} custom-call(f32[64,1152]{1,0:T(8,128)S(1)} %fusion.70.refs_0_), custom_call_target="tpu_custom_call" | custom-call | flops 42949672960 | bytes 16777216 | tf_op jit(solution)/shard_map/pallas_call | solution.py:590
  66.4 12.2 %shard_map.297 = (f32[384,512]{1,0:T(8,128)S(1)}, f32[384,64]{1,0:T(8,128)S(1)}, f32[384,64]{1,0:T(8,128)S(1)}, f32[13,64,512]{2,1,0:T(8,128)S(1)}, f32[13,64,512]{2,1,0:T(8,128)}) custom-call(bf16[384,512]{1,0:T(8,128)(2,1)S(1)} %copy-done.22, bf16[384,512]{1,0:T(8,128)(2,1)S(1)} %convolution_convert_fusion.1.k_ref, ...), custom_call_target="tpu_custom_call" | custom-call | flops 18253611008 | bytes 5242880 | tf_op jit(solution)/shard_map/pallas_call | solution.py:343
  85.2 47.5 %shard_map.298 = (f32[384,2048]{1,0:T(8,128)}, f32[4,384,256]{2,1,0:T(8,128)S(1)}, f32[4,384,256]{2,1,0:T(8,128)S(1)}) custom-call(f32[384,2048]{1,0:T(8,128)} %fusion.112.refs_0_, f32[4,384,256]{2,1,0:T(8,128)S(1)} %copy-done.8, f32[4,384,256]{2,1,0:T(8,128)} %maximum_convert_fusion.1.refs_2_), custom_call_target="tpu_custom_call" | custom-call | flops 42949672960 | bytes 16777216 | tf_op jit(solution)/shard_map/pallas_call | solution.py:590
  137.4 5.8 fusion.113
  143.3 5.3 fusion.104
  151.3 4.3 convolution_add_fusion.3.refs_0_
  155.7 53.8 %shard_map.299 = (f32[384,2048]{1,0:T(8,128)}, f32[384,1408]{1,0:T(8,128)S(1)}) custom-call(f32[384,2048]{1,0:T(8,128)} %convolution_add_fusion.3.refs_0_, f32[384,1408]{1,0:T(8,128)S(1)} %get-tuple-element.185.refs_1_), custom_call_target="tpu_custom_call" | custom-call | flops 42949672960 | bytes 16777216 | tf_op jit(solution)/shard_map/pallas_call | solution.py:590
  224.8 7.3 fusion.114.refs_0_
  235.3 69.7 %shard_map.300 = (f32[384,2048]{1,0:T(8,128)}, f32[4,384,256]{2,1,0:T(8,128)S(1)}, f32[384,1408]{1,0:T(8,128)S(1)}) custom-call(f32[384,2048]{1,0:T(8,128)} %fusion.114.refs_0_, f32[4,384,256]{2,1,0:T(8,128)S(1)} %maximum_convert_fusion.2.refs_1_, f32[384,1408]{1,0:T(8,128)} %get-tuple-element.183.refs_2_), custom_call_target="tpu_custom_call" | custom-call | flops 42949672960 | bytes 16777216 | tf_op jit(solution)/shard_map/pallas_call | solution.py:590
  306.2 4.2 convolution_add_fusion.1
  310.4 6.4 multiply_reduce_fusion.3
  326.3 11.3 %reduce-scatter.10.cloned.1.call-start = ((), (), s32[]{:S(2)}) async-start(), calls=%async_computation.7 | async-start | bytes 7208960 | tf_op jit(solution)/shard_map/reduce_scatter | solution.py:56
  340.6 25.7 %shard_map.301 = (f32[384,512]{1,0:T(8,128)S(1)}, f32[384,512]{1,0:T(8,128)S(1)}, f32[384,512]{1,0:T(8,128)S(1)}, f32[384,64]{1,0:T(8,128)S(1)}, f32[384,64]{1,0...) custom-call(bf16[384,512]{1,0:T(8,128)(2,1)S(1)} %copy-done.23, ...), custom_call_target="tpu_custom_call" | custom-call | flops 36507222016 | bytes 10485760 | tf_op jit(solution)/shard_map/pallas_call | solution.py:367
  368.2 81.9 %shard_map.302 = (f32[64,1152]{1,0:T(8,128)S(1)}, f32[384,1408]{1,0:T(8,128)S(1)}, f32[384,512]{1,0:T(8,128)S(1)}) custom-call(f32[64,1152]{1,0:T(8,128)S(1)} %fusion.71.refs_0_, f32[384,1408]{1,0:T(8,128)} %get-tuple-element.172.refs_1_, f32[384,512]{1,0:T(8,128)S(1)} %copy-done.24), custom_call_target="tpu_custom_call" | custom-call | flops 42949672960 | bytes 16777216 | tf_op jit(solution)/shard_map/pallas_call | solution.py:590
  450.1 4.3 convolution_add_fusion
  465.2 10.0 %shard_map.303 = (bf16[384,512]{1,0:T(8,128)(2,1)S(1)}, bf16[384,512]{1,0:T(8,128)(2,1)S(1)}, f32[384,64]{1,0:T(8,128)S(1)}) custom-call(bf16[384,512]{1,0:T(8,128)(2,1)S(1)} %copy-done.21, bf16[384,512]{1,0:T(8,128)(2,1)S(1)} %copy-done.19, f32[384,64]{1,0:T(8,128)S(1)} %copy-done.17, f32[384,64]{1,0:T(8,128)S(1)} %copy-done.15, f32[384,64]{1,0:T(8,128)S(1)} %copy-done.12, ...), custom_call_target="tpu_custom_call" | custom-call | flops 18253611008 | bytes 8388608 | tf_op jit(solution)/shard_map/pallas_call | solution.py:381
  488.0 89.3 %shard_map.304 = (f32[384,2048]{1,0:T(8,128)}, f32[4,384,256]{2,1,0:T(8,128)}, f32[384,512]{1,0:T(8,128)S(1)}, f32[384,512]{1,0:T(8,128)S(1)}, f32[384,512]{1,0:T(8,128)S(1)}, /*index=5*/f32[384,512]{1,0:T(8,128)S(1)}) custom-call(f32[384,2048]{1,0:T(8,128)} %add_add_fusion.refs_0_, f32[4,384,256]{2,1,0:T(8,128)} %maximum_convert_fusion.3.refs_1_, ...), custom_call_target="tpu_custom_call" | custom-call | flops 42949672960 | bytes 16777216 | tf_op jit(solution)/shard_map/pallas_call | solution.py:590
  580.9 5.9 convolution_add_fusion.2
  595.1 140.4 %reduce-scatter.12.cloned.1.call-done = f32[1,256,2048]{2,1,0:T(8,128)} async-done(((f32[4,256,2048]{2,1,0:T(8,128)}), f32[1,256,2048]{2,1,0:T(8,128)}) %reduce-scatter.12.cloned.1.call-update) | async-done | bytes 2097168 | tf_op jit(solution)/shard_map/reduce_scatter | solution.py:56
  744.5 10.2 %shard_map.305 = f32[40,128]{1,0:T(8,128)S(1)} custom-call(f32[8,40,128]{2,1,0:T(8,128)S(1)} %bitcast.189), custom_call_target="tpu_custom_call" | custom-call | flops 4294967296 | bytes 1048576 | tf_op jit(solution)/shard_map/pallas_call | solution.py:630
  758.5 5.5 fusion.6
  764.1 21.3 %reduce-scatter.14.cloned.1.call-done = f32[1,512,256]{2,1,0:T(8,128)} async-done(((f32[4,512,256]{2,1,0:T(8,128)}), f32[1,512,256]{2,1,0:T(8,128)}) %reduce-scatter.14.cloned.1.call-update) | async-done | bytes 524304 | tf_op jit(solution)/shard_map/reduce_scatter | solution.py:56
  (368 shorter events, 119.8 us)
Async XLA Ops:
  7.2 75.4 %copy-start = (bf16[512,2048]{1,0:T(8,128)(2,1)S(1)}, bf16[512,2048]{1,0:T(8,128)(2,1)}, u32[]{:S(2)}) copy-start(bf16[512,2048]{1,0:T(8,128)(2,1)} %param.28) | copy-start | bytes 6291460
  7.2 319.0 %reduce-scatter.6.cloned.1.call-start = ((), (), s32[]{:S(2)}) async-start(), calls=%async_computation.5 | async-start | bytes 7208960 | tf_op jit(solution)/shard_map/reduce_scatter | solution.py:56
  8.7 33.8 %collective-permute-start = (s32[1]{0:T(128)}, s32[1]{0:T(128)}, u32[]{:S(2)}, u32[]{:S(2)}) collective-permute-start(s32[1]{0:T(128)} %slice.57), channel_id=1, source_target_pairs={{0,4},{4,8},{8,12},{12,16},{16,20},{20,24},{24,28},{1,5},{5,9},{9,... | collective-permute-start | bytes 20 | tf_op jit(solution)/shard_map/ppermute | solution.py:26
  20.3 317.3 %copy-start.14 = (f32[384,64]{1,0:T(8,128)}, f32[384,64]{1,0:T(8,128)S(1)}, u32[]{:S(2)}) copy-start(f32[384,64]{1,0:T(8,128)S(1)} %get-tuple-element.230.new_ref) | copy-start | bytes 294916
  20.3 317.3 %copy-start.16 = (f32[384,64]{1,0:T(8,128)}, f32[384,64]{1,0:T(8,128)S(1)}, u32[]{:S(2)}) copy-start(f32[384,64]{1,0:T(8,128)S(1)} %get-tuple-element.231.log_ref) | copy-start | bytes 294916
  25.4 312.2 %copy-start.18 = (bf16[384,512]{1,0:T(8,128)(2,1)}, bf16[384,512]{1,0:T(8,128)(2,1)S(1)}, u32[]{:S(2)}) copy-start(bf16[384,512]{1,0:T(8,128)(2,1)S(1)} %convolution_convert_fusion.v_ref) | copy-start | bytes 1179652
  27.1 310.5 %copy-start.20 = (bf16[384,512]{1,0:T(8,128)(2,1)}, bf16[384,512]{1,0:T(8,128)(2,1)S(1)}, u32[]{:S(2)}) copy-start(bf16[384,512]{1,0:T(8,128)(2,1)S(1)} %convolution_convert_fusion.1.k_ref) | copy-start | bytes 1179652
  85.2 47.5 %copy-start.38 = (bf16[384,2048]{1,0:T(8,128)(2,1)S(1)}, bf16[384,2048]{1,0:T(8,128)(2,1)}, u32[]{:S(2)}) copy-start(bf16[384,2048]{1,0:T(8,128)(2,1)} %param.17) | copy-start | bytes 4718596
  148.6 60.8 %copy-start.118 = (bf16[384,1408]{1,0:T(8,128)(2,1)}, bf16[384,1408]{1,0:T(8,128)(2,1)S(1)}, u32[]{:S(2)}) copy-start(bf16[384,1408]{1,0:T(8,128)(2,1)S(1)} %get-tuple-element.186) | copy-start | bytes 3244036
  155.7 53.8 %copy-start.86 = (bf16[1,384,256]{2,1,0:T(8,128)(2,1)S(1)}, bf16[1,384,256]{2,1,0:T(8,128)(2,1)}, u32[]{:S(2)}) copy-start(bf16[1,384,256]{2,1,0:T(8,128)(2,1)} %get-tuple-element.243) | copy-start | bytes 589828
  155.7 53.8 %copy-start.87 = (bf16[1,384,256]{2,1,0:T(8,128)(2,1)S(1)}, bf16[1,384,256]{2,1,0:T(8,128)(2,1)}, u32[]{:S(2)}) copy-start(bf16[1,384,256]{2,1,0:T(8,128)(2,1)} %get-tuple-element.248) | copy-start | bytes 589828
  155.7 53.8 %copy-start.88 = (bf16[1,384,256]{2,1,0:T(8,128)(2,1)S(1)}, bf16[1,384,256]{2,1,0:T(8,128)(2,1)}, u32[]{:S(2)}) copy-start(bf16[1,384,256]{2,1,0:T(8,128)(2,1)} %get-tuple-element.249) | copy-start | bytes 589828
  155.7 53.8 %copy-start.89 = (bf16[1,384,256]{2,1,0:T(8,128)(2,1)S(1)}, bf16[1,384,256]{2,1,0:T(8,128)(2,1)}, u32[]{:S(2)}) copy-start(bf16[1,384,256]{2,1,0:T(8,128)(2,1)} %get-tuple-element.250) | copy-start | bytes 589828
  215.4 239.0 %reduce-scatter.8.cloned.1.call-start = ((), (), s32[]{:S(2)}) async-start(), calls=%async_computation.6 | async-start | bytes 7208960 | tf_op jit(solution)/shard_map/reduce_scatter | solution.py:56
  326.3 264.3 %reduce-scatter.10.cloned.1.call-start = ((), (), s32[]{:S(2)}) async-start(), calls=%async_computation.7 | async-start | bytes 7208960 | tf_op jit(solution)/shard_map/reduce_scatter | solution.py:56
  340.5 25.8 %copy-start.65 = (bf16[1,384,256]{1,2,0:T(8,128)(2,1)S(1)}, bf16[1,384,256]{1,2,0:T(8,128)(2,1)}, u32[]{:S(2)}) copy-start(bf16[1,384,256]{1,2,0:T(8,128)(2,1)} %copy.51) | copy-start | bytes 589828
  340.6 25.8 %copy-start.68 = (bf16[384,1408]{1,0:T(8,128)(2,1)S(1)}, bf16[384,1408]{1,0:T(8,128)(2,1)}, u32[]{:S(2)}) copy-start(bf16[384,1408]{1,0:T(8,128)(2,1)} %copy-done.67) | copy-start | bytes 3244036
  368.2 81.9 %copy-start.3 = (f32[4,384,256]{2,1,0:T(8,128)S(1)}, f32[4,384,256]{2,1,0:T(8,128)}, u32[]{:S(2)}) copy-start(f32[4,384,256]{2,1,0:T(8,128)} %copy-done.2) | copy-start | bytes 4718596
  454.4 281.0 %reduce-scatter.12.cloned.1.call-start = ((), (), s32[]{:S(2)}) async-start(), calls=%async_computation.8 | async-start | bytes 10485760 | tf_op jit(solution)/shard_map/reduce_scatter | solution.py:56
  586.8 198.6 %reduce-scatter.14.cloned.1.call-start = ((), (), s32[]{:S(2)}) async-start(), calls=%async_computation.9 | async-start | bytes 2621440 | tf_op jit(solution)/shard_map/reduce_scatter | solution.py:56
  594.8 143.4 %copy-start.39 = (bf16[384,2048]{1,0:T(8,128)(2,1)S(1)}, bf16[384,2048]{1,0:T(8,128)(2,1)}, u32[]{:S(2)}) copy-start(bf16[384,2048]{1,0:T(8,128)(2,1)} %param.17) | copy-start | bytes 4718596
  594.9 143.4 %copy-start.101 = (f32[2048]{0:T(1024)S(1)}, f32[2048]{0:T(1024)}, u32[]{:S(2)}) copy-start(f32[2048]{0:T(1024)} %param.19) | copy-start | bytes 24580
  594.9 143.4 %copy-start.105 = (f32[384]{0:T(512)S(1)}, f32[384]{0:T(512)}, u32[]{:S(2)}) copy-start(f32[384]{0:T(512)} %copy-done.104) | copy-start | bytes 4612
  758.5 26.8 %copy-start.1 = (bf16[512,2048]{1,0:T(8,128)(2,1)S(1)}, bf16[512,2048]{1,0:T(8,128)(2,1)}, u32[]{:S(2)}) copy-start(bf16[512,2048]{1,0:T(8,128)(2,1)} %param.28) | copy-start | bytes 6291460
  (106 other events, 523.2 us)
Sparse Core Ops, SparseCore 0:
  215.5 110.6 reduce-scatter.5
  329.1 123.2 reduce-scatter.7
  455.2 106.7 reduce-scatter.9
  586.9 148.4 reduce-scatter.11
  738.1 47.2 reduce-scatter.13

commit v3 on v2

--- a/solution.py
+++ b/solution.py
@@ -10,9 +10,8 @@
 CHUNK = 32
 CHUNKS = 4
 MESH = pl.DeviceIdType.MESH
-VMEM = 48 << 20
+VMEM = 50 << 20
 READ_COST = 17 << 30
-BACK_COST = 34 << 30
 
 
 EPSILON = 1e-06
@@ -20,34 +19,84 @@
 PRECISE = lax.Precision.HIGHEST
 
 
-def passed_along(array, axis, by):
-    devices = lax.axis_size(axis)
-    pairs = [(i, i + by) for i in range(devices) if 0 <= i + by < devices]
-    return lax.ppermute(array, axis, pairs)
-
-
-def width_blocks(array):
+def width_blocks(array, parity):
+    count = lax.axis_size("seq")
+    wide = array.shape[1] // count
+    return jnp.stack(
+        [
+            lax.dynamic_slice_in_dim(array, (2 * line + parity) * wide, wide, 1)
+            for line in range(count // 2)
+        ]
+    )
+
+
+def whole_tiles(array):
+    return array.shape[1] // lax.axis_size("seq") % 128 == 0
+
+
+def wide_to_send(array):
+    array = array.astype(jnp.float32)
+    if whole_tiles(array):
+        return array
+    return width_blocks(array, 1 - lax.axis_index("seq") % 2)
+
+
+def product_kernel(layout, *refs):
+    out_ref, sides = refs[-2:]
+    refs = list(refs[1:-2])
+    first = pl.program_id(0) == 0
+    at = 0
+    for narrows in layout:
+        own, theirs = refs.pop(0), refs.pop(0)
+        block = jnp.concatenate(
+            [own[...].reshape(own.shape[-2:]), theirs[0].astype(jnp.bfloat16)], axis=0
+        )
+        for _ in range(narrows):
+            own_narrow, their_narrow = refs.pop(0), refs.pop(0)
+            rows, size = own_narrow.shape
+
+            @pl.when(first)
+            def _(at=at, own_narrow=own_narrow, their_narrow=their_narrow, rows=rows, size=size):
+                sides[:rows, at : at + size] = own_narrow[...]
+                sides[rows:, at : at + size] = their_narrow[...].astype(jnp.bfloat16)
+
+            out_ref[0, :, at : at + size] = tn(block, sides[:, at : at + size])
+            at += size
+
+
+def pair_products(*jobs):
     count = lax.axis_size("seq")
     lines = count // 2
-    place = lax.axis_index("seq")
-    odd = place % 2
-    wide = array.shape[1] // count
-    roles = list(range(lines))
-
-    def blocks(parity):
-        return jnp.stack(
-            [lax.dynamic_slice_in_dim(array, (2 * r + parity) * wide, wide, 1) for r in roles]
-        )
-
-    return blocks(odd), blocks(1 - odd).astype(jnp.float32)
-
-
-def pair_product(wide, narrow, wide_first):
-    rule = "ztd,tf->zdf" if wide_first else "ztd,tf->zfd"
-    return sum(
-        jnp.einsum(rule, w, n, preferred_element_type=jnp.float32)
-        for w, n in zip(wide, narrow)
-    )
+    parity = lax.axis_index("seq") % 2
+    ins, specs, total = [], [], 0
+    for (own, theirs), narrows in jobs:
+        rows, wide = own.shape[0], own.shape[1] // count
+        if whole_tiles(own):
+            ins.append(own)
+            specs.append(pl.BlockSpec((rows, wide), lambda i, p: (0, 2 * i + p[0])))
+        else:
+            ins.append(width_blocks(own, parity))
+            specs.append(pl.BlockSpec((1, rows, wide), lambda i, p: (i, 0, 0)))
+        ins.append(theirs)
+        specs.append(pl.BlockSpec((1, rows, wide), lambda i, p: (i, 0, 0)))
+        for pair in narrows:
+            for side in pair:
+                ins.append(side)
+                specs.append(pl.BlockSpec(side.shape, lambda i, p: (0, 0)))
+            total += pair[0].shape[1]
+    return pl.pallas_call(
+        functools.partial(product_kernel, [len(narrows) for _, narrows in jobs]),
+        out_shape=jax.ShapeDtypeStruct((lines, wide, total), jnp.float32),
+        grid_spec=pltpu.PrefetchScalarGridSpec(
+            num_scalar_prefetch=1,
+            grid=(lines,),
+            in_specs=specs,
+            out_specs=pl.BlockSpec((1, wide, total), lambda i, p: (i, 0, 0)),
+            scratch_shapes=[pltpu.VMEM((2 * rows, total), jnp.bfloat16)],
+        ),
+        compiler_params=pltpu.CompilerParams(vmem_limit_bytes=VMEM),
+        cost_estimate=cost(4 * rows * wide * lines * total, 8 * wide * lines * total),
+    )(parity.reshape(1).astype(jnp.int32), *ins)
 
 
 def line_sum(product):
@@ -110,6 +159,12 @@
 def nt(left, right):
     return lax.dot_general(
         left, right, (((1,), (1,)), ((), ())), preferred_element_type=jnp.float32
+    )
+
+
+def tn(left, right):
+    return lax.dot_general(
+        left, right, (((0,), (0,)), ((), ())), preferred_element_type=jnp.float32
     )
 
 
@@ -219,7 +274,7 @@
 
 
 def back_query_kernel(
-    q_ref, k_ref, v_ref, log_ref, new_ref, doc_ref, prev_ref, score_ref, prob_ref, ks_ref, vs_ref, g_ref,
+    piece, pieces, q_ref, k_ref, v_ref, log_ref, new_ref, doc_ref, prev_ref, score_ref, prob_ref, ks_ref, vs_ref, g_ref,
     dq_ref, dk_ref, dv_ref, held_ref, gained_ref, xk_ref, xv_ref, dkin_ref, dvin_ref, span_s,
 ):
     size = span_s.shape[0]
@@ -364,13 +419,13 @@
     wide = jax.ShapeDtypeStruct((rows, width), f32)
     states = jax.ShapeDtypeStruct((count, slots, width), f32)
     state = jax.ShapeDtypeStruct((slots, width), f32)
-    return pl.pallas_call(
+    return (
         back_query_kernel,
-        out_shape=(wide, wide, wide, narrow, narrow, states, states, state, state),
-        scratch_shapes=[pltpu.VMEM((CHUNK, CHUNK, slots), f32)],
-        compiler_params=pltpu.CompilerParams(vmem_limit_bytes=VMEM),
-        cost_estimate=cost(BACK_COST, 10 << 20),
-    )(queries, keys, values, logs, new, docs, prev, scores, probs, key_states, value_states, grads)
+        (queries, keys, values, logs, new, docs, prev, scores, probs, key_states, value_states, grads),
+        (wide, wide, wide, narrow, narrow, states, states, state, state),
+        (pltpu.VMEM((CHUNK, CHUNK, slots), f32),),
+        (False,) * 12,
+    )
 
 
 def back_key(keys, values, logs, new, docs, prev, dk, dv, held, gained, xk, xv, dk_end, dv_end, total):
@@ -395,7 +450,7 @@
     return place + by * (1 - 2 * ((place // by) % 2))
 
 
-def exchange_kernel(names, count, heads, reverse, *refs):
+def exchange_kernel(names, count, heads, reverse, work, early, *refs):
     refs = dict(zip(names, refs))
     wides = [n for n in names if n.startswith("wide_in")]
     narrows = [n for n in names if n.startswith("narrow_in")]
@@ -408,7 +463,7 @@
     hops = [1 << k for k in range(1, heads.bit_length() - 1)]
 
     greeted = []
-    if wides or narrows:
+    if wides or narrows or early is not None:
         greeted.append((partner, None))
     if wides or "part" in refs:
         greeted.append((sibling, None))
@@ -445,7 +500,34 @@
         size = ref.shape[0] // 2
         return ref.at[pl.ds((head % 2) * size, size)]
 
+    def blocks_of(source, target, i):
+        lines, rows, wide = target.shape
+        if len(source.shape) == 3:
+            return [copy(half_of(source), half_of(target), sems("wide", i * lines), partner)]
+        copies = []
+        for k in range(lines // 2):
+            line = (head % 2) * (lines // 2) + k
+            start = pl.multiple_of((2 * line + 1 - place % 2) * wide, 128)
+            copies.append(
+                copy(
+                    source.at[:, pl.ds(start, wide)], target.at[line],
+                    sems("wide", i * lines + k), partner,
+                )
+            )
+        return copies
+
     waits, forwards, states = [], [], []
+    fill = None
+    if early is not None:
+        source, target = refs["early_scratch0"], refs["narrow_out0"]
+
+        def send_tile(i, columns):
+            moved = copy(source.at[:, columns], target.at[:, columns], sems("narrow", i), partner)
+            moved.start()
+            waits.append(moved)
+
+        fill = early(send_tile, refs, [refs[n] for n in names if n.startswith("early")])
+    tiles_sent, waits = waits, []
     if "state" in refs:
         inside, received, before = refs["inside"], refs["received"], refs["before"]
         inside[0] = refs["state"][...]
@@ -463,55 +545,10 @@
         rows = part.shape[0] // CHUNKS
         half = rows // 2
         low = head % 2
-        for c in range(CHUNKS):
-            start = pl.multiple_of(c * rows + (1 - low) * half, 8)
-            moved = copy(part.at[pl.ds(start, half)], refs["near"].at[c], sems("near", c), sibling)
-            moved.start()
-            waits.append(moved)
-    for i, name in enumerate(wides):
-        moved = copy(
-            half_of(refs[name]), half_of(refs[name.replace("in", "out")]), sems("wide", i), partner
-        )
-        moved.start()
-        forwards.append((name.replace("in", "out"), moved))
-    for i, name in enumerate(narrows):
-        moved = copy(refs[name], refs[name.replace("in", "out")], sems("narrow", i), partner)
-        moved.start()
-        waits.append(moved)
-
-    if "state" in refs:
-        lane = lax.broadcasted_iota(jnp.int32, before.shape, 1)
-        before[...] = jnp.where(lane < 128, 1.0, 0.0)
-
-        def composed(earlier, later):
-            return later[:, :1] * earlier + jnp.where(lane >= 128, later, 0.0)
-
-        for k, by in enumerate(spans_of):
-            moved = states[k]
-            if k:
-
-                @pl.when(left >= by)
-                def _(moved=moved):
-                    moved.start()
-
-            if k + 1 < len(spans_of):
-                inside[k + 1] = inside[k]
-
-            @pl.when(ahead >= by)
-            def _(k=k, moved=moved):
-                moved.wait_recv()
-                before[...] = composed(received[k], before[...])
-                if k + 1 < len(spans_of):
-                    inside[k + 1] = composed(received[k], inside[k])
-
-            @pl.when(left >= by)
-            def _(moved=moved):
-                moved.wait_send()
-
-    if "part" in refs:
         own, arrived = refs["own"], refs["arrived"]
         across = []
-        for c in range(CHUNKS):
+
+        def cross(c):
             waits[c].wait_recv()
             start = pl.multiple_of(c * rows + low * half, 8)
             own[0, c] = part[pl.ds(start, half), :] + refs["near"][c]
@@ -520,6 +557,74 @@
             )
             moved.start()
             across.append(moved)
+
+        for c in range(CHUNKS):
+            if fill is not None:
+                fill(c, rows)
+            start = pl.multiple_of(c * rows + (1 - low) * half, 8)
+            moved = copy(part.at[pl.ds(start, half)], refs["near"].at[c], sems("near", c), sibling)
+            moved.start()
+            waits.append(moved)
+            if fill is not None:
+                cross(c)
+    for i, name in enumerate(wides):
+        name, source = name.replace("in", "out"), refs[name]
+        moved = blocks_of(source, refs[name], i)
+        for one in moved:
+            one.start()
+        forwards.append((name, moved))
+    for i, name in enumerate(narrows):
+        moved = copy(refs[name], refs[name.replace("in", "out")], sems("narrow", i), partner)
+        moved.start()
+        waits.append(moved)
+
+    def run_work(piece, pieces):
+        if early is not None:
+            outer_product_beside(piece, pieces, refs)
+        if work is not None:
+            work(piece, pieces, *[refs[n] for n in names if n.startswith("work")])
+
+    if "part" in refs and fill is None:
+        for c in range(CHUNKS):
+            cross(c)
+    if "state" not in refs:
+        run_work(0, 1)
+    if "state" in refs:
+        lane = lax.broadcasted_iota(jnp.int32, before.shape, 1)
+        before[...] = jnp.where(lane < 64, 1.0, jnp.where(lane < 128, -1.0, 0.0))
+
+        def composed(earlier, later):
+            keep = later[:, :1]
+            if not reverse:
+                keep = jnp.where(earlier[:, 64:65] == later[:, 64:65], keep, 0.0)
+            values = keep * earlier + later
+            return jnp.where(lane >= 128, values, jnp.where(lane < 64, earlier * later, later))
+
+        for k, by in enumerate(spans_of):
+            moved = states[k]
+            if k:
+
+                @pl.when(left >= by)
+                def _(moved=moved):
+                    moved.start()
+
+            if k + 1 < len(spans_of):
+                inside[k + 1] = inside[k]
+
+            run_work(k, len(spans_of))
+
+            @pl.when(ahead >= by)
+            def _(k=k, moved=moved):
+                moved.wait_recv()
+                before[...] = composed(received[k], before[...]) if k else received[k]
+                if k + 1 < len(spans_of):
+                    inside[k + 1] = composed(received[k], inside[k])
+
+            @pl.when(left >= by)
+            def _(moved=moved):
+                moved.wait_send()
+
+    if "part" in refs:
         for k in range(1, len(hops)):
             later = []
             for c in range(CHUNKS):
@@ -547,21 +652,30 @@
             back[c].wait()
         waits = waits[CHUNKS:]
     for i, (name, moved) in enumerate(forwards):
-        moved.wait()
+        for one in moved:
+            one.wait()
         onward = copy(half_of(refs[name]), half_of(refs[name]), sems("onward", i), sibling)
         onward.start()
         waits.append(onward)
-    for moved in waits:
+    for moved in waits + tiles_sent:
         moved.wait()
-
-
-def exchange(number, part=None, state=None, reverse=False, wides=(), narrows=()):
+    if early is not None:
+        for one in refs["finish"][-1]:
+            one.wait()
+
+
+def exchange(
+    number, part=None, state=None, reverse=False, wides=(), narrows=(), work=None, early=None
+):
     count, heads = lax.axis_size("seq"), lax.axis_size("head")
     f32 = jnp.float32
     vmem, hbm = pl.BlockSpec(memory_space=pltpu.VMEM), pl.BlockSpec(memory_space=pl.ANY)
     ins, outs, scratch = [], [], []
     if part is not None:
-        ins.append(("part", part, vmem))
+        if early is None:
+            ins.append(("part", part, vmem))
+        else:
+            scratch.append(("part", pltpu.VMEM(part.shape, f32)))
         outs.append(("sum", part, vmem))
         half = (CHUNKS, part.shape[0] // CHUNKS // 2, part.shape[1])
         steps = heads.bit_length() - 2
@@ -578,18 +692,36 @@
         steps = count.bit_length() - 1
         scratch += [(n, pltpu.VMEM((steps,) + state.shape, f32)) for n in ("inside", "received")]
         scratch += [("state" + end, pltpu.SemaphoreType.DMA((steps,))) for end in ("_send", "_recv")]
-    for kind, arrays in (("wide", wides), ("narrow", narrows)):
-        ins += [(f"{kind}_in{i}", a, hbm) for i, a in enumerate(arrays)]
-        outs += [(f"{kind}_out{i}", a, hbm) for i, a in enumerate(arrays)]
-        for name in (kind, "onward") if kind == "wide" else (kind,):
+    lines = count // 2
+    for kind, arrays, each in (("wide", wides, lines), ("narrow", narrows, 1)):
+        for i, a in enumerate(arrays):
+            shape = a.shape
+            if kind == "wide" and len(shape) == 2:
+                shape = (lines, shape[0], shape[1] // count)
+            ins.append((f"{kind}_in{i}", a, hbm))
+            outs.append((f"{kind}_out{i}", jax.ShapeDtypeStruct(shape, f32), hbm))
+        for name, size in ((kind, each), ("onward", 1)) if kind == "wide" else ((kind, 1),):
             if arrays:
                 scratch += [
-                    (name + end, pltpu.SemaphoreType.DMA((len(arrays),))) for end in ("_send", "_recv")
+                    (name + end, pltpu.SemaphoreType.DMA((len(arrays) * size,)))
+                    for end in ("_send", "_recv")
                 ]
+    if early is not None:
+        early, given, sent_shape, tiles, made, extra = early
+        ins += [(f"early_in{i}", a, hbm) for i, a in enumerate(given)]
+        outs.append(("narrow_out0", jax.ShapeDtypeStruct(sent_shape, f32), hbm))
+        outs += [(f"early_out{i}", a, hbm) for i, a in enumerate(made)]
+        scratch += [(f"early_scratch{i}", a) for i, a in enumerate(extra)]
+        scratch += [("narrow" + end, pltpu.SemaphoreType.DMA((tiles,))) for end in ("_send", "_recv")]
+    if work is not None:
+        work, given, made, extra, places = work
+        ins += [(f"work_in{i}", a, hbm if p else vmem) for i, (a, p) in enumerate(zip(given, places))]
+        outs += [(f"work_out{i}", a, vmem) for i, a in enumerate(made)]
+        scratch += [(f"work_scratch{i}", a) for i, a in enumerate(extra)]
     names = [n for n, *_ in ins] + [n for n, *_ in outs] + [n for n, _ in scratch]
     return pl.pallas_call(
-        functools.partial(exchange_kernel, names, count, heads, reverse),
-        out_shape=tuple(jax.ShapeDtypeStruct(a.shape, f32) for _, a, _ in outs),
+        functools.partial(exchange_kernel, names, count, heads, reverse, work, early),
+        out_shape=tuple(jax.ShapeDtypeStruct(a.shape, a.dtype) for _, a, _ in outs),
         in_specs=[spec for *_, spec in ins],
         out_specs=tuple(spec for *_, spec in outs),
         scratch_shapes=[s for _, s in scratch],
@@ -644,8 +776,168 @@
     )(array)
 
 
-def state_of(keep, keys, values):
-    return jnp.concatenate([jnp.broadcast_to(keep[:, None], (keep.shape[0], 128)), keys, values], axis=1)
+def state_of(keep, doc, keys, values):
+    keep = jnp.broadcast_to(keep[:, None], (keep.shape[0], 64))
+    return jnp.concatenate([keep, jnp.full_like(keep, doc), keys, values], axis=1)
+
+
+def matmul_work(product, column, piece, pieces, left_ref, right_ref, out_ref, left, right, sems):
+    copies = [
+        pltpu.make_async_copy(left_ref, left, sems.at[0]),
+        pltpu.make_async_copy(right_ref, right, sems.at[1]),
+    ]
+    if piece == 0:
+        for one in copies:
+            one.start()
+        for one in copies:
+            one.wait()
+
+    def tile(i, carry):
+        columns = pl.ds(pl.multiple_of(i * column, column), column)
+        side = right[columns, :] if product is nt else right[:, columns]
+        out_ref[:, columns] = product(left[...], side)
+        return carry
+
+    tiles = out_ref.shape[1] // column
+    lax.fori_loop(tiles * piece // pieces, tiles * (piece + 1) // pieces, tile, 0)
+
+
+def column_tiles(size):
+    wide = 256 if size >= 256 else size
+    return [(at, min(wide, size - at)) for at in range(0, size, wide)]
+
+
+def hidden_units(send_tile, refs, own):
+    (normed_in, gate_in, up_in, down_in, d_act_in, act_out, d_gate_out, d_up_out, gate_f_out, up_f_out, ffn_out,
+     act_f, act_ref, d_gate_ref, d_up_ref, gate_f_ref, up_f_ref, ffn_ref, normed, w_gate, w_up, w_down, d_act, sems, tile_sems, out_sems) = own
+    whole = [
+        pltpu.make_async_copy(normed_in, normed, sems.at[0]),
+        pltpu.make_async_copy(d_act_in, d_act, sems.at[1]),
+        pltpu.make_async_copy(down_in, w_down, sems.at[2]),
+    ]
+    parts = []
+    tiles = column_tiles(act_ref.shape[1])
+    for i, (at, size) in enumerate(tiles):
+        columns = pl.ds(at, size)
+        parts.append(
+            [
+                pltpu.make_async_copy(gate_in.at[:, columns], w_gate.at[:, columns], tile_sems.at[0, i]),
+                pltpu.make_async_copy(up_in.at[:, columns], w_up.at[:, columns], tile_sems.at[1, i]),
+            ]
+        )
+    whole[0].start()
+    for one in parts[0]:
+        one.start()
+    whole[1].start()
+    for pair in parts[1:]:
+        for one in pair:
+            one.start()
+    whole[2].start()
+    whole[0].wait()
+    for i, (at, size) in enumerate(tiles):
+        columns = pl.ds(at, size)
+        for one in parts[i]:
+            one.wait()
+        gate = nn(normed[...], w_gate[:, columns])
+        up = nn(normed[...], w_up[:, columns])
+        if i == 0:
+            whole[1].wait()
+        sig = jax.nn.sigmoid(gate)
+        silu = gate * sig
+        pull = d_act[:, columns]
+        act = (silu * up).astype(jnp.bfloat16)
+        act_ref[:, columns] = act
+        act_f[:, columns] = act.astype(jnp.float32)
+        send_tile(i, columns)
+        d_gate = (pull * up * sig * (1.0 + gate * (1.0 - sig))).astype(jnp.bfloat16)
+        d_up = (pull * silu).astype(jnp.bfloat16)
+        d_gate_ref[:, columns] = d_gate
+        d_up_ref[:, columns] = d_up
+        gate_f_ref[:, columns] = d_gate.astype(jnp.float32)
+        up_f_ref[:, columns] = d_up.astype(jnp.float32)
+
+    kept = [(act_ref, act_out), (d_gate_ref, d_gate_out), (d_up_ref, d_up_out),
+            (gate_f_ref, gate_f_out), (up_f_ref, up_f_out), (ffn_ref, ffn_out)]
+    kept = [pltpu.make_async_copy(a, b, out_sems.at[i]) for i, (a, b) in enumerate(kept)]
+    for one in kept[:-1]:
+        one.start()
+    part = refs["part"]
+
+    def fill(c, rows):
+        mine = pl.ds(c * rows, rows)
+
+        def tile(i, carry):
+            columns = pl.ds(pl.multiple_of(i * 256, 256), 256)
+            part[mine, columns] = nt(d_gate_ref[mine, :], w_gate[columns, :]) + nt(
+                d_up_ref[mine, :], w_up[columns, :]
+            )
+            return carry
+
+        lax.fori_loop(0, part.shape[1] // 256, tile, 0)
+
+    refs["finish"] = (whole[2], act_ref, w_down, ffn_ref, kept)
+    return fill
+
+
+def outer_product_beside(piece, pieces, refs):
+    copied, act, w_down, out, kept = refs["finish"]
+    copied.wait()
+
+    def tile(i, carry):
+        columns = pl.ds(pl.multiple_of(i * 256, 256), 256)
+        out[:, columns] = nn(act[...], w_down[:, columns])
+        return carry
+
+    lax.fori_loop(0, out.shape[1] // 256, tile, 0)
+    kept[-1].start()
+
+
+def hidden_units_early(normed_mid, w_gate, w_up, w_down, d_act):
+    rows, width = normed_mid.shape
+    hidden = w_gate.shape[1]
+    tiles = len(column_tiles(hidden))
+    half = jax.ShapeDtypeStruct((rows, hidden), jnp.bfloat16)
+    full = jax.ShapeDtypeStruct((rows, hidden), jnp.float32)
+    return (
+        hidden_units,
+        (normed_mid, w_gate, w_up, w_down, d_act),
+        (rows, hidden),
+        tiles,
+        (half, half, half, full, full, jax.ShapeDtypeStruct((rows, width), jnp.float32)),
+        (
+            pltpu.VMEM((rows, hidden), jnp.float32),
+            pltpu.VMEM((rows, hidden), jnp.bfloat16),
+            pltpu.VMEM((rows, hidden), jnp.bfloat16),
+            pltpu.VMEM((rows, hidden), jnp.bfloat16),
+            pltpu.VMEM((rows, hidden), jnp.float32),
+            pltpu.VMEM((rows, hidden), jnp.float32),
+            pltpu.VMEM((rows, width), jnp.float32),
+            pltpu.VMEM(normed_mid.shape, jnp.bfloat16),
+            pltpu.VMEM(w_gate.shape, jnp.bfloat16),
+            pltpu.VMEM(w_up.shape, jnp.bfloat16),
+            pltpu.VMEM(w_down.shape, jnp.bfloat16),
+            pltpu.VMEM(d_act.shape, jnp.float32),
+            pltpu.SemaphoreType.DMA((3,)),
+            pltpu.SemaphoreType.DMA((2, tiles)),
+            pltpu.SemaphoreType.DMA((6,)),
+        ),
+    )
+
+
+def matmul_beside(product, left, right):
+    columns = right.shape[0] if product is nt else right.shape[1]
+    column = 256 if columns % 256 == 0 else 128
+    return (
+        functools.partial(matmul_work, product, column),
+        (left, right),
+        (jax.ShapeDtypeStruct((left.shape[0], columns), jnp.float32),),
+        (
+            pltpu.VMEM(left.shape, left.dtype),
+            pltpu.VMEM(right.shape, right.dtype),
+            pltpu.SemaphoreType.DMA((2,)),
+        ),
+        (True, True),
+    )
 
 
 def body(
@@ -671,7 +963,6 @@
     width = stream.shape[1]
     slots = w_slot.shape[2]
     head_width = w_query.shape[1]
-    prior = passed_along(seg_ids[tok_rows - 1 :], "seq", 1)[0]
     stream_f = stream.astype(jnp.float32)
     scale_in = rms_scale(stream_f)
     normed_in = (stream_f * scale_in * attn_gain).astype(jnp.bfloat16)
@@ -692,26 +983,20 @@
     total = running[tok_rows - 1]
     in_last = (seg_ids == last_doc)[:, None]
     factor = jnp.where(in_last, jnp.exp(jnp.where(in_last, total - running, 0.0)) * new, 0.0)
+    def wide_float(array):
+        return array.astype(jnp.float32)
+
+    local_key = precise_left_t(factor, key_rows.astype(jnp.float32))
+    local_value = precise_left_t(factor, value_rows.astype(jnp.float32))
     docs = seg_ids.astype(jnp.float32)
-    before = jnp.concatenate([prior.astype(jnp.float32)[None], docs[CHUNK - 1 : -1 : CHUNK]])
+    own_state = state_of(jnp.exp(total), docs[tok_rows - 1], local_key, local_value)
+    prefix, d_act = exchange(0, state=own_state, work=matmul_beside(nt, cotangent, w_down))
+    key_in, value_in = prefix[:, 128 : 128 + head_width], prefix[:, 128 + head_width :]
+    prior = prefix[0, 64]
+    decay_all = jnp.where(docs[tok_rows - 1] == prior, jnp.exp(total), 0.0)
+    before = jnp.concatenate([prior[None], docs[CHUNK - 1 : -1 : CHUNK]])
     docs = jnp.broadcast_to(docs[:, None], (tok_rows, slots))
     before = jnp.broadcast_to(jnp.repeat(before, CHUNK)[:, None], (tok_rows, slots))
-
-    def with_partner(own, received):
-        return own, received.astype(jnp.bfloat16)
-
-    def wide_float(array):
-        return array.astype(jnp.float32)
-
-    local_key = precise_left_t(factor, key_rows.astype(jnp.float32))
-    local_value = precise_left_t(factor, value_rows.astype(jnp.float32))
-    decay_all = jnp.where(last_doc == prior, jnp.exp(total), 0.0)
-    (prefix,) = exchange(0, state=state_of(decay_all, local_key, local_value))
-    key_in, value_in = prefix[:, 128 : 128 + head_width], prefix[:, 128 + head_width :]
-    d_act = dot_right_t(cotangent, w_down)
-    key_in, d_act = together(key_in, d_act)
-    own_dy, their_dy = width_blocks(cotangent)
-    own_in, their_in = width_blocks(normed_in)
     slot_read, scores, probs, key_states, value_states = read_slots(
         query_rows, key_rows, value_rows, log_decay, new, docs, before, key_in, value_in
     )
@@ -721,37 +1006,24 @@
     gate_silu = gate_act * gate_sig
     mixed_heads = (normed_read * gate_silu).astype(jnp.bfloat16)
     branch, from_dy, from_in = exchange(
-        1, part=plain_dot(mixed_heads, w_out), wides=(their_dy, their_in)
-    )
-    wide_dy = with_partner(own_dy, from_dy)
-    wide_in = with_partner(own_in, from_in)
+        1,
+        part=plain_dot(mixed_heads, w_out),
+        wides=(wide_to_send(cotangent), wide_to_send(normed_in)),
+    )
+    wide_dy = cotangent, from_dy
+    wide_in = normed_in, from_in
     hidden = stream_f + branch
     scale_mid = rms_scale(hidden)
     normed_mid = (hidden * scale_mid * mlp_gain).astype(jnp.bfloat16)
-    gate_pre = plain_dot(normed_mid, w_gate)
-    up_pre = plain_dot(normed_mid, w_up)
-    pre_sig = jax.nn.sigmoid(gate_pre)
-    pre_silu = gate_pre * pre_sig
-    ffn_act = (pre_silu * up_pre).astype(jnp.bfloat16)
     upstream = cotangent.astype(jnp.float32)
-    d_gate = (d_act * up_pre * pre_sig * (1.0 + gate_pre * (1.0 - pre_sig))).astype(jnp.bfloat16)
-    d_up = (d_act * pre_silu).astype(jnp.bfloat16)
-    d_mid, from_act = exchange(
+    d_mid, from_act, ffn_act, d_gate, d_up, d_gate_f, d_up_f, ffn_part = exchange(
         2,
-        part=dot_right_t(d_gate, w_gate) + dot_right_t(d_up, w_up),
-        narrows=(wide_float(ffn_act),),
-    )
-    grad_down = pair_product(wide_dy, with_partner(ffn_act, from_act), False)
+        part=jax.ShapeDtypeStruct((tok_rows, width), jnp.float32),
+        early=hidden_units_early(normed_mid, w_gate, w_up, w_down, d_act),
+    )
+    grad_down = pair_products((wide_dy, [(ffn_act, from_act)]))
     d_mid, grad_down = together(d_mid, grad_down)
     grad_down = line_sum(grad_down)
-    own_mid, their_mid = width_blocks(normed_mid)
-    ffn_part, d_mid = together(plain_dot(ffn_act, w_down), d_mid)
-    ffn_out, from_mid, from_gate = exchange(
-        3, part=ffn_part, wides=(their_mid,), narrows=(wide_float(d_gate),)
-    )
-    wide_mid = with_partner(own_mid, from_mid)
-    grad_gate = pair_product(wide_mid, with_partner(d_gate, from_gate), True)
-    d_mid, grad_gate = together(d_mid, grad_gate)
     grad_mlp_gain = jnp.sum(d_mid * hidden * scale_mid, axis=0)
     scaled_mid = d_mid * mlp_gain
     d_hidden = (
@@ -761,7 +1033,6 @@
     )
     d_branch = d_hidden.astype(jnp.bfloat16)
     d_mixed = dot_right_t(d_branch, w_out)
-    own_branch, their_branch = width_blocks(d_branch)
     d_gate_act = (d_mixed * normed_read * gate_sig * (1.0 + gate_act * (1.0 - gate_sig))).astype(
         jnp.bfloat16
     )
@@ -771,24 +1042,32 @@
     d_read = scale_read * scaled_read - slot_read * scale_read**3 * jnp.mean(
         scaled_read * slot_read, axis=1, keepdims=True
     )
-    grad_gate, grad_down, unused_read = together(grad_gate, grad_down, d_read)
+    from_mid, from_gate, *back = exchange(
+        3,
+        wides=(wide_to_send(normed_mid),),
+        narrows=(d_gate_f,),
+        work=back_query(
+            query_rows, key_rows, value_rows, log_decay, new, docs, before, scores, probs, key_states, value_states, d_read
+        ),
+    )
+    wide_mid = normed_mid, from_mid
+    grad_gate = pair_products((wide_mid, [(d_gate, from_gate)]))
+    d_query, d_key, d_value, held, gained, to_keys, to_values, key_back, value_back = back
+    query_back = d_query.astype(jnp.bfloat16)
+    key_back, grad_gate = together(key_back, grad_gate)
+    grad_gate, grad_down = together(grad_gate, grad_down)
     grad_gate = line_sum(grad_gate)
-    d_query, d_key, d_value, held, gained, to_keys, to_values, key_back, value_back = back_query(
-        query_rows, key_rows, value_rows, log_decay, new, docs, before, scores, probs, key_states, value_states, d_read
-    )
-    query_back = d_query.astype(jnp.bfloat16)
-    suffix, from_up, from_outgate = exchange(
+    ffn_out, suffix, from_up, from_outgate = exchange(
         4,
-        state=state_of(decay_all, key_back, value_back),
+        part=ffn_part,
+        state=state_of(decay_all, 0.0, key_back, value_back),
         reverse=True,
-        narrows=(wide_float(d_up), wide_float(d_gate_act)),
-    )
-    grad_up = pair_product(wide_mid, with_partner(d_up, from_up), True)
+        narrows=(d_up_f, wide_float(d_gate_act)),
+    )
+    grad_up = pair_products((wide_mid, [(d_up, from_up)]))
     key_end, value_end = suffix[:, 128 : 128 + head_width], suffix[:, 128 + head_width :]
     end_total = jnp.sum(key_states[-1] * key_end + value_states[-1] * value_end, axis=1)[None, :]
     d_key, grad_up = together(d_key, grad_up)
-    grad_up, grad_gate = together(grad_up, grad_gate)
-    grad_up = line_sum(grad_up)
     key_back, value_back, d_logs = back_key(
         key_rows, value_rows, log_decay, new, docs, before, d_key, d_value, held, gained,
         to_keys, to_values, key_end, value_end, end_total,
@@ -803,23 +1082,29 @@
         + dot_right_t(d_gate_act, w_outgate)
         + precise_right_t(d_ranked, w_low.astype(jnp.float32))
     )
+    grad_up, grad_gate, d_in_part = together(grad_up, grad_gate, d_in_part)
+    grad_up = line_sum(grad_up)
     d_in, from_branch, *from_mixer = exchange(
         5,
         part=d_in_part,
-        wides=(their_branch,),
+        wides=(wide_to_send(d_branch),),
         narrows=[wide_float(a) for a in (query_back, key_back, value_back, mixed_heads)],
     )
-    from_mixed = from_mixer.pop()
-    from_mixer = [from_outgate, *from_mixer]
-    wide_branch = with_partner(own_branch, from_branch)
-    grad_out = pair_product(wide_branch, with_partner(mixed_heads, from_mixed), False)
-    own_mixer = jnp.concatenate([d_gate_act, query_back, key_back, value_back], axis=1)
-    their_mixer = jnp.concatenate([a.astype(jnp.bfloat16) for a in from_mixer], axis=1)
-    grad_mixer = pair_product(wide_in, (own_mixer, their_mixer), True)
-    grad_out, grad_up, d_in = together(grad_out, grad_up, d_in)
-    grad_out = line_sum(grad_out)
-    grad_mixer = line_sum(grad_mixer)
-    grad_outgate, grad_query, grad_key, grad_value = jnp.split(grad_mixer, 4, axis=1)
+    grad_rest = pair_products(
+        (
+            wide_in,
+            [
+                (d_gate_act, from_outgate),
+                (query_back, from_mixer[0]),
+                (key_back, from_mixer[1]),
+                (value_back, from_mixer[2]),
+            ],
+        ),
+        ((d_branch, from_branch), [(mixed_heads, from_mixer[3])]),
+    )
+    grad_rest, grad_up, d_in = together(grad_rest, grad_up, d_in)
+    grad_rest = line_sum(grad_rest)
+    grad_outgate, grad_query, grad_key, grad_value, grad_out = jnp.split(grad_rest, 5, axis=1)
     result = hidden + ffn_out
     squares = jnp.stack(
         [jnp.sum(stream_f * stream_f), jnp.sum(hidden * hidden), jnp.sum(result * result)]
@@ -858,11 +1143,11 @@
         small[3].reshape(1, -1, slots // count),
         small[4][None, :],
         small[5][None, :],
-        grad_out,
+        grad_out.T,
         small[1],
         grad_gate,
         grad_up,
-        grad_down,
+        grad_down.T,
     )
     mixer_parts = summed[:10]
     ffn_parts = summed[10:]

time: 800 us -> 753 us (0.941)
  matrix products: 89.1 us -> 28.6 us
  Pallas kernels: 420 us -> 445 us
  starting transfers between devices: 17.4 us -> 0.62 us
  other arithmetic: 37.5 us -> 51.1 us
    dot_general x10 -> x0, matrix products: 28.8 us -> none  [pair_product(): jnp.einsum(rule, w, n, preferred_element_type=jnp.float32)]
    dot_general x9 -> x6, matrix products: 29.6 us -> 11.1 us  [plain_dot(): return jnp.dot(left, right, preferred_element_type=jnp.float32)]
    another operation x11 -> x0, local copies, waits for them, and re-layouts: 14.9 us -> none  [blocks(): jnp.stack([lax.dynamic_slice_in_dim(array, (2 * r + parity) * wide, wide,...]
    dot_general x8 -> x5, matrix products: 23 us -> 8.8 us  [dot_right_t(): lax.dot_general(left, right, (((1,), (1,)), ((), ())), preferred_element_...]
    pallas_call x6, Pallas kernels: 362 us -> 376 us  [exchange(): pl.pallas_call(functools.partial(exchange_kernel, names, count, heads, re...]
    reduce_scatter x5 -> x4, starting transfers between devices: 12 us -> 0.62 us  [line_sum(): lax.psum_scatter(product, 'seq', scatter_dimension=0, axis_index_groups=g...]
    unnamed x252 -> x176, local copies, waits for them, and re-layouts: 22.6 us -> 31.2 us
    pallas_call x1 -> x4, Pallas kernels: 25.7 us -> 33.9 us  [pair_products(): pl.pallas_call(functools.partial(product_kernel, [len(narrows) for _, nar...]
  transfers between devices with their start and end apart: 6 -> 4, of which waited for: 3 -> 4; matrix products, arithmetic and copies ran while one was open for 15% -> 7% of each run, Pallas kernels for 36% -> 40%
where the time goes in v3:
time: 753 us; the launch traced here: 746 us
  Pallas kernels  445 us (59%)
  waiting for transfers between devices  163 us (22%)
  other arithmetic  51.1 us (7%)
  local copies, waits for them, and re-layouts  41.6 us (6%)
  matrix products  28.6 us (4%)
  between operations  16.3 us (2%)
    pallas_call x6, Pallas kernels, exchange(): pl.pallas_call(functools.partial(exchange_kernel, names, count, heads, re...  376 us
    reduce_scatter x4, waiting for transfers between devices, line_sum(): lax.psum_scatter(product, 'seq', scatter_dimension=0, axis_index_groups=g...  163 us
    pallas_call x4, Pallas kernels, pair_products(): pl.pallas_call(functools.partial(product_kernel, [len(narrows) for _, nar...  33.9 us
    unnamed x176, local copies, waits for them, and re-layouts  31.2 us
    convert_element_type x4, other arithmetic, wide_to_send(): array = array.astype(jnp.float32)  17.3 us
  transfers between devices with their start and end apart: 4, of which 4 were waited for; matrix products, arithmetic and copies ran while one was open for 7% of the time, Pallas kernels for 40%

profile of v3, /device:TPU:0, one launch (start us, length us, event | category | flops | bytes accessed | tf_op | source)
XLA Modules:
  0.0 746.1 jit_solution(10945522078712780344)
XLA Ops:
  12.4 3.5 fusion.42
  20.9 3.7 convert_element_type.80.refs_1_
  30.6 23.8 %shard_map.296 = (f32[64,1152]{1,0:T(8,128)S(1)}, f32[384,1408]{1,0:T(8,128)}) custom-call(f32[64,1152]{1,0:T(8,128)S(1)} %concatenate.12.refs_0_, bf16[384,2048]{1,0:T(8,128)(2,1)S(1)} %copy-done.3, bf16[1408,2048]{1,0:T(8,128)(2,1)} %refs_3_.1), custom_call_target="tpu_custom_call" | custom-call | flops 42949672960 | bytes 16777216 | tf_op jit(solution)/shard_map/pallas_call | solution.py:722
  55.0 3.8 convolution_convert_fusion.2.q_ref.refs_2_
  64.8 13.0 %shard_map.297 = (f32[384,512]{1,0:T(8,128)S(1)}, f32[384,64]{1,0:T(8,128)S(1)}, f32[384,64]{1,0:T(8,128)S(1)}, f32[13,64,512]{2,1,0:T(8,128)}, f32[13,64,512]{2,1,0:T(8,128)}) custom-call(bf16[384,512]{1,0:T(8,128)(2,1)S(1)} %copy-done.38, bf16[384,512]{1,0:T(8,128)(2,1)S(1)} %copy-done.35, bf16[384,512]{1,0:T(8,128)(2,1)S(1)} %copy-done.31, ...), custom_call_target="tpu_custom_call" | custom-call | flops 18253611008 | bytes 5242880 | tf_op jit(solution)/shard_map/pallas_call | solution.py:398
  82.9 47.7 %shard_map.298 = (f32[384,2048]{1,0:T(8,128)}, f32[4,384,256]{2,1,0:T(8,128)S(1)}, f32[4,384,256]{2,1,0:T(8,128)S(1)}) custom-call(f32[384,2048]{1,0:T(8,128)} %fusion.46.refs_0_, f32[384,2048]{1,0:T(8,128)} %convert_element_type.80.refs_1_, f32[384,2048]{1,0:T(8,128)} %get-tuple-element.187.refs_2_), custom_call_target="tpu_custom_call" | custom-call | flops 42949672960 | bytes 16777216 | tf_op jit(solution)/shard_map/pallas_call | solution.py:722
  130.6 5.0 multiply_reduce_fusion.4
  135.7 4.5 fusion.41
  140.2 58.5 %shard_map.299 = (f32[384,2048]{1,0:T(8,128)}, f32[384,1408]{1,0:T(8,128)}, bf16[384,1408]{1,0:T(8,128)(2,1)S(1)}, bf16[384,1408]{1,0:T(8,128)(2,1)S(1)}, bf16[3...) custom-call(bf16[384,2048]{1,0:T(8,128)(2,1)} %get-tuple-element.184.refs_0_.refs_1_, ...), custom_call_target="tpu_custom_call" | custom-call | flops 42949672960 | bytes 16777216 | tf_op jit(solution)/shard_map/pallas_call | solution.py:722
  200.6 7.2 shard_map.300
  208.1 4.4 multiply_reduce_fusion.1
  212.5 5.6 fusion.39
  223.2 71.6 %shard_map.301 = (f32[4,384,256]{2,1,0:T(8,128)}, f32[384,1408]{1,0:T(8,128)}, f32[384,512]{1,0:T(8,128)S(1)}, f32[384,512]{1,0:T(8,128)}, f32[384,512]{1,0:T(8,...) custom-call(f32[384,2048]{1,0:T(8,128)} %get-tuple-element.183.refs_, ...), custom_call_target="tpu_custom_call" | custom-call | flops 42949672960 | bytes 16777216 | tf_op jit(solution)/shard_map/pallas_call | solution.py:722
  297.0 7.2 shard_map.302
  304.3 14.9 %reduce-scatter.5.cloned.1.call-done = f32[1,256,1408]{2,1,0:T(8,128)} async-done(((f32[4,256,1408]{2,1,0:T(8,128)}), f32[1,256,1408]{2,1,0:T(8,128)}) %reduce-scatter.5.cloned.1.call-update) | async-done | bytes 1441808 | tf_op jit(solution)/shard_map/reduce_scatter | solution.py:105
  321.8 83.0 %shard_map.303 = (f32[384,2048]{1,0:T(8,128)}, f32[64,1152]{1,0:T(8,128)S(1)}, f32[384,1408]{1,0:T(8,128)}, f32[384,512]{1,0:T(8,128)S(1)}) custom-call(f32[384,2048]{1,0:T(8,128)} %get-tuple-element.77.refs_0_, f32[64,1152]{1,0:T(8,128)S(1)} %concatenate.14.refs_1_, f32[384,1408]{1,0:T(8,128)} %get-tuple-element.94.refs_2_, f32[384,512]{1,0:T(8,128)S(1)} %copy-done.40), custom_call_target="tpu_custom_call" | custom-call | flops 42949672960 | bytes 16777216 | tf_op jit(solution)/shard_map/pallas_call | solution.py:722
  405.8 7.4 shard_map.304
  420.2 9.6 %shard_map.305 = (bf16[384,512]{1,0:T(8,128)(2,1)S(1)}, bf16[384,512]{1,0:T(8,128)(2,1)S(1)}, f32[384,64]{1,0:T(8,128)S(1)}) custom-call(bf16[384,512]{1,0:T(8,128)(2,1)S(1)} %copy-done.37, bf16[384,512]{1,0:T(8,128)(2,1)S(1)} %copy-done.33, f32[384,64]{1,0:T(8,128)S(1)} %copy-done.29, f32[384,64]{1,0:T(8,128)S(1)} %copy-done.26, ...), custom_call_target="tpu_custom_call" | custom-call | flops 18253611008 | bytes 8388608 | tf_op jit(solution)/shard_map/pallas_call | solution.py:436
  443.3 91.3 %shard_map.306 = (f32[384,2048]{1,0:T(8,128)}, f32[4,384,256]{2,1,0:T(8,128)}, f32[384,512]{1,0:T(8,128)S(1)}, f32[384,512]{1,0:T(8,128)S(1)}, f32[384,512]{1,0:T(8,128)S(1)}, /*index=5*/f32[384,512]{1,0:T(8,128)S(1)}) custom-call(f32[384,2048]{1,0:T(8,128)} %add_add_fusion.refs_0_, f32[384,2048]{1,0:T(8,128)} %get-tuple-element.178.refs_1_, ...), custom_call_target="tpu_custom_call" | custom-call | flops 42949672960 | bytes 16777216 | tf_op jit(solution)/shard_map/pallas_call | solution.py:722
  537.4 12.1 %shard_map.307 = f32[4,256,2560]{2,1,0:T(8,128)} custom-call(s32[1]{0:T(128)} %bitcast.7.refs_0_, bf16[384,2048]{1,0:T(8,128)(2,1)} %copy-done.53, f32[4,384,256]{2,1,0:T(8,128)} %copy-done.6, bf16[384,512]{1,0:T(8,128)(2,1)S(1)} %get-tuple-element.182.refs_3_, f32[384,512]{1,0:T(8,128)S(1)} %copy-done.15, bf16[384,512]{1,0:T(8,128)(2,1)S(1)} %get-tuple-element.177.refs_5_, ...), custom_call_target="tpu_custom_call" | custom-call | flops 4026531840 | bytes 20971520 | tf_op jit(solution)/shard_map/pallas_call | solution.py:87
  559.1 4.9 fusion.9
  564.0 7.5 %multiply_reduce_fusion.3 = (f32[]{:T(128)}, f32[]{:T(128)}, bf16[384,2048]{1,0:T(8,128)(2,1)}, bf16[384,2048]{1,0:T(8,128)(2,1)}) fusion(f32[384,2048]{1,0:T(8,128)} %get-tuple-element.186, f32[384,2048]{1,0:T(8,128)} %get-tuple-element.95, f32[384]{0:T(512)S(1)} %broadcast_multiply_fusion.1, f32[384]{0:T(512)S(1)} %copy-done.76, ...), kind=kLoop, calls=%fused_computation.22 | loop fusion | flops 11010046 | bytes 17314312 | tf_op jit(solution)/shard_map/reduce_sum | solution.py:1110
  573.7 13.0 %shard_map.308 = f32[40,128]{1,0:T(8,128)S(1)} custom-call(f32[8,40,128]{2,1,0:T(8,128)S(1)} %bitcast.83), custom_call_target="tpu_custom_call" | custom-call | flops 4294967296 | bytes 1048576 | tf_op jit(solution)/shard_map/pallas_call | solution.py:762
  590.5 144.4 %reduce-scatter.11.cloned.1.call-done = f32[1,256,2560]{2,1,0:T(8,128)} async-done(((f32[4,256,2560]{2,1,0:T(8,128)}), f32[1,256,2560]{2,1,0:T(8,128)}) %reduce-scatter.11.cloned.1.call-update) | async-done | bytes 2621456 | tf_op jit(solution)/shard_map/reduce_scatter | solution.py:105
  (260 shorter events, 82.2 us)
Async XLA Ops:
  7.2 73.0 %copy-start = (bf16[512,2048]{1,0:T(8,128)(2,1)S(1)}, bf16[512,2048]{1,0:T(8,128)(2,1)}, u32[]{:S(2)}) copy-start(bf16[512,2048]{1,0:T(8,128)(2,1)} %param.28) | copy-start | bytes 6291460
  7.2 311.9 %reduce-scatter.5.cloned.1.call-start = ((), (), s32[]{:S(2)}) async-start(), calls=%async_computation.4 | async-start | bytes 7208960 | tf_op jit(solution)/shard_map/reduce_scatter | solution.py:105
  19.0 8.7 %copy-start.67 = (f32[384,64]{1,0:T(8,128)}, f32[384,64]{1,0:T(8,128)S(1)}, u32[]{:S(2)}) copy-start(f32[384,64]{1,0:T(8,128)S(1)} %get-tuple-element.212) | copy-start | bytes 294916
  59.9 17.9 %copy-start.21 = (f32[384,64]{1,0:T(8,128)}, f32[384,64]{1,0:T(8,128)S(1)}, u32[]{:S(2)}) copy-start(f32[384,64]{1,0:T(8,128)S(1)} %broadcast_in_dim.94.prev_ref.refs_8_) | copy-start | bytes 294916
  64.8 13.2 %copy-start.55 = (bf16[384,2048]{1,0:T(8,128)(2,1)S(1)}, bf16[384,2048]{1,0:T(8,128)(2,1)}, u32[]{:S(2)}) copy-start(bf16[384,2048]{1,0:T(8,128)(2,1)} %copy-done.53) | copy-start | bytes 4718596
  64.8 13.2 %copy-start.57 = (bf16[2048,512]{1,0:T(8,128)(2,1)S(1)}, bf16[2048,512]{1,0:T(8,128)(2,1)}, u32[]{:S(2)}) copy-start(bf16[2048,512]{1,0:T(8,128)(2,1)} %param.23) | copy-start | bytes 6291460
  64.8 13.2 %copy-start.80 = (f32[1,512]{1,0:T(1,128)S(1)}, f32[1,512]{1,0:T(1,128)}, u32[]{:S(2)}) copy-start(f32[1,512]{1,0:T(1,128)} %param.27) | copy-start | bytes 6148
  82.9 47.7 %copy-start.51 = (bf16[384,2048]{1,0:T(8,128)(2,1)S(1)}, bf16[384,2048]{1,0:T(8,128)(2,1)}, u32[]{:S(2)}) copy-start(bf16[384,2048]{1,0:T(8,128)(2,1)} %param.17) | copy-start | bytes 4718596
  140.2 60.4 %copy-start.4 = (bf16[384,2048]{1,0:T(8,128)(2,1)S(1)}, bf16[384,2048]{1,0:T(8,128)(2,1)}, u32[]{:S(2)}) copy-start(bf16[384,2048]{1,0:T(8,128)(2,1)} %refs_1_.5) | copy-start | bytes 4718596
  207.9 233.2 %reduce-scatter.7.cloned.1.call-start = ((), (), s32[]{:S(2)}) async-start(), calls=%async_computation.5 | async-start | bytes 7208960 | tf_op jit(solution)/shard_map/reduce_scatter | solution.py:105
  223.2 73.9 %copy-start.2 = (bf16[384,2048]{1,0:T(8,128)(2,1)S(1)}, bf16[384,2048]{1,0:T(8,128)(2,1)}, u32[]{:S(2)}) copy-start(bf16[384,2048]{1,0:T(8,128)(2,1)} %get-tuple-element.184.refs_0_.refs_1_) | copy-start | bytes 4718596
  223.2 73.9 %copy-start.13 = (bf16[384,1408]{1,0:T(8,128)(2,1)S(1)}, bf16[384,1408]{1,0:T(8,128)(2,1)}, u32[]{:S(2)}) copy-start(bf16[384,1408]{1,0:T(8,128)(2,1)} %copy-done.12) | copy-start | bytes 3244036
  304.3 16.3 %copy-start.83 = (f32[64]{0:T(128)S(1)}, f32[64]{0:T(128)}, u32[]{:S(2)}) copy-start(f32[64]{0:T(128)} %copy-done.82) | copy-start | bytes 772
  319.2 231.6 %reduce-scatter.9.cloned.1.call-start = ((), (), s32[]{:S(2)}) async-start(), calls=%async_computation.6 | async-start | bytes 7208960 | tf_op jit(solution)/shard_map/reduce_scatter | solution.py:105
  321.8 83.9 %copy-start.11 = (bf16[384,1408]{1,0:T(8,128)(2,1)S(1)}, bf16[384,1408]{1,0:T(8,128)(2,1)}, u32[]{:S(2)}) copy-start(bf16[384,1408]{1,0:T(8,128)(2,1)} %copy-done.10) | copy-start | bytes 3244036
  405.8 8.5 %copy-start.23 = (f32[384,64]{1,0:T(8,128)S(1)}, f32[384,64]{1,0:T(8,128)}, u32[]{:S(2)}) copy-start(f32[384,64]{1,0:T(8,128)} %copy-done.21) | copy-start | bytes 294916
  405.8 8.5 %copy-start.26 = (f32[384,64]{1,0:T(8,128)S(1)}, f32[384,64]{1,0:T(8,128)}, u32[]{:S(2)}) copy-start(f32[384,64]{1,0:T(8,128)} %get-tuple-element.202.new_ref.refs_6_) | copy-start | bytes 294916
  420.2 9.6 %copy-start.68 = (f32[384,64]{1,0:T(8,128)S(1)}, f32[384,64]{1,0:T(8,128)}, u32[]{:S(2)}) copy-start(f32[384,64]{1,0:T(8,128)} %copy-done.67) | copy-start | bytes 294916
  420.2 9.8 %copy-start.78 = (f32[1,16,64]{2,1,0:T(8,128)S(1)}, f32[1,16,64]{2,1,0:T(8,128)}, u32[]{:S(2)}) copy-start(f32[1,16,64]{2,1,0:T(8,128)} %param.25) | copy-start | bytes 12292
  420.2 10.2 %copy-start.20 = (f32[384,512]{1,0:T(8,128)S(1)}, f32[384,512]{1,0:T(8,128)}, u32[]{:S(2)}) copy-start(f32[384,512]{1,0:T(8,128)} %copy-done.19) | copy-start | bytes 2359300
  420.2 10.3 %copy-start.66 = (bf16[2048,16]{0,1:T(8,128)(2,1)S(1)}, bf16[2048,16]{0,1:T(8,128)(2,1)}, u32[]{:S(2)}) copy-start(bf16[2048,16]{0,1:T(8,128)(2,1)} %param.24) | copy-start | bytes 196612
  441.1 293.8 %reduce-scatter.11.cloned.1.call-start = ((), (), s32[]{:S(2)}) async-start(), calls=%async_computation.7 | async-start | bytes 13107200 | tf_op jit(solution)/shard_map/reduce_scatter | solution.py:105
  443.3 94.0 %copy-start.9 = (bf16[384,512]{1,0:T(8,128)(2,1)S(1)}, bf16[384,512]{1,0:T(8,128)(2,1)}, u32[]{:S(2)}) copy-start(bf16[384,512]{1,0:T(8,128)(2,1)} %copy-done.8) | copy-start | bytes 1179652
  443.3 94.0 %copy-start.15 = (f32[384,512]{1,0:T(8,128)S(1)}, f32[384,512]{1,0:T(8,128)}, u32[]{:S(2)}) copy-start(f32[384,512]{1,0:T(8,128)} %copy-done.14) | copy-start | bytes 2359300
  (65 other events, 163.7 us)
Sparse Core Ops, SparseCore 0:
  208.0 111.1 reduce-scatter.4
  322.0 118.9 reduce-scatter.6
  444.0 106.7 reduce-scatter.8
  553.0 181.9 reduce-scatter.10

commit v4 on v3

--- a/solution.py
+++ b/solution.py
@@ -1,4 +1,5 @@
 import functools
+import math
 
 import jax
 import jax.numpy as jnp
@@ -10,7 +11,10 @@
 CHUNK = 32
 CHUNKS = 4
 MESH = pl.DeviceIdType.MESH
-VMEM = 50 << 20
+VMEM = 24 << 20
+MORE = 10 << 20
+EXCHANGE_VMEM = 50 << 20
+FINAL_VMEM = 60 << 20
 READ_COST = 17 << 30
 
 
@@ -277,6 +281,8 @@
     piece, pieces, q_ref, k_ref, v_ref, log_ref, new_ref, doc_ref, prev_ref, score_ref, prob_ref, ks_ref, vs_ref, g_ref,
     dq_ref, dk_ref, dv_ref, held_ref, gained_ref, xk_ref, xv_ref, dkin_ref, dvin_ref, span_s,
 ):
+    if piece is None:
+        return
     size = span_s.shape[0]
     count = q_ref.shape[0] // size
     lower = triangle(size, False)
@@ -386,6 +392,14 @@
     lax.fori_loop(0, count, chunk, 0)
 
 
+def room(arrays):
+    total = 0
+    for a in arrays:
+        shape = a.shape[:-1] + (-(-a.shape[-1] // 128) * 128,)
+        total += math.prod(shape) * jnp.dtype(a.dtype).itemsize
+    return total + MORE
+
+
 def cost(flops, moved):
     return pl.CostEstimate(flops=flops, bytes_accessed=moved, transcendentals=0)
 
@@ -450,7 +464,7 @@
     return place + by * (1 - 2 * ((place // by) % 2))
 
 
-def exchange_kernel(names, count, heads, reverse, work, early, *refs):
+def exchange_kernel(names, count, heads, reverse, work, early, after, *refs):
     refs = dict(zip(names, refs))
     wides = [n for n in names if n.startswith("wide_in")]
     narrows = [n for n in names if n.startswith("narrow_in")]
@@ -462,16 +476,25 @@
     spans_of = [1 << k for k in range(count.bit_length() - 1)]
     hops = [1 << k for k in range(1, heads.bit_length() - 1)]
 
+    relays = [n for n in names if n.startswith("relay_out")]
+    relayed = bool(relays) or "ends_out" in refs
+    beside = {"seq": other_of(place, 2)}
+    at_end = (place // 2 == 0) | (place // 2 == 3)
+    in_middle = jnp.logical_not(at_end)
     greeted = []
+    if relayed:
+        greeted.append((beside, None))
     if wides or narrows or early is not None:
         greeted.append((partner, None))
-    if wides or "part" in refs:
+    if wides or relays or "part" in refs:
         greeted.append((sibling, None))
     if "part" in refs:
         greeted += [({"head": other_of(head, by)}, None) for by in hops]
     if "state" in refs:
         greeted += [({"seq": place + line * by}, left >= by) for by in spans_of]
         greeted += [({"seq": place - line * by}, ahead >= by) for by in spans_of]
+    if work is not None:
+        work(None, None, *[refs[n] for n in names if n.startswith("work")])
     barrier = pltpu.get_barrier_semaphore()
     total = 0
     for device, ok in greeted:
@@ -518,16 +541,6 @@
 
     waits, forwards, states = [], [], []
     fill = None
-    if early is not None:
-        source, target = refs["early_scratch0"], refs["narrow_out0"]
-
-        def send_tile(i, columns):
-            moved = copy(source.at[:, columns], target.at[:, columns], sems("narrow", i), partner)
-            moved.start()
-            waits.append(moved)
-
-        fill = early(send_tile, refs, [refs[n] for n in names if n.startswith("early")])
-    tiles_sent, waits = waits, []
     if "state" in refs:
         inside, received, before = refs["inside"], refs["received"], refs["before"]
         inside[0] = refs["state"][...]
@@ -540,6 +553,53 @@
         def _():
             states[0].start()
 
+    for i, name in enumerate(wides):
+        name, source = name.replace("in", "out"), refs[name]
+        moved = blocks_of(source, refs[name], i)
+        for one in moved:
+            one.start()
+        forwards.append((name, moved))
+    end_tiles, end_blocks = [], []
+    for i, name in enumerate(relays):
+        source, target = refs[f"relay_in{i}"], refs[name]
+        lines, _, wide = target.shape
+        for k in range(lines // 2):
+            at = (head % 2) * (lines // 2) + k
+            if len(source.shape) == 2:
+                start = pl.multiple_of((2 * at + place % 2) * wide, 128)
+                block = source.at[:, pl.ds(start, wide)]
+            else:
+                block = source.at[at]
+            end_blocks.append(
+                copy(block, target.at[at], sems("relay", i * (lines // 2) + k), beside)
+            )
+
+    @pl.when(at_end)
+    def _():
+        for moved in end_blocks:
+            moved.start()
+
+    if early is not None:
+        source, target = refs["early_b0"], refs["narrow_out0"]
+
+        def send_tile(i, columns):
+            moved = copy(source.at[:, columns], target.at[:, columns], sems("narrow", i), partner)
+            moved.start()
+            waits.append(moved)
+            if relayed:
+                onward = copy(
+                    refs["early_b1"].at[:, columns], refs["ends_out"].at[:, columns],
+                    sems("ends", i), beside,
+                )
+
+                @pl.when(at_end)
+                def _():
+                    onward.start()
+
+                end_tiles.append(onward)
+
+        fill = early(send_tile, refs, [refs[n] for n in names if n.startswith("early")])
+    tiles_sent, waits = waits, []
     if "part" in refs:
         part, added = refs["part"], refs["sum"]
         rows = part.shape[0] // CHUNKS
@@ -567,12 +627,6 @@
             waits.append(moved)
             if fill is not None:
                 cross(c)
-    for i, name in enumerate(wides):
-        name, source = name.replace("in", "out"), refs[name]
-        moved = blocks_of(source, refs[name], i)
-        for one in moved:
-            one.start()
-        forwards.append((name, moved))
     for i, name in enumerate(narrows):
         moved = copy(refs[name], refs[name.replace("in", "out")], sems("narrow", i), partner)
         moved.start()
@@ -624,6 +678,17 @@
             def _(moved=moved):
                 moved.wait_send()
 
+    def pass_on():
+        for i, (name, moved) in enumerate(forwards):
+            for one in moved:
+                one.wait()
+            onward = copy(half_of(refs[name]), half_of(refs[name]), sems("onward", i), sibling)
+            onward.start()
+            waits.append(onward)
+
+    early_pass = "part" in refs and "state" not in refs
+    if early_pass:
+        pass_on()
     if "part" in refs:
         for k in range(1, len(hops)):
             later = []
@@ -639,6 +704,13 @@
             across = later
         back = []
         k = len(hops) - 1
+
+        def close(c):
+            waits[c].wait_send()
+            back[c].wait()
+            if after is not None:
+                after(c, rows, added, [refs[n] for n in names if n.startswith("after")])
+
         for c in range(CHUNKS):
             across[c].wait()
             start = pl.multiple_of(c * rows + low * half, 8)
@@ -647,30 +719,49 @@
             moved = copy(added.at[mine], added.at[mine], sems("back", c), sibling)
             moved.start()
             back.append(moved)
-        for c in range(CHUNKS):
-            waits[c].wait_send()
-            back[c].wait()
+            if c:
+                close(c - 1)
+        close(CHUNKS - 1)
         waits = waits[CHUNKS:]
-    for i, (name, moved) in enumerate(forwards):
-        for one in moved:
-            one.wait()
-        onward = copy(half_of(refs[name]), half_of(refs[name]), sems("onward", i), sibling)
-        onward.start()
-        waits.append(onward)
+    if after is not None:
+        after(None, rows, added, [refs[n] for n in names if n.startswith("after")])
+    if not early_pass:
+        pass_on()
     for moved in waits + tiles_sent:
         moved.wait()
+    if relayed:
+
+        @pl.when(at_end)
+        def _():
+            for moved in end_tiles + end_blocks:
+                moved.wait_send()
+
+        @pl.when(in_middle)
+        def _():
+            for moved in end_tiles + end_blocks:
+                moved.wait_recv()
+            passed = [
+                copy(half_of(refs[name]), half_of(refs[name]), sems("passed", i), sibling)
+                for i, name in enumerate(relays)
+            ]
+            for moved in passed:
+                moved.start()
+            for moved in passed:
+                moved.wait()
+
     if early is not None:
         for one in refs["finish"][-1]:
             one.wait()
 
 
 def exchange(
-    number, part=None, state=None, reverse=False, wides=(), narrows=(), work=None, early=None
+    number, part=None, state=None, reverse=False, wides=(), narrows=(), work=None, early=None, relay=(), after=None
 ):
     count, heads = lax.axis_size("seq"), lax.axis_size("head")
     f32 = jnp.float32
     vmem, hbm = pl.BlockSpec(memory_space=pltpu.VMEM), pl.BlockSpec(memory_space=pl.ANY)
     ins, outs, scratch = [], [], []
+    buffers = ["part", "near", "own", "arrived", "inside", "received"]
     if part is not None:
         if early is None:
             ins.append(("part", part, vmem))
@@ -706,27 +797,48 @@
                     (name + end, pltpu.SemaphoreType.DMA((len(arrays) * size,)))
                     for end in ("_send", "_recv")
                 ]
+    for i, a in enumerate(relay):
+        ins.append((f"relay_in{i}", a, hbm))
+        shape = a.shape if len(a.shape) == 3 else (lines, a.shape[0], a.shape[1] // count)
+        outs.append((f"relay_out{i}", jax.ShapeDtypeStruct(shape, f32), hbm))
+    if relay:
+        for name, size in (("relay", len(relay) * shape[0] // 2), ("passed", len(relay))):
+            scratch += [(name + end, pltpu.SemaphoreType.DMA((size,))) for end in ("_send", "_recv")]
     if early is not None:
         early, given, sent_shape, tiles, made, extra = early
         ins += [(f"early_in{i}", a, hbm) for i, a in enumerate(given)]
         outs.append(("narrow_out0", jax.ShapeDtypeStruct(sent_shape, f32), hbm))
+        if lines == 4:
+            outs.append(("ends_out", jax.ShapeDtypeStruct(sent_shape, f32), hbm))
+            scratch += [("ends" + end, pltpu.SemaphoreType.DMA((tiles,))) for end in ("_send", "_recv")]
         outs += [(f"early_out{i}", a, hbm) for i, a in enumerate(made)]
-        scratch += [(f"early_scratch{i}", a) for i, a in enumerate(extra)]
+        scratch += [(f"early_b{i}", a) for i, a in enumerate(extra)]
+        buffers += [f"early_b{i}" for i in range(len(extra) - 3)]
         scratch += [("narrow" + end, pltpu.SemaphoreType.DMA((tiles,))) for end in ("_send", "_recv")]
+    if after is not None:
+        after, given, made, extra = after
+        ins += [(f"after_in{i}", a, vmem) for i, a in enumerate(given)]
+        outs += [(f"after_out{i}", a, hbm) for i, a in enumerate(made)]
+        scratch += [(f"after_b{i}", a) for i, a in enumerate(extra)]
+        buffers += [f"after_b{i}" for i in range(len(extra) - 1)]
     if work is not None:
         work, given, made, extra, places = work
+        beside = work is not back_query_kernel
         ins += [(f"work_in{i}", a, hbm if p else vmem) for i, (a, p) in enumerate(zip(given, places))]
         outs += [(f"work_out{i}", a, vmem) for i, a in enumerate(made)]
-        scratch += [(f"work_scratch{i}", a) for i, a in enumerate(extra)]
+        scratch += [(f"work_b{i}", a) for i, a in enumerate(extra)]
+        buffers += [f"work_b{i}" for i in range(len(extra) - beside)]
     names = [n for n, *_ in ins] + [n for n, *_ in outs] + [n for n, _ in scratch]
+    held = [a for _, a, spec in ins + outs if spec is vmem]
+    held += [jax.ShapeDtypeStruct(a.shape, a.dtype) for n, a in scratch if n in buffers]
     return pl.pallas_call(
-        functools.partial(exchange_kernel, names, count, heads, reverse, work, early),
+        functools.partial(exchange_kernel, names, count, heads, reverse, work, early, after),
         out_shape=tuple(jax.ShapeDtypeStruct(a.shape, a.dtype) for _, a, _ in outs),
         in_specs=[spec for *_, spec in ins],
         out_specs=tuple(spec for *_, spec in outs),
         scratch_shapes=[s for _, s in scratch],
         compiler_params=pltpu.CompilerParams(
-            collective_id=number, has_side_effects=True, vmem_limit_bytes=VMEM
+            collective_id=number, has_side_effects=True, vmem_limit_bytes=EXCHANGE_VMEM
         ),
         cost_estimate=cost(40 << 30, 16 << 20),
     )(*[a for _, a, _ in ins])
@@ -781,25 +893,357 @@
     return jnp.concatenate([keep, jnp.full_like(keep, doc), keys, values], axis=1)
 
 
-def matmul_work(product, column, piece, pieces, left_ref, right_ref, out_ref, left, right, sems):
-    copies = [
-        pltpu.make_async_copy(left_ref, left, sems.at[0]),
-        pltpu.make_async_copy(right_ref, right, sems.at[1]),
+def final_kernel(tiles, head_count, *refs):
+    act_in, near_in, dy_own, dy_their, dy_near, dy_far, in_own, in_their, branch_own, branch_their = refs[:10]
+    sides = refs[10 : 10 + 2 * head_count]
+    part, outs = refs[10 + 2 * head_count], refs[11 + 2 * head_count : 11 + 3 * head_count]
+    (out_down, added, far, across, wide_in, wide_branch, heads, stage, stage_head,
+     act, their_act, near_act, far_act, wide_dy, head_tile, to_middle, from_middle, near, own_sum, arrived,
+     own_sems, head_sems, stage_sems, act_sems, *sems) = refs[11 + 3 * head_count :]
+    place = lax.axis_index("seq")
+    line = place // 2
+    at_end = (line == 0) | (line == 3)
+    in_middle = jnp.logical_not(at_end)
+    partner, beside = {"seq": other_of(place, 1)}, {"seq": other_of(place, 2)}
+    opposite = {"seq": place + jnp.where(line == 1, 2, -2)}
+    rows = act.shape[0]
+    wide = out_down.shape[0]
+    head = heads.shape[1] // head_count
+    columns = [pl.ds(i * 256, 256) for i in range(heads.shape[1] // 256)]
+    down = [pl.ds(*tile) for tile in tiles]
+    out = [outs[i // 2].at[:, pl.ds(i % 2 * 256, 256)] for i in range(len(columns))]
+
+    number = lax.axis_index("head")
+    sibling, over_y = {"head": other_of(number, 1)}, {"head": other_of(number, 2)}
+    barrier = pltpu.get_barrier_semaphore()
+    for device in (beside, partner, sibling, over_y):
+        pl.semaphore_signal(barrier, inc=1, device_id=device, device_id_type=MESH)
+
+    @pl.when(in_middle)
+    def _():
+        pl.semaphore_signal(barrier, inc=1, device_id=opposite, device_id_type=MESH)
+
+    roles = [jnp.where(line < 2, a, b) for a, b in ((2, 1), (3, 0), (1, 2), (0, 3))]
+    starts = [pl.multiple_of((2 * role + place % 2) * wide, 128) for role in roles]
+
+    def load(source, target, sem):
+        copied = pltpu.make_async_copy(source, target, sem)
+        copied.start()
+        return copied
+
+    in_loads, branch_loads, dy_loads = (
+        [
+            load(
+                source.at[:, pl.ds(start, wide)],
+                target.at[pl.ds(0, rows), pl.ds(r * wide, wide)],
+                own_sems.at[k, r],
+            )
+            for r, start in enumerate(starts)
+        ]
+        for k, (source, target) in enumerate(
+            ((in_own, wide_in), (branch_own, wide_branch), (dy_own, wide_dy))
+        )
+    )
+    head_loads = [
+        load(sides[2 * i], heads.at[pl.ds(0, rows), pl.ds(i * head, head)], head_sems.at[0, i])
+        for i in range(head_count)
     ]
+    ready = (0, head_count - 1)
+    head_loads += [load(sides[2 * i + 1], stage_head.at[i], head_sems.at[1, i]) for i in ready]
+    act_loads = [
+        load(act_in, act, act_sems.at[0]),
+        load(near_in, near_act, act_sems.at[1]),
+    ]
+    jobs = [(in_their, wide_in, 1), (branch_their, wide_branch, 1)]
+    jobs += [(dy_their, wide_dy, 1), (dy_near, wide_dy, 2), (dy_far, wide_dy, 3)]
+
+    def staged(k):
+        return [
+            load(jobs[k][0].at[role], stage.at[k % 2, r], stage_sems.at[k % 2, r])
+            for r, role in enumerate(roles)
+        ]
+
+    under_way = {0: staged(0), 1: staged(1)}
+
+    def settle(k):
+        for one in under_way[k]:
+            one.wait()
+        _, target, group = jobs[k]
+        for r in range(4):
+            target[group * rows : (group + 1) * rows, r * wide : (r + 1) * wide] = stage[
+                k % 2, r
+            ].astype(jnp.bfloat16)
+
+    pl.semaphore_wait(barrier, 4 + in_middle.astype(jnp.int32))
+
+    def remote(source, target, kind, i, device):
+        return pltpu.make_async_remote_copy(
+            src_ref=source, dst_ref=target, send_sem=sems[2 * kind].at[i],
+            recv_sem=sems[2 * kind + 1].at[i], device_id=device, device_id_type=MESH,
+        )
+
+    chunk = part.shape[0] // CHUNKS
+    half = chunk // 2
+    low = number % 2
+    mine_of = [pl.ds(pl.multiple_of(c * chunk + low * half, 8), half) for c in range(CHUNKS)]
+    other_half = [pl.ds(pl.multiple_of(c * chunk + (1 - low) * half, 8), half) for c in range(CHUNKS)]
+    nears = [remote(part.at[h], near.at[c], 8, c, sibling) for c, h in enumerate(other_half)]
+    sums = [remote(own_sum.at[c], arrived.at[c], 9, c, over_y) for c in range(CHUNKS)]
+    backs = [remote(added.at[h], added.at[h], 10, c, sibling) for c, h in enumerate(mine_of)]
+    head_trades = [
+        remote(sides[2 * i + 1], stage_head.at[i], 7, i - 1, partner)
+        for i in range(1, head_count - 1)
+    ]
+    for one in nears:
+        one.start()
+    for one in in_loads + head_loads:
+        one.wait()
+    settle(0)
+    settle(1)
+
+    second = pl.ds(wide, wide)
+    to_side = [remote(far.at[:, c], far.at[:, c], 0, i, beside) for i, c in enumerate(columns)]
+    over = [
+        remote(far.at[pl.ds(0, 2 * wide), c], across.at[:, c], 1, i, opposite) for i, c in enumerate(columns)
+    ]
+    home = [remote(across.at[second, c], out[i], 2, i, beside) for i, c in enumerate(columns)]
+    trades = [remote(act_in.at[:, c], their_act.at[:, c], 3, i, partner) for i, c in enumerate(down)]
+    passes = [remote(near_in.at[:, c], far_act.at[:, c], 4, i, partner) for i, c in enumerate(down)]
+    over_down = [
+        remote(to_middle.at[:, c], from_middle.at[:, c], 5, i, opposite) for i, c in enumerate(down)
+    ]
+    home_down = [
+        remote(from_middle.at[second, c], out_down.at[:, c], 6, i, beside) for i, c in enumerate(down)
+    ]
+
+    @pl.when(at_end)
+    def _():
+        for one in head_trades:
+            one.start()
+
+    @pl.when(in_middle)
+    def _():
+        under_way[2], under_way[3] = staged(2), staged(3)
+        settle(2)
+        under_way[4] = staged(4)
+        settle(3)
+        settle(4)
+        for i, (trade, onward) in enumerate(zip(trades, passes)):
+            trade.start()
+            onward.start()
+            if i < len(head_trades):
+                head_trades[i].start()
+
+    for c in range(CHUNKS):
+        nears[c].wait_recv()
+        own_sum[c] = part[mine_of[c], :] + near[c]
+        sums[c].start()
+
+    def receive(i):
+        if 0 < i < head_count - 1:
+            head_trades[i - 1].wait_recv()
+        heads[rows:, i * head : (i + 1) * head] = stage_head[i].astype(jnp.bfloat16)
+
+    for i in ready:
+        receive(i)
+
+    down_at = {min(2 * j, len(columns) - len(down) + j): j for j in range(len(down))}
+    order = [0, 1, 2 * head_count - 2, 2 * head_count - 1, *range(2, 2 * head_count - 2)]
+
+    def wide_of(i):
+        return wide_branch if i >= 2 * (head_count - 1) else wide_in
+
+    def settle_down():
+        for one in dy_loads + act_loads:
+            one.wait()
+
+    for one in branch_loads:
+        one.wait()
+
+    @pl.when(at_end)
+    def _():
+        for k, i in enumerate(order):
+            if k > 3 and i % 2 == 0:
+                receive(i // 2)
+            far[:, columns[i]] = tn(wide_of(i)[:, : 3 * wide], heads[:, columns[i]])
+            to_side[i].start()
+        settle_down()
+
+    @pl.when(at_end)
+    def _():
+        for k, i in enumerate(order):
+            c = columns[i]
+            mine = tn(wide_of(i)[:, 3 * wide :], heads[:, c])
+            home[i].wait_recv()
+            out[i][...] = out[i][...] + mine
+            if k in down_at:
+                home_down[down_at[k]].wait_recv()
+        for one in to_side:
+            one.wait_send()
+
+    @pl.when(in_middle)
+    def _():
+        def finish(i):
+            c = columns[i]
+            mine = tn(wide_of(i)[:, 3 * wide :], heads[:, c])
+            over[i].wait_recv()
+            across[wide:, c] = across[wide:, c] + mine
+            home[i].start()
+            out[i][...] = far[2 * wide :, c] + across[:wide, c]
+
+        settle_down()
+        for k, i in enumerate(order):
+            c = columns[i]
+            if k > 3 and i % 2 == 0:
+                receive(i // 2)
+            j = down_at.get(k)
+            if j is not None:
+                d = down[j]
+                size = tiles[j][1]
+                tile = head_tile.at[:, pl.ds(0, size)]
+                trades[j].wait_recv()
+                passes[j].wait_recv()
+                for g, side in enumerate((act, their_act, near_act, far_act)):
+                    tile[g * rows : (g + 1) * rows, :] = side[:, d].astype(jnp.bfloat16)
+                to_middle[:, d] = tn(wide_dy[:, : 2 * wide], tile[...])
+                over_down[j].start()
+                out_down[:, d] = tn(wide_dy[:, 2 * wide : 3 * wide], tile[...])
+                home_part = tn(wide_dy[:, 3 * wide :], tile[...])
+            mine = tn(wide_of(i)[:, : 3 * wide], heads[:, c])
+            to_side[i].wait_recv()
+            far[:, c] = far[:, c] + mine
+            over[i].start()
+            if j is not None:
+                over_down[j].wait_recv()
+                from_middle[wide:, d] = from_middle[wide:, d] + home_part
+                home_down[j].start()
+                out_down[:, d] = out_down[:, d] + from_middle[:wide, d]
+            if k:
+                finish(order[k - 1])
+        finish(order[-1])
+        for one in over + home + trades + passes + over_down + home_down:
+            one.wait_send()
+
+    for c in range(CHUNKS):
+        sums[c].wait()
+        added[mine_of[c], :] = own_sum[c] + arrived[c]
+        backs[c].start()
+    for one in head_trades + nears:
+        one.wait_send()
+    for one in backs:
+        one.wait()
+
+
+def final_gradients(number, part, act, near_act, dy, wide_in, wide_branch, heads):
+    rows, hidden = act.shape
+    wide = dy[1].shape[2]
+    head = heads[0][0].shape[1]
+    count = len(heads)
+    total = head * count
+    tiles = column_tiles(hidden)
+    f32, bf16 = jnp.float32, jnp.bfloat16
+    dma = pltpu.SemaphoreType.DMA
+    hbm, vmem = pl.BlockSpec(memory_space=pl.ANY), pl.BlockSpec(memory_space=pltpu.VMEM)
+    whole = pltpu.VMEM((rows, hidden), f32)
+    sides = [a for pair in heads for a in pair]
+    half = (CHUNKS, rows // CHUNKS // 2, part.shape[1])
+    return pl.pallas_call(
+        functools.partial(final_kernel, tiles, count),
+        out_shape=(
+            *[jax.ShapeDtypeStruct((wide, head), f32)] * count,
+            jax.ShapeDtypeStruct((wide, hidden), f32),
+            jax.ShapeDtypeStruct(part.shape, f32),
+        ),
+        in_specs=[hbm] * (10 + len(sides)) + [vmem],
+        out_specs=(vmem,) * (count + 2),
+        scratch_shapes=[
+            pltpu.VMEM((3 * wide, total), f32),
+            pltpu.VMEM((2 * wide, total), f32),
+            pltpu.VMEM((2 * rows, 4 * wide), bf16),
+            pltpu.VMEM((2 * rows, 4 * wide), bf16),
+            pltpu.VMEM((2 * rows, total), bf16),
+            pltpu.VMEM((2, 4, rows, wide), f32),
+            pltpu.VMEM((count, rows, head), f32),
+            whole, whole, whole, whole,
+            pltpu.VMEM((4 * rows, 4 * wide), bf16),
+            pltpu.VMEM((4 * rows, 256), bf16),
+            pltpu.VMEM((2 * wide, hidden), f32),
+            pltpu.VMEM((2 * wide, hidden), f32),
+            pltpu.VMEM(half, f32), pltpu.VMEM(half, f32), pltpu.VMEM(half, f32),
+            dma((3, 4)), dma((2, count)), dma((2, 4)), dma((2,)),
+        ]
+        + [dma((total // 256,))] * 6
+        + [dma((len(tiles),))] * 8
+        + [dma((count - 2,))] * 2
+        + [dma((CHUNKS,))] * 6,
+        compiler_params=pltpu.CompilerParams(
+            collective_id=number, has_side_effects=True, vmem_limit_bytes=FINAL_VMEM
+        ),
+        cost_estimate=cost(200 << 30, 16 << 20),
+    )(act, near_act, *dy, *wide_in, *wide_branch, *sides, part)
+
+
+def normed_after(c, rows, added, own):
+    stream, gain, normed_out, float_out, normed, normed_f, sems = own
+
+    def copies(c):
+        mine = pl.ds(c * rows, rows)
+        return [
+            pltpu.make_async_copy(normed.at[mine], normed_out.at[mine], sems.at[0, c]),
+            pltpu.make_async_copy(normed_f.at[mine], float_out.at[mine], sems.at[1, c]),
+        ]
+
+    if c is None:
+        for i in range(CHUNKS):
+            for one in copies(i):
+                one.wait()
+        return
+    mine = pl.ds(c * rows, rows)
+    hidden = stream[mine, :].astype(jnp.float32) + added[mine, :]
+    added[mine, :] = hidden
+    rounded = (hidden * rms_scale(hidden) * gain[...]).astype(jnp.bfloat16)
+    normed[mine, :] = rounded
+    normed_f[mine, :] = rounded.astype(jnp.float32)
+    for one in copies(c):
+        one.start()
+
+
+def norm_after(stream, gain):
+    half, full = (jax.ShapeDtypeStruct(stream.shape, t) for t in (jnp.bfloat16, jnp.float32))
+    return (
+        normed_after,
+        (stream, gain.reshape(1, -1)),
+        (half, full),
+        (
+            pltpu.VMEM(stream.shape, jnp.bfloat16),
+            pltpu.VMEM(stream.shape, jnp.float32),
+            pltpu.SemaphoreType.DMA((2, CHUNKS)),
+        ),
+    )
+
+
+def matmul_work(product, column, count, piece, pieces, left_ref, *refs):
+    rights, outs, left = refs[:count], refs[count : 2 * count], refs[2 * count]
+    sides, sems = refs[2 * count + 1 : -1], refs[-1]
+    copies = [pltpu.make_async_copy(left_ref, left, sems.at[0])]
+    copies += [pltpu.make_async_copy(a, b, sems.at[1 + i]) for i, (a, b) in enumerate(zip(rights, sides))]
+    if piece is None:
+        for one in copies:
+            one.start()
+        return
     if piece == 0:
         for one in copies:
-            one.start()
-        for one in copies:
             one.wait()
-
-    def tile(i, carry):
-        columns = pl.ds(pl.multiple_of(i * column, column), column)
-        side = right[columns, :] if product is nt else right[:, columns]
-        out_ref[:, columns] = product(left[...], side)
-        return carry
-
-    tiles = out_ref.shape[1] // column
-    lax.fori_loop(tiles * piece // pieces, tiles * (piece + 1) // pieces, tile, 0)
+    for right, out in zip(sides, outs):
+
+        def tile(i, carry):
+            columns = pl.ds(pl.multiple_of(i * column, column), column)
+            side = right[columns, :] if product is nt else right[:, columns]
+            out[:, columns] = product(left[...], side)
+            return carry
+
+        tiles = out.shape[1] // column
+        lax.fori_loop(tiles * piece // pieces, tiles * (piece + 1) // pieces, tile, 0)
 
 
 def column_tiles(size):
@@ -808,8 +1252,8 @@
 
 
 def hidden_units(send_tile, refs, own):
-    (normed_in, gate_in, up_in, down_in, d_act_in, act_out, d_gate_out, d_up_out, gate_f_out, up_f_out, ffn_out,
-     act_f, act_ref, d_gate_ref, d_up_ref, gate_f_ref, up_f_ref, ffn_ref, normed, w_gate, w_up, w_down, d_act, sems, tile_sems, out_sems) = own
+    (normed_in, gate_in, up_in, down_in, d_act_in, act_f_out, d_gate_out, d_up_out, up_f_out, ffn_out,
+     gate_f, act_f, act_ref, d_gate_ref, d_up_ref, up_f_ref, ffn_ref, normed, w_gate, w_up, w_down, d_act, sems, tile_sems, out_sems) = own
     whole = [
         pltpu.make_async_copy(normed_in, normed, sems.at[0]),
         pltpu.make_async_copy(d_act_in, d_act, sems.at[1]),
@@ -848,16 +1292,16 @@
         act = (silu * up).astype(jnp.bfloat16)
         act_ref[:, columns] = act
         act_f[:, columns] = act.astype(jnp.float32)
-        send_tile(i, columns)
         d_gate = (pull * up * sig * (1.0 + gate * (1.0 - sig))).astype(jnp.bfloat16)
         d_up = (pull * silu).astype(jnp.bfloat16)
         d_gate_ref[:, columns] = d_gate
         d_up_ref[:, columns] = d_up
-        gate_f_ref[:, columns] = d_gate.astype(jnp.float32)
+        gate_f[:, columns] = d_gate.astype(jnp.float32)
+        send_tile(i, columns)
         up_f_ref[:, columns] = d_up.astype(jnp.float32)
 
-    kept = [(act_ref, act_out), (d_gate_ref, d_gate_out), (d_up_ref, d_up_out),
-            (gate_f_ref, gate_f_out), (up_f_ref, up_f_out), (ffn_ref, ffn_out)]
+    kept = [(act_f, act_f_out), (d_gate_ref, d_gate_out), (d_up_ref, d_up_out),
+            (up_f_ref, up_f_out), (ffn_ref, ffn_out)]
     kept = [pltpu.make_async_copy(a, b, out_sems.at[i]) for i, (a, b) in enumerate(kept)]
     for one in kept[:-1]:
         one.start()
@@ -903,13 +1347,13 @@
         (normed_mid, w_gate, w_up, w_down, d_act),
         (rows, hidden),
         tiles,
-        (half, half, half, full, full, jax.ShapeDtypeStruct((rows, width), jnp.float32)),
+        (full, half, half, full, jax.ShapeDtypeStruct((rows, width), jnp.float32)),
         (
+            pltpu.VMEM((rows, hidden), jnp.float32),
             pltpu.VMEM((rows, hidden), jnp.float32),
             pltpu.VMEM((rows, hidden), jnp.bfloat16),
             pltpu.VMEM((rows, hidden), jnp.bfloat16),
             pltpu.VMEM((rows, hidden), jnp.bfloat16),
-            pltpu.VMEM((rows, hidden), jnp.float32),
             pltpu.VMEM((rows, hidden), jnp.float32),
             pltpu.VMEM((rows, width), jnp.float32),
             pltpu.VMEM(normed_mid.shape, jnp.bfloat16),
@@ -919,24 +1363,24 @@
             pltpu.VMEM(d_act.shape, jnp.float32),
             pltpu.SemaphoreType.DMA((3,)),
             pltpu.SemaphoreType.DMA((2, tiles)),
-            pltpu.SemaphoreType.DMA((6,)),
+            pltpu.SemaphoreType.DMA((5,)),
         ),
     )
 
 
-def matmul_beside(product, left, right):
-    columns = right.shape[0] if product is nt else right.shape[1]
+def matmul_beside(product, left, *rights):
+    columns = rights[0].shape[0] if product is nt else rights[0].shape[1]
     column = 256 if columns % 256 == 0 else 128
     return (
-        functools.partial(matmul_work, product, column),
-        (left, right),
-        (jax.ShapeDtypeStruct((left.shape[0], columns), jnp.float32),),
+        functools.partial(matmul_work, product, column, len(rights)),
+        (left, *rights),
+        (jax.ShapeDtypeStruct((left.shape[0], columns), jnp.float32),) * len(rights),
         (
             pltpu.VMEM(left.shape, left.dtype),
-            pltpu.VMEM(right.shape, right.dtype),
-            pltpu.SemaphoreType.DMA((2,)),
+            *[pltpu.VMEM(right.shape, right.dtype) for right in rights],
+            pltpu.SemaphoreType.DMA((1 + len(rights),)),
         ),
-        (True, True),
+        (True,) * (1 + len(rights)),
     )
 
 
@@ -966,10 +1410,8 @@
     stream_f = stream.astype(jnp.float32)
     scale_in = rms_scale(stream_f)
     normed_in = (stream_f * scale_in * attn_gain).astype(jnp.bfloat16)
-    query_rows = plain_dot(normed_in, w_query).astype(jnp.bfloat16)
     key_rows = plain_dot(normed_in, w_key).astype(jnp.bfloat16)
     value_rows = plain_dot(normed_in, w_value).astype(jnp.bfloat16)
-    gate_act = plain_dot(normed_in, w_outgate)
     ranked = plain_dot(normed_in, w_low)
 
     def decay_logs(ranked_in, slot_map, bias_row):
@@ -990,7 +1432,13 @@
     local_value = precise_left_t(factor, value_rows.astype(jnp.float32))
     docs = seg_ids.astype(jnp.float32)
     own_state = state_of(jnp.exp(total), docs[tok_rows - 1], local_key, local_value)
-    prefix, d_act = exchange(0, state=own_state, work=matmul_beside(nt, cotangent, w_down))
+    dy_f = cotangent.astype(jnp.float32)
+    prefix, query_rows, gate_act = exchange(
+        0,
+        state=own_state,
+        work=matmul_beside(nn, normed_in, w_query, w_outgate),
+    )
+    query_rows = query_rows.astype(jnp.bfloat16)
     key_in, value_in = prefix[:, 128 : 128 + head_width], prefix[:, 128 + head_width :]
     prior = prefix[0, 64]
     decay_all = jnp.where(docs[tok_rows - 1] == prior, jnp.exp(total), 0.0)
@@ -1005,25 +1453,34 @@
     gate_sig = jax.nn.sigmoid(gate_act)
     gate_silu = gate_act * gate_sig
     mixed_heads = (normed_read * gate_silu).astype(jnp.bfloat16)
-    branch, from_dy, from_in = exchange(
+    four = lax.axis_size("seq") == 8
+    hidden, from_dy, *near_dy, normed_mid, normed_mid_f, d_act = exchange(
         1,
         part=plain_dot(mixed_heads, w_out),
-        wides=(wide_to_send(cotangent), wide_to_send(normed_in)),
+        wides=(wide_to_send(cotangent),),
+        relay=(dy_f,) if four else (),
+        work=matmul_beside(nt, cotangent, w_down),
+        after=norm_after(stream, mlp_gain),
     )
     wide_dy = cotangent, from_dy
-    wide_in = normed_in, from_in
-    hidden = stream_f + branch
     scale_mid = rms_scale(hidden)
-    normed_mid = (hidden * scale_mid * mlp_gain).astype(jnp.bfloat16)
     upstream = cotangent.astype(jnp.float32)
-    d_mid, from_act, ffn_act, d_gate, d_up, d_gate_f, d_up_f, ffn_part = exchange(
+    d_mid, from_mid, *made = exchange(
         2,
         part=jax.ShapeDtypeStruct((tok_rows, width), jnp.float32),
+        wides=(wide_to_send(normed_mid_f),),
+        relay=(from_dy,) if four else (),
         early=hidden_units_early(normed_mid, w_gate, w_up, w_down, d_act),
     )
-    grad_down = pair_products((wide_dy, [(ffn_act, from_act)]))
-    d_mid, grad_down = together(d_mid, grad_down)
-    grad_down = line_sum(grad_down)
+    if four:
+        far_dy, from_gate, end_act, *made = made
+    else:
+        from_gate, *made = made
+    act_f, d_gate, d_up, d_up_f, ffn_part = made
+    wide_mid = normed_mid, from_mid
+    grad_gate = pair_products((wide_mid, [(d_gate, from_gate)]))
+    d_mid, grad_gate = together(d_mid, grad_gate)
+    grad_gate = line_sum(grad_gate)
     grad_mlp_gain = jnp.sum(d_mid * hidden * scale_mid, axis=0)
     scaled_mid = d_mid * mlp_gain
     d_hidden = (
@@ -1042,32 +1499,37 @@
     d_read = scale_read * scaled_read - slot_read * scale_read**3 * jnp.mean(
         scaled_read * slot_read, axis=1, keepdims=True
     )
-    from_mid, from_gate, *back = exchange(
+    normed_f, ffn_part = together(wide_to_send(normed_in), ffn_part)
+    ffn_out, from_in, from_up, *back = exchange(
         3,
-        wides=(wide_to_send(normed_mid),),
-        narrows=(d_gate_f,),
+        part=ffn_part,
+        wides=(normed_f,),
+        narrows=(d_up_f,),
         work=back_query(
             query_rows, key_rows, value_rows, log_decay, new, docs, before, scores, probs, key_states, value_states, d_read
         ),
     )
-    wide_mid = normed_mid, from_mid
-    grad_gate = pair_products((wide_mid, [(d_gate, from_gate)]))
+    wide_in = normed_in, from_in
+    grad_up = pair_products((wide_mid, [(d_up, from_up)]))
     d_query, d_key, d_value, held, gained, to_keys, to_values, key_back, value_back = back
     query_back = d_query.astype(jnp.bfloat16)
-    key_back, grad_gate = together(key_back, grad_gate)
-    grad_gate, grad_down = together(grad_gate, grad_down)
-    grad_gate = line_sum(grad_gate)
-    ffn_out, suffix, from_up, from_outgate = exchange(
+    result = hidden + ffn_out
+    squares = jnp.stack(
+        [jnp.sum(stream_f * stream_f), jnp.sum(hidden * hidden), jnp.sum(result * result)]
+    )
+    key_back, grad_up, grad_gate, grad_mlp_gain, grad_head_gain, squares = together(
+        key_back, grad_up, grad_gate, grad_mlp_gain, grad_head_gain, squares
+    )
+    grad_up = line_sum(grad_up)
+    suffix, from_branch, from_outgate, from_mixed = exchange(
         4,
-        part=ffn_part,
         state=state_of(decay_all, 0.0, key_back, value_back),
         reverse=True,
-        narrows=(d_up_f, wide_float(d_gate_act)),
-    )
-    grad_up = pair_products((wide_mid, [(d_up, from_up)]))
+        wides=(wide_to_send(d_branch),),
+        narrows=(wide_float(d_gate_act), wide_float(mixed_heads)),
+    )
     key_end, value_end = suffix[:, 128 : 128 + head_width], suffix[:, 128 + head_width :]
     end_total = jnp.sum(key_states[-1] * key_end + value_states[-1] * value_end, axis=1)[None, :]
-    d_key, grad_up = together(d_key, grad_up)
     key_back, value_back, d_logs = back_key(
         key_rows, value_rows, log_decay, new, docs, before, d_key, d_value, held, gained,
         to_keys, to_values, key_end, value_end, end_total,
@@ -1082,33 +1544,24 @@
         + dot_right_t(d_gate_act, w_outgate)
         + precise_right_t(d_ranked, w_low.astype(jnp.float32))
     )
-    grad_up, grad_gate, d_in_part = together(grad_up, grad_gate, d_in_part)
-    grad_up = line_sum(grad_up)
-    d_in, from_branch, *from_mixer = exchange(
-        5,
-        part=d_in_part,
-        wides=(wide_to_send(d_branch),),
-        narrows=[wide_float(a) for a in (query_back, key_back, value_back, mixed_heads)],
-    )
-    grad_rest = pair_products(
-        (
-            wide_in,
-            [
-                (d_gate_act, from_outgate),
-                (query_back, from_mixer[0]),
-                (key_back, from_mixer[1]),
-                (value_back, from_mixer[2]),
-            ],
-        ),
-        ((d_branch, from_branch), [(mixed_heads, from_mixer[3])]),
-    )
-    grad_rest, grad_up, d_in = together(grad_rest, grad_up, d_in)
-    grad_rest = line_sum(grad_rest)
-    grad_outgate, grad_query, grad_key, grad_value, grad_out = jnp.split(grad_rest, 5, axis=1)
-    result = hidden + ffn_out
-    squares = jnp.stack(
-        [jnp.sum(stream_f * stream_f), jnp.sum(hidden * hidden), jnp.sum(result * result)]
-    )
+    late = [wide_float(a) for a in (query_back, key_back, value_back)]
+    wide_branch = d_branch, from_branch
+    if four:
+        sides = [(d_gate_act, from_outgate), *zip((query_back, key_back, value_back), late), (mixed_heads, from_mixed)]
+        act_f, grad_up = together(act_f, grad_up)
+        *grad_rest, grad_down, d_in = final_gradients(
+            5, d_in_part, act_f, end_act, (cotangent, from_dy, *near_dy, far_dy), wide_in, wide_branch, sides
+        )
+    else:
+        d_in, *late = exchange(5, part=d_in_part, narrows=late)
+        head_sides = [(d_gate_act, from_outgate), *zip((query_back, key_back, value_back), late), (mixed_heads, from_mixed)]
+        grad_rest = pair_products((wide_in, head_sides[:4]), (wide_branch, head_sides[4:]))
+        grad_rest = line_sum(grad_rest)
+        (from_act,) = exchange(6, narrows=(act_f,))
+        grad_down = pair_products((wide_dy, [(act_f.astype(jnp.bfloat16), from_act)]))
+        grad_down = line_sum(grad_down)
+        grad_rest = jnp.split(grad_rest, 5, axis=1)
+    grad_outgate, grad_query, grad_key, grad_value, grad_out = grad_rest
     grad_attn_gain = jnp.sum(d_in * stream_f * scale_in, axis=0)
     scaled_in = d_in * attn_gain
     grad_stream = (
@@ -1129,7 +1582,7 @@
     sizes = [a.shape[1] for a in small]
     packed = jnp.concatenate(small, axis=1)
     packed = jnp.pad(packed, ((0, 0), (0, -packed.shape[1] % 1024)))
-    packed = scatter_sum(6, packed.reshape(count, -1, 128)).reshape(-1)
+    packed = scatter_sum(7, packed.reshape(count, -1, 128)).reshape(-1)
     ends = [sum(sizes[: i + 1]) for i in range(len(sizes))]
     small = [packed[end - size : end] for end, size in zip(ends, sizes)]
     stream_rms = jnp.sqrt(small[6] / (tok_rows * count * width))

time: 753 us -> 718 us (0.954)
  waiting for transfers between devices: 163 us -> 10.9 us
  Pallas kernels: 445 us -> 561 us
    pallas_call x0 -> x1, Pallas kernels: none -> 223 us  [final_gradients(): pl.pallas_call(functools.partial(final_kernel, tiles, count), out_shape=(...]
    reduce_scatter x4 -> x2, waiting for transfers between devices: 163 us -> 10.9 us  [line_sum(): lax.psum_scatter(product, 'seq', scatter_dimension=0, axis_index_groups=g...]
    pallas_call x6 -> x5, Pallas kernels: 376 us -> 300 us  [exchange(): pl.pallas_call(functools.partial(exchange_kernel, names, count, heads, re...]
    pallas_call x4 -> x2, Pallas kernels: 33.9 us -> 7.57 us  [pair_products(): pl.pallas_call(functools.partial(product_kernel, [len(narrows) for _, nar...]
    convert_element_type x4 -> x3, other arithmetic: 17.3 us -> 11 us  [wide_to_send(): array = array.astype(jnp.float32)]
    unnamed x176 -> x218, local copies, waits for them, and re-layouts: 31.2 us -> 35.7 us
  transfers between devices with their start and end apart: 4 -> 2, of which waited for: 4 -> 2; matrix products, arithmetic and copies ran while one was open for 7% -> 6% of each run, Pallas kernels for 40% -> 23%
where the time goes in v4:
time: 718 us; the launch traced here: 712 us
  Pallas kernels  561 us (78%)
  local copies, waits for them, and re-layouts  48.5 us (7%)
  other arithmetic  46.8 us (7%)
  matrix products  27.3 us (4%)
  between operations  17 us (2%)
  waiting for transfers between devices  10.9 us (2%)
    pallas_call x5, Pallas kernels, exchange(): pl.pallas_call(functools.partial(exchange_kernel, names, count, heads, re...  300 us
    pallas_call x1, Pallas kernels, final_gradients(): pl.pallas_call(functools.partial(final_kernel, tiles, count), out_shape=(...  223 us
    unnamed x218, local copies, waits for them, and re-layouts  35.7 us
  transfers between devices with their start and end apart: 2, of which 2 were waited for; matrix products, arithmetic and copies ran while one was open for 6% of the time, Pallas kernels for 23%

profile of v4, /device:TPU:0, one launch (start us, length us, event | category | flops | bytes accessed | tf_op | source)
XLA Modules:
  0.0 711.9 jit_solution(11444572525112735194)
XLA Ops:
  10.0 2.9 fusion
  13.5 3.5 fusion.41
  22.0 3.3 convolution_convert_fusion.v_ref.refs_5_
  29.7 22.6 %shard_map.296 = (f32[64,1152]{1,0:T(8,128)S(1)}, f32[384,512]{1,0:T(8,128)S(1)}, f32[384,512]{1,0:T(8,128)S(1)}) custom-call(f32[64,1152]{1,0:T(8,128)S(1)} %concatenate.12.refs_0_, bf16[384,2048]{1,0:T(8,128)(2,1)S(1)} %copy-done.6, bf16[2048,512]{1,0:T(8,128)(2,1)} %refs_2_.2, bf16[2048,512]{1,0:T(8,128)(2,1)} %refs_3_.3), custom_call_target="tpu_custom_call" | custom-call | flops 42949672960 | bytes 16777216 | tf_op jit(solution)/shard_map/pallas_call | solution.py:834
  54.5 3.5 convert_element_type.75.refs_1_.refs_2_
  64.9 11.2 %shard_map.297 = (f32[384,512]{1,0:T(8,128)S(1)}, f32[384,64]{1,0:T(8,128)S(1)}, f32[384,64]{1,0:T(8,128)S(1)}, f32[13,64,512]{2,1,0:T(8,128)S(1)}, f32[13,64,512]{2,1,0:T(8,128)S(1)}) custom-call(bf16[384,512]{1,0:T(8,128)(2,1)S(1)} %convert_element_type.73.q_ref.refs_3_, bf16[384,512]{1,0:T(8,128)(2,1)S(1)} %copy-done.42, bf16[384,512]{1,0:T(8,128)(2,1)S(1)} %copy-done.38, ...), custom_call_target="tpu_custom_call" | custom-call | flops 18253611008 | bytes 5242880 | tf_op jit(solution)/shard_map/pallas_call | solution.py:412
  82.4 2.7 fusion.45.refs_0_
  85.1 54.2 %shard_map.298 = (f32[384,2048]{1,0:T(8,128)}, f32[4,384,256]{2,1,0:T(8,128)S(1)}, f32[4,384,256]{2,1,0:T(8,128)S(1)}, bf16[384,2048]{1,0:T(8,128)(2,1)}, f32[384,2048]{1,0:T(8,128)}, /*index=5*/f32[384,1408]{1,0:T(8,128)}) custom-call(f32[384,2048]{1,0:T(8,128)} %fusion.45.refs_0_, f32[384,2048]{1,0:T(8,128)} %convert_element_type.75.refs_1_.refs_2_, ...), custom_call_target="tpu_custom_call" | custom-call | flops 42949672960 | bytes 16777216 | tf_op jit(solution)/shard_map/pallas_call | solution.py:834
  141.7 71.2 %shard_map.299 = (f32[384,2048]{1,0:T(8,128)}, f32[4,384,256]{2,1,0:T(8,128)S(1)}, f32[4,384,256]{2,1,0:T(8,128)}, f32[384,1408]{1,0:T(8,128)}, f32[384,1408]{1,...) custom-call(f32[384,2048]{1,0:T(8,128)} %get-tuple-element.84.refs_0, ...), custom_call_target="tpu_custom_call" | custom-call | flops 42949672960 | bytes 16777216 | tf_op jit(solution)/shard_map/pallas_call | solution.py:834
  215.5 3.8 shard_map.300
  226.2 2.8 multiply_reduce_fusion.1
  229.5 4.0 fusion.40
  237.6 73.4 %shard_map.301 = (f32[384,2048]{1,0:T(8,128)}, f32[4,384,256]{2,1,0:T(8,128)}, f32[384,1408]{1,0:T(8,128)}, f32[384,512]{1,0:T(8,128)S(1)}, f32[384,512]{1,0:T(8...) custom-call(f32[384,2048]{1,0:T(8,128)} %get-tuple-element.89.refs_0, ...), custom_call_target="tpu_custom_call" | custom-call | flops 42949672960 | bytes 16777216 | tf_op jit(solution)/shard_map/pallas_call | solution.py:834
  311.7 4.6 multiply_reduce_fusion.3
  318.8 3.8 shard_map.302
  329.8 4.5 fusion.46
  337.1 79.0 %shard_map.303 = (f32[64,1152]{1,0:T(8,128)S(1)}, f32[4,384,256]{2,1,0:T(8,128)}, f32[384,512]{1,0:T(8,128)S(1)}, f32[384,512]{1,0:T(8,128)S(1)}) custom-call(f32[64,1152]{1,0:T(8,128)S(1)} %concatenate.14.refs_0_, f32[384,2048]{1,0:T(8,128)} %get-tuple-element.193.refs_1_, f32[384,512]{1,0:T(8,128)S(1)} %copy-done.45, f32[384,512]{1,0:T(8,128)S(1)} %copy-done.20), custom_call_target="tpu_custom_call" | custom-call | flops 42949672960 | bytes 16777216 | tf_op jit(solution)/shard_map/pallas_call | solution.py:834
  417.7 7.3 %shard_map.304 = (bf16[384,512]{1,0:T(8,128)(2,1)S(1)}, bf16[384,512]{1,0:T(8,128)(2,1)S(1)}, f32[384,64]{1,0:T(8,128)S(1)}) custom-call(bf16[384,512]{1,0:T(8,128)(2,1)S(1)} %copy-done.44, bf16[384,512]{1,0:T(8,128)(2,1)S(1)} %copy-done.40, f32[384,64]{1,0:T(8,128)S(1)} %copy-done.36, f32[384,64]{1,0:T(8,128)S(1)} %copy-done.33, ...), custom_call_target="tpu_custom_call" | custom-call | flops 18253611008 | bytes 8388608 | tf_op jit(solution)/shard_map/pallas_call | solution.py:450
  440.6 2.9 add_add_fusion.refs_20_
  443.5 8.6 %reduce-scatter.5.cloned.1.call-done = f32[1,256,1408]{2,1,0:T(8,128)} async-done(((f32[4,256,1408]{2,1,0:T(8,128)}), f32[1,256,1408]{2,1,0:T(8,128)}) %reduce-scatter.5.cloned.1.call-update) | async-done | bytes 1441808 | tf_op jit(solution)/shard_map/reduce_scatter | solution.py:109
  452.1 222.6 %shard_map.305 = (f32[256,512]{1,0:T(8,128)}, f32[256,512]{1,0:T(8,128)}, f32[256,512]{1,0:T(8,128)}, f32[256,512]{1,0:T(8,128)}, f32[256,512]{1,0:T(8,128)}, /*index=5*/f32[256,1408]{1,0:T(8,128)}, f32[384,2048]{1,0:T(8,128)}) custom-call(f32[384,1408]{1,0:T(8,128)} %get-tuple-element.108.refs_0_, f32[384,1408]{1,0:T(8,128)} %get-tuple-element.109.refs_1_, ...), custom_call_target="tpu_custom_call" | custom-call | flops 214748364800 | bytes 16777216 | tf_op jit(solution)/shard_map/pallas_call | solution.py:1150
  674.8 2.7 fusion.9
  677.8 11.7 %shard_map.306 = f32[40,128]{1,0:T(8,128)S(1)} custom-call(f32[8,40,128]{2,1,0:T(8,128)S(1)} %bitcast.78), custom_call_target="tpu_custom_call" | custom-call | flops 4294967296 | bytes 1048576 | tf_op jit(solution)/shard_map/pallas_call | solution.py:874
  695.9 5.5 fusion.6
  (295 shorter events, 82.6 us)
Async XLA Ops:
  7.2 75.2 %copy-start = (bf16[512,2048]{1,0:T(8,128)(2,1)S(1)}, bf16[512,2048]{1,0:T(8,128)(2,1)}, u32[]{:S(2)}) copy-start(bf16[512,2048]{1,0:T(8,128)(2,1)} %param.28) | copy-start | bytes 6291460
  7.2 320.2 %reduce-scatter.3.cloned.1.call-start = ((), (), s32[]{:S(2)}) async-start(), calls=%async_computation.2 | async-start | bytes 7208960 | tf_op jit(solution)/shard_map/reduce_scatter | solution.py:109
  59.2 17.0 %copy-start.21 = (f32[384,64]{1,0:T(8,128)}, f32[384,64]{1,0:T(8,128)S(1)}, u32[]{:S(2)}) copy-start(f32[384,64]{1,0:T(8,128)S(1)} %broadcast_in_dim.96.prev_ref.refs_9_) | copy-start | bytes 294916
  64.9 15.2 %copy-start.98 = (f32[1,512]{1,0:T(1,128)S(1)}, f32[1,512]{1,0:T(1,128)}, u32[]{:S(2)}) copy-start(f32[1,512]{1,0:T(1,128)} %param.27) | copy-start | bytes 6148
  141.7 72.2 %copy-start.8 = (bf16[384,2048]{1,0:T(8,128)(2,1)S(1)}, bf16[384,2048]{1,0:T(8,128)(2,1)}, u32[]{:S(2)}) copy-start(bf16[384,2048]{1,0:T(8,128)(2,1)} %get-tuple-element.86.refs_2_.refs_1_) | copy-start | bytes 4718596
  222.9 229.2 %reduce-scatter.5.cloned.1.call-start = ((), (), s32[]{:S(2)}) async-start(), calls=%async_computation.3 | async-start | bytes 7208960 | tf_op jit(solution)/shard_map/reduce_scatter | solution.py:109
  337.0 80.6 %copy-start.23 = (f32[384,64]{1,0:T(8,128)S(1)}, f32[384,64]{1,0:T(8,128)}, u32[]{:S(2)}) copy-start(f32[384,64]{1,0:T(8,128)} %copy-done.21) | copy-start | bytes 294916
  337.0 80.6 %copy-start.33 = (f32[384,64]{1,0:T(8,128)S(1)}, f32[384,64]{1,0:T(8,128)}, u32[]{:S(2)}) copy-start(f32[384,64]{1,0:T(8,128)} %get-tuple-element.206.new_ref.refs_7_) | copy-start | bytes 294916
  337.0 80.6 %copy-start.36 = (f32[384,64]{1,0:T(8,128)S(1)}, f32[384,64]{1,0:T(8,128)}, u32[]{:S(2)}) copy-start(f32[384,64]{1,0:T(8,128)} %get-tuple-element.207.log_ref.refs_6_) | copy-start | bytes 294916
  337.0 80.6 %copy-start.40 = (bf16[384,512]{1,0:T(8,128)(2,1)S(1)}, bf16[384,512]{1,0:T(8,128)(2,1)}, u32[]{:S(2)}) copy-start(bf16[384,512]{1,0:T(8,128)(2,1)} %copy-done.37) | copy-start | bytes 1179652
  337.0 80.6 %copy-start.44 = (bf16[384,512]{1,0:T(8,128)(2,1)S(1)}, bf16[384,512]{1,0:T(8,128)(2,1)}, u32[]{:S(2)}) copy-start(bf16[384,512]{1,0:T(8,128)(2,1)} %copy-done.41) | copy-start | bytes 1179652
  337.0 80.6 %copy-start.46 = (f32[12,64,512]{2,1,0:T(8,128)S(1)}, f32[12,64,512]{2,1,0:T(8,128)}, u32[]{:S(2)}) copy-start(f32[12,64,512]{2,1,0:T(8,128)} %get-tuple-element.122.xk_ref) | copy-start | bytes 4718596
  337.0 80.6 %copy-start.47 = (f32[12,64,512]{2,1,0:T(8,128)S(1)}, f32[12,64,512]{2,1,0:T(8,128)}, u32[]{:S(2)}) copy-start(f32[12,64,512]{2,1,0:T(8,128)} %get-tuple-element.123.xv_ref) | copy-start | bytes 4718596
  337.0 80.6 %copy-start.48 = (f32[384,512]{1,0:T(8,128)S(1)}, f32[384,512]{1,0:T(8,128)}, u32[]{:S(2)}) copy-start(f32[384,512]{1,0:T(8,128)} %get-tuple-element.118.dk_in_ref) | copy-start | bytes 2359300
  337.0 80.6 %copy-start.49 = (f32[384,512]{1,0:T(8,128)S(1)}, f32[384,512]{1,0:T(8,128)}, u32[]{:S(2)}) copy-start(f32[384,512]{1,0:T(8,128)} %get-tuple-element.119.dv_in_ref) | copy-start | bytes 2359300
  337.0 80.6 %copy-start.53 = (f32[384,64]{1,0:T(8,128)S(1)}, f32[384,64]{1,0:T(8,128)}, u32[]{:S(2)}) copy-start(f32[384,64]{1,0:T(8,128)} %copy-done.52) | copy-start | bytes 294916
  337.1 80.6 %copy-start.55 = (f32[384,64]{1,0:T(8,128)S(1)}, f32[384,64]{1,0:T(8,128)}, u32[]{:S(2)}) copy-start(f32[384,64]{1,0:T(8,128)} %copy-done.54) | copy-start | bytes 294916
  425.1 11.3 %copy-start.16 = (bf16[384,512]{1,0:T(8,128)(2,1)}, bf16[384,512]{1,0:T(8,128)(2,1)S(1)}, u32[]{:S(2)}) copy-start(bf16[384,512]{1,0:T(8,128)(2,1)S(1)} %get-tuple-element.125.refs_14_) | copy-start | bytes 1179652
  425.1 12.4 %copy-start.17 = (bf16[384,512]{1,0:T(8,128)(2,1)}, bf16[384,512]{1,0:T(8,128)(2,1)S(1)}, u32[]{:S(2)}) copy-start(bf16[384,512]{1,0:T(8,128)(2,1)S(1)} %get-tuple-element.126.refs_16_) | copy-start | bytes 1179652
  452.1 222.7 %copy-start.63 = (bf16[384,2048]{1,0:T(8,128)(2,1)S(1)}, bf16[384,2048]{1,0:T(8,128)(2,1)}, u32[]{:S(2)}) copy-start(bf16[384,2048]{1,0:T(8,128)(2,1)} %refs_3_.4) | copy-start | bytes 4718596
  452.1 222.7 %copy-start.88 = (f32[2048]{0:T(1024)S(1)}, f32[2048]{0:T(1024)}, u32[]{:S(2)}) copy-start(f32[2048]{0:T(1024)} %param.19) | copy-start | bytes 24580
  452.1 222.7 %copy-start.91 = (f32[384]{0:T(512)S(1)}, f32[384]{0:T(512)}, u32[]{:S(2)}) copy-start(f32[384]{0:T(512)} %copy-done.90) | copy-start | bytes 4612
  677.8 15.6 %copy-start.80 = (f32[256,512]{1,0:T(8,128)S(1)}, f32[256,512]{1,0:T(8,128)}, u32[]{:S(2)}) copy-start(f32[256,512]{1,0:T(8,128)} %get-tuple-element.137) | copy-start | bytes 1572868
  677.8 16.6 %copy-start.74 = (f32[256,1408]{1,0:T(8,128)S(1)}, f32[256,1408]{1,0:T(8,128)}, u32[]{:S(2)}) copy-start(f32[256,1408]{1,0:T(8,128)} %get-tuple-element.140) | copy-start | bytes 4325380
  (82 other events, 290.5 us)
Sparse Core Ops, SparseCore 0:
  223.0 104.3 reduce-scatter.2
  330.3 121.7 reduce-scatter.4

commit v5 on v4

--- a/solution.py
+++ b/solution.py
@@ -8,7 +8,7 @@
 from jax.experimental.pallas import tpu as pltpu
 from jax.sharding import PartitionSpec as P
 
-CHUNK = 32
+CHUNK = 64
 CHUNKS = 4
 MESH = pl.DeviceIdType.MESH
 VMEM = 24 << 20
@@ -893,6 +893,13 @@
     return jnp.concatenate([keep, jnp.full_like(keep, doc), keys, values], axis=1)
 
 
+def head_parts(size, count):
+    whole = [(at, 256) for at in range(0, size, 256)]
+    last = whole[:-1] + [(size - 256, 128), (size - 128, 128)]
+    sides = [0, count - 1, *range(1, count - 1)]
+    return [(i, *tile) for i in sides for tile in (last if i == sides[-1] else whole)]
+
+
 def final_kernel(tiles, head_count, *refs):
     act_in, near_in, dy_own, dy_their, dy_near, dy_far, in_own, in_their, branch_own, branch_their = refs[:10]
     sides = refs[10 : 10 + 2 * head_count]
@@ -909,9 +916,10 @@
     rows = act.shape[0]
     wide = out_down.shape[0]
     head = heads.shape[1] // head_count
-    columns = [pl.ds(i * 256, 256) for i in range(heads.shape[1] // 256)]
+    parts = head_parts(head, head_count)
+    columns = [pl.ds(i * head + begin, size) for i, begin, size in parts]
     down = [pl.ds(*tile) for tile in tiles]
-    out = [outs[i // 2].at[:, pl.ds(i % 2 * 256, 256)] for i in range(len(columns))]
+    out = [outs[i].at[:, pl.ds(begin, size)] for i, begin, size in parts]
 
     number = lax.axis_index("head")
     sibling, over_y = {"head": other_of(number, 1)}, {"head": other_of(number, 2)}
@@ -933,7 +941,7 @@
 
     in_loads, branch_loads, dy_loads = (
         [
-            load(
+            pltpu.make_async_copy(
                 source.at[:, pl.ds(start, wide)],
                 target.at[pl.ds(0, rows), pl.ds(r * wide, wide)],
                 own_sems.at[k, r],
@@ -944,6 +952,8 @@
             ((in_own, wide_in), (branch_own, wide_branch), (dy_own, wide_dy))
         )
     )
+    for one in in_loads:
+        one.start()
     head_loads = [
         load(sides[2 * i], heads.at[pl.ds(0, rows), pl.ds(i * head, head)], head_sems.at[0, i])
         for i in range(head_count)
@@ -951,8 +961,8 @@
     ready = (0, head_count - 1)
     head_loads += [load(sides[2 * i + 1], stage_head.at[i], head_sems.at[1, i]) for i in ready]
     act_loads = [
-        load(act_in, act, act_sems.at[0]),
-        load(near_in, near_act, act_sems.at[1]),
+        pltpu.make_async_copy(act_in, act, act_sems.at[0]),
+        pltpu.make_async_copy(near_in, near_act, act_sems.at[1]),
     ]
     jobs = [(in_their, wide_in, 1), (branch_their, wide_branch, 1)]
     jobs += [(dy_their, wide_dy, 1), (dy_near, wide_dy, 2), (dy_far, wide_dy, 3)]
@@ -963,7 +973,12 @@
             for r, role in enumerate(roles)
         ]
 
-    under_way = {0: staged(0), 1: staged(1)}
+    under_way = {0: staged(0)}
+    for one in branch_loads:
+        one.start()
+    under_way[1] = staged(1)
+    for one in dy_loads + act_loads:
+        one.start()
 
     def settle(k):
         for one in under_way[k]:
@@ -994,13 +1009,6 @@
         remote(sides[2 * i + 1], stage_head.at[i], 7, i - 1, partner)
         for i in range(1, head_count - 1)
     ]
-    for one in nears:
-        one.start()
-    for one in in_loads + head_loads:
-        one.wait()
-    settle(0)
-    settle(1)
-
     second = pl.ds(wide, wide)
     to_side = [remote(far.at[:, c], far.at[:, c], 0, i, beside) for i, c in enumerate(columns)]
     over = [
@@ -1016,6 +1024,45 @@
         remote(from_middle.at[second, c], out_down.at[:, c], 6, i, beside) for i, c in enumerate(down)
     ]
 
+    down_at = {min(2 * j, len(columns) - len(down) + j - 2): j for j in range(len(down))}
+    order = range(len(parts))
+
+    def wide_of(i):
+        return wide_branch if parts[i][0] == head_count - 1 else wide_in
+
+    for one in nears:
+        one.start()
+
+    @pl.when(in_middle)
+    def _():
+        trades[0].start()
+        passes[0].start()
+
+    for one in in_loads + head_loads:
+        one.wait()
+    settle(0)
+
+    def receive(i):
+        if 0 < i < head_count - 1:
+            head_trades[i - 1].wait_recv()
+        heads[rows:, i * head : (i + 1) * head] = stage_head[i].astype(jnp.bfloat16)
+
+    receive(0)
+
+    def to_middle_tile(i):
+        far[:, columns[i]] = tn(wide_of(i)[:, : 3 * wide], heads[:, columns[i]])
+        to_side[i].start()
+
+    first = [i for i in range(len(parts)) if parts[i][0] == 0]
+
+    @pl.when(at_end)
+    def _():
+        for i in first:
+            to_middle_tile(i)
+
+    settle(1)
+    receive(head_count - 1)
+
     @pl.when(at_end)
     def _():
         for one in head_trades:
@@ -1029,8 +1076,9 @@
         settle(3)
         settle(4)
         for i, (trade, onward) in enumerate(zip(trades, passes)):
-            trade.start()
-            onward.start()
+            if i:
+                trade.start()
+                onward.start()
             if i < len(head_trades):
                 head_trades[i].start()
 
@@ -1039,20 +1087,6 @@
         own_sum[c] = part[mine_of[c], :] + near[c]
         sums[c].start()
 
-    def receive(i):
-        if 0 < i < head_count - 1:
-            head_trades[i - 1].wait_recv()
-        heads[rows:, i * head : (i + 1) * head] = stage_head[i].astype(jnp.bfloat16)
-
-    for i in ready:
-        receive(i)
-
-    down_at = {min(2 * j, len(columns) - len(down) + j): j for j in range(len(down))}
-    order = [0, 1, 2 * head_count - 2, 2 * head_count - 1, *range(2, 2 * head_count - 2)]
-
-    def wide_of(i):
-        return wide_branch if i >= 2 * (head_count - 1) else wide_in
-
     def settle_down():
         for one in dy_loads + act_loads:
             one.wait()
@@ -1063,10 +1097,10 @@
     @pl.when(at_end)
     def _():
         for k, i in enumerate(order):
-            if k > 3 and i % 2 == 0:
-                receive(i // 2)
-            far[:, columns[i]] = tn(wide_of(i)[:, : 3 * wide], heads[:, columns[i]])
-            to_side[i].start()
+            if parts[i][0] not in ready and parts[i][1] == 0:
+                receive(parts[i][0])
+            if i not in first:
+                to_middle_tile(i)
         settle_down()
 
     @pl.when(at_end)
@@ -1094,8 +1128,8 @@
         settle_down()
         for k, i in enumerate(order):
             c = columns[i]
-            if k > 3 and i % 2 == 0:
-                receive(i // 2)
+            if parts[i][0] not in ready and parts[i][1] == 0:
+                receive(parts[i][0])
             j = down_at.get(k)
             if j is not None:
                 d = down[j]
@@ -1172,7 +1206,7 @@
             pltpu.VMEM(half, f32), pltpu.VMEM(half, f32), pltpu.VMEM(half, f32),
             dma((3, 4)), dma((2, count)), dma((2, 4)), dma((2,)),
         ]
-        + [dma((total // 256,))] * 6
+        + [dma((len(head_parts(head, count)),))] * 6
         + [dma((len(tiles),))] * 8
         + [dma((count - 2,))] * 2
         + [dma((CHUNKS,))] * 6,

time: 718 us -> 711 us (level)
  Pallas kernels: 561 us -> 550 us
where the time goes in v5:
time: 711 us; the launch traced here: 705 us
  Pallas kernels  550 us (77%)
  local copies, waits for them, and re-layouts  48.1 us (7%)
  other arithmetic  46.9 us (7%)
  matrix products  27.3 us (4%)
  between operations  16.7 us (2%)
  waiting for transfers between devices  15.5 us (2%)
    pallas_call x5, Pallas kernels, exchange(): pl.pallas_call(functools.partial(exchange_kernel, names, count, heads, re...  299 us
    pallas_call x1, Pallas kernels, final_gradients(): pl.pallas_call(functools.partial(final_kernel, tiles, count), out_shape=(...  222 us
    unnamed x218, local copies, waits for them, and re-layouts  35.3 us
    reduce_scatter x2, waiting for transfers between devices, line_sum(): lax.psum_scatter(product, 'seq', scatter_dimension=0, axis_index_groups=g...  15.5 us
  transfers between devices with their start and end apart: 2, of which 2 were waited for; matrix products, arithmetic and copies ran while one was open for 6% of the time, Pallas kernels for 23%

profile of v5, /device:TPU:0, one launch (start us, length us, event | category | flops | bytes accessed | tf_op | source)
XLA Modules:
  0.0 704.8 jit_solution(16435017011022706571)
XLA Ops:
  10.0 2.9 fusion
  13.5 3.5 fusion.41
  22.0 3.3 convolution_convert_fusion.v_ref.refs_5_
  29.7 22.6 %shard_map.296 = (f32[64,1152]{1,0:T(8,128)S(1)}, f32[384,512]{1,0:T(8,128)S(1)}, f32[384,512]{1,0:T(8,128)S(1)}) custom-call(f32[64,1152]{1,0:T(8,128)S(1)} %concatenate.12.refs_0_, bf16[384,2048]{1,0:T(8,128)(2,1)S(1)} %copy-done.6, bf16[2048,512]{1,0:T(8,128)(2,1)} %refs_2_.2, bf16[2048,512]{1,0:T(8,128)(2,1)} %refs_3_.3), custom_call_target="tpu_custom_call" | custom-call | flops 42949672960 | bytes 16777216 | tf_op jit(solution)/shard_map/pallas_call | solution.py:834
  54.5 3.5 convert_element_type.75.refs_1_.refs_2_
  64.9 8.6 %shard_map.297 = (f32[384,512]{1,0:T(8,128)S(1)}, f32[384,64]{1,0:T(8,128)S(1)}, f32[384,64]{1,0:T(8,128)S(1)}, f32[7,64,512]{2,1,0:T(8,128)S(1)}, f32[7,64,512]{2,1,0:T(8,128)S(1)}) custom-call(bf16[384,512]{1,0:T(8,128)(2,1)S(1)} %convert_element_type.73.q_ref.refs_3_, bf16[384,512]{1,0:T(8,128)(2,1)S(1)} %copy-done.42, bf16[384,512]{1,0:T(8,128)(2,1)S(1)} %copy-done.38, ...), custom_call_target="tpu_custom_call" | custom-call | flops 18253611008 | bytes 5242880 | tf_op jit(solution)/shard_map/pallas_call | solution.py:412
  81.9 54.3 %shard_map.298 = (f32[384,2048]{1,0:T(8,128)}, f32[4,384,256]{2,1,0:T(8,128)S(1)}, f32[4,384,256]{2,1,0:T(8,128)S(1)}, bf16[384,2048]{1,0:T(8,128)(2,1)}, f32[384,2048]{1,0:T(8,128)}, /*index=5*/f32[384,1408]{1,0:T(8,128)}) custom-call(f32[384,2048]{1,0:T(8,128)} %fusion.45.refs_0_, f32[384,2048]{1,0:T(8,128)} %convert_element_type.75.refs_1_.refs_2_, ...), custom_call_target="tpu_custom_call" | custom-call | flops 42949672960 | bytes 16777216 | tf_op jit(solution)/shard_map/pallas_call | solution.py:834
  138.5 71.2 %shard_map.299 = (f32[384,2048]{1,0:T(8,128)}, f32[4,384,256]{2,1,0:T(8,128)S(1)}, f32[4,384,256]{2,1,0:T(8,128)}, f32[384,1408]{1,0:T(8,128)}, f32[384,1408]{1,...) custom-call(f32[384,2048]{1,0:T(8,128)} %get-tuple-element.84.refs_0, ...), custom_call_target="tpu_custom_call" | custom-call | flops 42949672960 | bytes 16777216 | tf_op jit(solution)/shard_map/pallas_call | solution.py:834
  212.3 4.3 shard_map.300
  223.2 2.8 multiply_reduce_fusion.1
  226.5 4.1 fusion.40
  234.8 72.3 %shard_map.301 = (f32[384,2048]{1,0:T(8,128)}, f32[4,384,256]{2,1,0:T(8,128)}, f32[384,1408]{1,0:T(8,128)}, f32[384,512]{1,0:T(8,128)S(1)}, f32[384,512]{1,0:T(8...) custom-call(f32[384,2048]{1,0:T(8,128)} %get-tuple-element.89.refs_0, ...), custom_call_target="tpu_custom_call" | custom-call | flops 42949672960 | bytes 16777216 | tf_op jit(solution)/shard_map/pallas_call | solution.py:834
  307.8 4.6 multiply_reduce_fusion.3
  314.9 3.8 shard_map.302
  321.2 3.9 reduce-scatter.3.cloned.1.call-done
  327.5 4.5 fusion.46
  334.8 78.8 %shard_map.303 = (f32[64,1152]{1,0:T(8,128)S(1)}, f32[4,384,256]{2,1,0:T(8,128)}, f32[384,512]{1,0:T(8,128)S(1)}, f32[384,512]{1,0:T(8,128)S(1)}) custom-call(f32[64,1152]{1,0:T(8,128)S(1)} %concatenate.14.refs_0_, f32[384,2048]{1,0:T(8,128)} %get-tuple-element.193.refs_1_, f32[384,512]{1,0:T(8,128)S(1)} %copy-done.45, f32[384,512]{1,0:T(8,128)S(1)} %copy-done.20), custom_call_target="tpu_custom_call" | custom-call | flops 42949672960 | bytes 16777216 | tf_op jit(solution)/shard_map/pallas_call | solution.py:834
  415.2 4.5 shard_map.304
  435.4 2.9 add_add_fusion.refs_20_
  438.2 11.6 %reduce-scatter.5.cloned.1.call-done = f32[1,256,1408]{2,1,0:T(8,128)} async-done(((f32[4,256,1408]{2,1,0:T(8,128)}), f32[1,256,1408]{2,1,0:T(8,128)}) %reduce-scatter.5.cloned.1.call-update) | async-done | bytes 1441808 | tf_op jit(solution)/shard_map/reduce_scatter | solution.py:109
  449.8 221.8 %shard_map.305 = (f32[256,512]{1,0:T(8,128)}, f32[256,512]{1,0:T(8,128)}, f32[256,512]{1,0:T(8,128)}, f32[256,512]{1,0:T(8,128)}, f32[256,512]{1,0:T(8,128)}, /*index=5*/f32[256,1408]{1,0:T(8,128)}, f32[384,2048]{1,0:T(8,128)}) custom-call(f32[384,1408]{1,0:T(8,128)} %get-tuple-element.108.refs_0_, f32[384,1408]{1,0:T(8,128)} %get-tuple-element.109.refs_1_, ...), custom_call_target="tpu_custom_call" | custom-call | flops 214748364800 | bytes 16777216 | tf_op jit(solution)/shard_map/pallas_call | solution.py:1184
  671.7 2.7 fusion.9
  674.7 8.1 %shard_map.306 = f32[40,128]{1,0:T(8,128)S(1)} custom-call(f32[8,40,128]{2,1,0:T(8,128)S(1)} %bitcast.78), custom_call_target="tpu_custom_call" | custom-call | flops 4294967296 | bytes 1048576 | tf_op jit(solution)/shard_map/pallas_call | solution.py:874
  689.1 5.5 fusion.6
  (295 shorter events, 82.2 us)
Async XLA Ops:
  7.2 72.0 %copy-start = (bf16[512,2048]{1,0:T(8,128)(2,1)S(1)}, bf16[512,2048]{1,0:T(8,128)(2,1)}, u32[]{:S(2)}) copy-start(bf16[512,2048]{1,0:T(8,128)(2,1)} %param.28) | copy-start | bytes 6291460
  7.2 317.9 %reduce-scatter.3.cloned.1.call-start = ((), (), s32[]{:S(2)}) async-start(), calls=%async_computation.2 | async-start | bytes 7208960 | tf_op jit(solution)/shard_map/reduce_scatter | solution.py:109
  59.1 14.4 %copy-start.21 = (f32[384,64]{1,0:T(8,128)}, f32[384,64]{1,0:T(8,128)S(1)}, u32[]{:S(2)}) copy-start(f32[384,64]{1,0:T(8,128)S(1)} %broadcast_in_dim.96.prev_ref.refs_9_) | copy-start | bytes 294916
  64.9 12.0 %copy-start.98 = (f32[1,512]{1,0:T(1,128)S(1)}, f32[1,512]{1,0:T(1,128)}, u32[]{:S(2)}) copy-start(f32[1,512]{1,0:T(1,128)} %param.27) | copy-start | bytes 6148
  138.5 72.2 %copy-start.8 = (bf16[384,2048]{1,0:T(8,128)(2,1)S(1)}, bf16[384,2048]{1,0:T(8,128)(2,1)}, u32[]{:S(2)}) copy-start(bf16[384,2048]{1,0:T(8,128)(2,1)} %get-tuple-element.86.refs_2_.refs_1_) | copy-start | bytes 4718596
  220.3 229.5 %reduce-scatter.5.cloned.1.call-start = ((), (), s32[]{:S(2)}) async-start(), calls=%async_computation.3 | async-start | bytes 7208960 | tf_op jit(solution)/shard_map/reduce_scatter | solution.py:109
  334.7 80.4 %copy-start.23 = (f32[384,64]{1,0:T(8,128)S(1)}, f32[384,64]{1,0:T(8,128)}, u32[]{:S(2)}) copy-start(f32[384,64]{1,0:T(8,128)} %copy-done.21) | copy-start | bytes 294916
  334.7 80.4 %copy-start.33 = (f32[384,64]{1,0:T(8,128)S(1)}, f32[384,64]{1,0:T(8,128)}, u32[]{:S(2)}) copy-start(f32[384,64]{1,0:T(8,128)} %get-tuple-element.206.new_ref.refs_7_) | copy-start | bytes 294916
  334.7 80.4 %copy-start.36 = (f32[384,64]{1,0:T(8,128)S(1)}, f32[384,64]{1,0:T(8,128)}, u32[]{:S(2)}) copy-start(f32[384,64]{1,0:T(8,128)} %get-tuple-element.207.log_ref.refs_6_) | copy-start | bytes 294916
  334.7 80.4 %copy-start.40 = (bf16[384,512]{1,0:T(8,128)(2,1)S(1)}, bf16[384,512]{1,0:T(8,128)(2,1)}, u32[]{:S(2)}) copy-start(bf16[384,512]{1,0:T(8,128)(2,1)} %copy-done.37) | copy-start | bytes 1179652
  334.7 80.4 %copy-start.44 = (bf16[384,512]{1,0:T(8,128)(2,1)S(1)}, bf16[384,512]{1,0:T(8,128)(2,1)}, u32[]{:S(2)}) copy-start(bf16[384,512]{1,0:T(8,128)(2,1)} %copy-done.41) | copy-start | bytes 1179652
  334.7 80.4 %copy-start.46 = (f32[384,512]{1,0:T(8,128)S(1)}, f32[384,512]{1,0:T(8,128)}, u32[]{:S(2)}) copy-start(f32[384,512]{1,0:T(8,128)} %get-tuple-element.118.dk_in_ref) | copy-start | bytes 2359300
  334.7 80.4 %copy-start.47 = (f32[384,512]{1,0:T(8,128)S(1)}, f32[384,512]{1,0:T(8,128)}, u32[]{:S(2)}) copy-start(f32[384,512]{1,0:T(8,128)} %get-tuple-element.119.dv_in_ref) | copy-start | bytes 2359300
  334.7 80.4 %copy-start.48 = (f32[6,64,512]{2,1,0:T(8,128)S(1)}, f32[6,64,512]{2,1,0:T(8,128)}, u32[]{:S(2)}) copy-start(f32[6,64,512]{2,1,0:T(8,128)} %get-tuple-element.122.xk_ref) | copy-start | bytes 2359300
  334.7 80.4 %copy-start.49 = (f32[6,64,512]{2,1,0:T(8,128)S(1)}, f32[6,64,512]{2,1,0:T(8,128)}, u32[]{:S(2)}) copy-start(f32[6,64,512]{2,1,0:T(8,128)} %get-tuple-element.123.xv_ref) | copy-start | bytes 2359300
  334.8 80.4 %copy-start.53 = (f32[384,64]{1,0:T(8,128)S(1)}, f32[384,64]{1,0:T(8,128)}, u32[]{:S(2)}) copy-start(f32[384,64]{1,0:T(8,128)} %copy-done.52) | copy-start | bytes 294916
  334.8 80.4 %copy-start.55 = (f32[384,64]{1,0:T(8,128)S(1)}, f32[384,64]{1,0:T(8,128)}, u32[]{:S(2)}) copy-start(f32[384,64]{1,0:T(8,128)} %copy-done.54) | copy-start | bytes 294916
  419.7 11.3 %copy-start.16 = (bf16[384,512]{1,0:T(8,128)(2,1)}, bf16[384,512]{1,0:T(8,128)(2,1)S(1)}, u32[]{:S(2)}) copy-start(bf16[384,512]{1,0:T(8,128)(2,1)S(1)} %get-tuple-element.125.refs_14_) | copy-start | bytes 1179652
  419.7 12.4 %copy-start.17 = (bf16[384,512]{1,0:T(8,128)(2,1)}, bf16[384,512]{1,0:T(8,128)(2,1)S(1)}, u32[]{:S(2)}) copy-start(bf16[384,512]{1,0:T(8,128)(2,1)S(1)} %get-tuple-element.126.refs_16_) | copy-start | bytes 1179652
  449.8 221.9 %copy-start.63 = (bf16[384,2048]{1,0:T(8,128)(2,1)S(1)}, bf16[384,2048]{1,0:T(8,128)(2,1)}, u32[]{:S(2)}) copy-start(bf16[384,2048]{1,0:T(8,128)(2,1)} %refs_3_.4) | copy-start | bytes 4718596
  449.8 221.9 %copy-start.88 = (f32[2048]{0:T(1024)S(1)}, f32[2048]{0:T(1024)}, u32[]{:S(2)}) copy-start(f32[2048]{0:T(1024)} %param.19) | copy-start | bytes 24580
  449.8 221.9 %copy-start.91 = (f32[384]{0:T(512)S(1)}, f32[384]{0:T(512)}, u32[]{:S(2)}) copy-start(f32[384]{0:T(512)} %copy-done.90) | copy-start | bytes 4612
  674.7 11.9 %copy-start.80 = (f32[256,512]{1,0:T(8,128)S(1)}, f32[256,512]{1,0:T(8,128)}, u32[]{:S(2)}) copy-start(f32[256,512]{1,0:T(8,128)} %get-tuple-element.137) | copy-start | bytes 1572868
  674.7 12.9 %copy-start.74 = (f32[256,1408]{1,0:T(8,128)S(1)}, f32[256,1408]{1,0:T(8,128)}, u32[]{:S(2)}) copy-start(f32[256,1408]{1,0:T(8,128)} %get-tuple-element.140) | copy-start | bytes 4325380
  (82 other events, 280.8 us)
Sparse Core Ops, SparseCore 0:
  220.4 104.6 reduce-scatter.2
  328.0 121.7 reduce-scatter.4

commit v6 on v5

--- a/solution.py
+++ b/solution.py
@@ -212,6 +212,11 @@
             span_s[j, 8 * r : 8 * r + 8] = jnp.where(ok, jnp.exp(run[r] - running[j : j + 1]), 0.0)
 
 
+def doc_before(doc_ref, first_ref, i, size):
+    row = doc_ref[pl.ds(jnp.maximum(i * size - 1, 0), 1), :]
+    return jnp.where(i == 0, first_ref[...], row)
+
+
 def to_end(running, docs):
     last = running.shape[0] - 1
     return jnp.where(
@@ -242,7 +247,7 @@
         queries, keys, values = q_ref[rows, :], k_ref[rows, :], v_ref[rows, :]
         new, docs = new_ref[rows, :], doc_ref[rows, :]
         running = exact_dot(lower, log_ref[rows, :])
-        carried = jnp.where(docs == prev_ref[rows, :], jnp.exp(running), 0.0)
+        carried = jnp.where(docs == doc_before(doc_ref, prev_ref, i, size), jnp.exp(running), 0.0)
         key_state, value_state = ks_ref[i], vs_ref[i]
         spans(running, docs, span_s)
         affinity = row_blocks(nt(queries, keys))
@@ -298,7 +303,7 @@
         queries, keys, values, grads = q_ref[rows, :], k_ref[rows, :], v_ref[rows, :], g_ref[rows, :]
         new, docs = new_ref[rows, :], doc_ref[rows, :]
         running = exact_dot(lower, log_ref[rows, :])
-        carried = jnp.where(docs == prev_ref[rows, :], jnp.exp(running), 0.0)
+        carried = jnp.where(docs == doc_before(doc_ref, prev_ref, i, size), jnp.exp(running), 0.0)
         spans(running, docs, span_s)
         affinity = row_blocks(nt(queries, keys))
         grad_high, grad_low = split(grads)
@@ -374,7 +379,7 @@
         keys, values = k_ref[rows, :], v_ref[rows, :]
         logs, new, docs = log_ref[rows, :], new_ref[rows, :], doc_ref[rows, :]
         running = exact_dot(lower, logs)
-        carried = jnp.where(docs == prev_ref[rows, :], jnp.exp(running), 0.0)
+        carried = jnp.where(docs == doc_before(doc_ref, prev_ref, i, size), jnp.exp(running), 0.0)
         end = to_end(running, docs)
         weight = end * new
         dk_ref[rows, :] = (dk_in_ref[rows, :] + three(nn, weight, ks[...])).astype(dk_ref.dtype)
@@ -1476,9 +1481,8 @@
     key_in, value_in = prefix[:, 128 : 128 + head_width], prefix[:, 128 + head_width :]
     prior = prefix[0, 64]
     decay_all = jnp.where(docs[tok_rows - 1] == prior, jnp.exp(total), 0.0)
-    before = jnp.concatenate([prior[None], docs[CHUNK - 1 : -1 : CHUNK]])
     docs = jnp.broadcast_to(docs[:, None], (tok_rows, slots))
-    before = jnp.broadcast_to(jnp.repeat(before, CHUNK)[:, None], (tok_rows, slots))
+    before = jnp.broadcast_to(prior, (1, slots))
     slot_read, scores, probs, key_states, value_states = read_slots(
         query_rows, key_rows, value_rows, log_decay, new, docs, before, key_in, value_in
     )

time: 711 us -> 705 us (level)
    unnamed x218 -> x212, local copies, waits for them, and re-layouts: 35.3 us -> 28.8 us
  transfers between devices with their start and end apart: 2 -> 2, of which waited for: 2 -> 2; matrix products, arithmetic and copies ran while one was open for 6% -> 7% of each run, Pallas kernels for 23% -> 23%
where the time goes in v6:
time: 705 us; the launch traced here: 699 us
  Pallas kernels  551 us (78%)
  other arithmetic  46.4 us (7%)
  local copies, waits for them, and re-layouts  41.9 us (6%)
  matrix products  27 us (4%)
  between operations  16.7 us (2%)
  waiting for transfers between devices  16.2 us (2%)
    pallas_call x5, Pallas kernels, exchange(): pl.pallas_call(functools.partial(exchange_kernel, names, count, heads, re...  299 us
    pallas_call x1, Pallas kernels, final_gradients(): pl.pallas_call(functools.partial(final_kernel, tiles, count), out_shape=(...  222 us
    unnamed x212, local copies, waits for them, and re-layouts  28.8 us
    reduce_scatter x2, waiting for transfers between devices, line_sum(): lax.psum_scatter(product, 'seq', scatter_dimension=0, axis_index_groups=g...  16.1 us
  transfers between devices with their start and end apart: 2, of which 2 were waited for; matrix products, arithmetic and copies ran while one was open for 7% of the time, Pallas kernels for 23%

profile of v6, /device:TPU:0, one launch (start us, length us, event | category | flops | bytes accessed | tf_op | source)
XLA Modules:
  0.0 698.8 jit_solution(16512197621418197862)
XLA Ops:
  9.3 2.9 fusion
  12.8 3.5 fusion.41
  21.9 3.0 convolution_convert_fusion.v_ref.refs_5_
  29.3 22.6 %shard_map.296 = (f32[64,1152]{1,0:T(8,128)S(1)}, f32[384,512]{1,0:T(8,128)S(1)}, f32[384,512]{1,0:T(8,128)S(1)}) custom-call(f32[64,1152]{1,0:T(8,128)S(1)} %concatenate.9.refs_0_, bf16[384,2048]{1,0:T(8,128)(2,1)S(1)} %copy-done.6, bf16[2048,512]{1,0:T(8,128)(2,1)} %refs_2_.2, bf16[2048,512]{1,0:T(8,128)(2,1)} %refs_3_.3), custom_call_target="tpu_custom_call" | custom-call | flops 42949672960 | bytes 16777216 | tf_op jit(solution)/shard_map/pallas_call | solution.py:839
  54.2 3.6 convert_element_type.75.refs_1_.refs_2_
  58.6 8.6 %shard_map.297 = (f32[384,512]{1,0:T(8,128)S(1)}, f32[384,64]{1,0:T(8,128)S(1)}, f32[384,64]{1,0:T(8,128)S(1)}, f32[7,64,512]{2,1,0:T(8,128)S(1)}, f32[7,64,512]{2,1,0:T(8,128)S(1)}) custom-call(bf16[384,512]{1,0:T(8,128)(2,1)S(1)} %convert_element_type.73.q_ref.refs_3_, bf16[384,512]{1,0:T(8,128)(2,1)S(1)} %copy-done.39, bf16[384,512]{1,0:T(8,128)(2,1)S(1)} %copy-done.35, ...), custom_call_target="tpu_custom_call" | custom-call | flops 18253611008 | bytes 5242880 | tf_op jit(solution)/shard_map/pallas_call | solution.py:417
  75.6 54.3 %shard_map.298 = (f32[384,2048]{1,0:T(8,128)}, f32[4,384,256]{2,1,0:T(8,128)S(1)}, f32[4,384,256]{2,1,0:T(8,128)S(1)}, bf16[384,2048]{1,0:T(8,128)(2,1)}, f32[384,2048]{1,0:T(8,128)}, /*index=5*/f32[384,1408]{1,0:T(8,128)}) custom-call(f32[384,2048]{1,0:T(8,128)} %fusion.45.refs_0_, f32[384,2048]{1,0:T(8,128)} %convert_element_type.75.refs_1_.refs_2_, ...), custom_call_target="tpu_custom_call" | custom-call | flops 42949672960 | bytes 16777216 | tf_op jit(solution)/shard_map/pallas_call | solution.py:839
  132.2 71.1 %shard_map.299 = (f32[384,2048]{1,0:T(8,128)}, f32[4,384,256]{2,1,0:T(8,128)S(1)}, f32[4,384,256]{2,1,0:T(8,128)}, f32[384,1408]{1,0:T(8,128)}, f32[384,1408]{1,...) custom-call(f32[384,2048]{1,0:T(8,128)} %get-tuple-element.84.refs_0, ...), custom_call_target="tpu_custom_call" | custom-call | flops 42949672960 | bytes 16777216 | tf_op jit(solution)/shard_map/pallas_call | solution.py:839
  206.0 4.3 shard_map.300
  216.9 2.8 multiply_reduce_fusion.1
  220.2 4.1 fusion.40
  228.4 72.3 %shard_map.301 = (f32[384,2048]{1,0:T(8,128)}, f32[4,384,256]{2,1,0:T(8,128)}, f32[384,1408]{1,0:T(8,128)}, f32[384,512]{1,0:T(8,128)S(1)}, f32[384,512]{1,0:T(8...) custom-call(f32[384,2048]{1,0:T(8,128)} %get-tuple-element.89.refs_0, ...), custom_call_target="tpu_custom_call" | custom-call | flops 42949672960 | bytes 16777216 | tf_op jit(solution)/shard_map/pallas_call | solution.py:839
  300.8 4.6 multiply_reduce_fusion.3
  308.0 3.8 shard_map.302
  314.3 4.5 reduce-scatter.3.cloned.1.call-done
  321.3 4.5 fusion.46
  328.5 78.9 %shard_map.303 = (f32[64,1152]{1,0:T(8,128)S(1)}, f32[4,384,256]{2,1,0:T(8,128)}, f32[384,512]{1,0:T(8,128)S(1)}, f32[384,512]{1,0:T(8,128)S(1)}) custom-call(f32[64,1152]{1,0:T(8,128)S(1)} %concatenate.10.refs_0_, f32[384,2048]{1,0:T(8,128)} %get-tuple-element.193.refs_1_, f32[384,512]{1,0:T(8,128)S(1)} %copy-done.42, f32[384,512]{1,0:T(8,128)S(1)} %copy-done.20), custom_call_target="tpu_custom_call" | custom-call | flops 42949672960 | bytes 16777216 | tf_op jit(solution)/shard_map/pallas_call | solution.py:839
  408.9 4.5 shard_map.304
  429.1 2.8 add_add_fusion.refs_20_
  431.9 11.6 %reduce-scatter.5.cloned.1.call-done = f32[1,256,1408]{2,1,0:T(8,128)} async-done(((f32[4,256,1408]{2,1,0:T(8,128)}), f32[1,256,1408]{2,1,0:T(8,128)}) %reduce-scatter.5.cloned.1.call-update) | async-done | bytes 1441808 | tf_op jit(solution)/shard_map/reduce_scatter | solution.py:109
  443.5 221.8 %shard_map.305 = (f32[256,512]{1,0:T(8,128)}, f32[256,512]{1,0:T(8,128)}, f32[256,512]{1,0:T(8,128)}, f32[256,512]{1,0:T(8,128)}, f32[256,512]{1,0:T(8,128)}, /*index=5*/f32[256,1408]{1,0:T(8,128)}, f32[384,2048]{1,0:T(8,128)}) custom-call(f32[384,1408]{1,0:T(8,128)} %get-tuple-element.108.refs_0_, f32[384,1408]{1,0:T(8,128)} %get-tuple-element.109.refs_1_, ...), custom_call_target="tpu_custom_call" | custom-call | flops 214748364800 | bytes 16777216 | tf_op jit(solution)/shard_map/pallas_call | solution.py:1189
  665.4 2.7 fusion.9
  668.4 8.4 %shard_map.306 = f32[40,128]{1,0:T(8,128)S(1)} custom-call(f32[8,40,128]{2,1,0:T(8,128)S(1)} %bitcast.77), custom_call_target="tpu_custom_call" | custom-call | flops 4294967296 | bytes 1048576 | tf_op jit(solution)/shard_map/pallas_call | solution.py:879
  683.1 5.5 fusion.6
  (285 shorter events, 75.3 us)
Async XLA Ops:
  7.2 65.7 %copy-start = (bf16[512,2048]{1,0:T(8,128)(2,1)S(1)}, bf16[512,2048]{1,0:T(8,128)(2,1)}, u32[]{:S(2)}) copy-start(bf16[512,2048]{1,0:T(8,128)(2,1)} %param.28) | copy-start | bytes 6291460
  7.2 311.7 %reduce-scatter.3.cloned.1.call-start = ((), (), s32[]{:S(2)}) async-start(), calls=%async_computation.2 | async-start | bytes 7208960 | tf_op jit(solution)/shard_map/reduce_scatter | solution.py:109
  58.6 12.0 %copy-start.95 = (f32[1,512]{1,0:T(1,128)S(1)}, f32[1,512]{1,0:T(1,128)}, u32[]{:S(2)}) copy-start(f32[1,512]{1,0:T(1,128)} %param.27) | copy-start | bytes 6148
  132.2 72.1 %copy-start.8 = (bf16[384,2048]{1,0:T(8,128)(2,1)S(1)}, bf16[384,2048]{1,0:T(8,128)(2,1)}, u32[]{:S(2)}) copy-start(bf16[384,2048]{1,0:T(8,128)(2,1)} %get-tuple-element.86.refs_2_.refs_1_) | copy-start | bytes 4718596
  214.0 229.5 %reduce-scatter.5.cloned.1.call-start = ((), (), s32[]{:S(2)}) async-start(), calls=%async_computation.3 | async-start | bytes 7208960 | tf_op jit(solution)/shard_map/reduce_scatter | solution.py:109
  328.4 80.4 %copy-start.30 = (f32[384,64]{1,0:T(8,128)S(1)}, f32[384,64]{1,0:T(8,128)}, u32[]{:S(2)}) copy-start(f32[384,64]{1,0:T(8,128)} %get-tuple-element.206.new_ref.refs_7_) | copy-start | bytes 294916
  328.4 80.4 %copy-start.33 = (f32[384,64]{1,0:T(8,128)S(1)}, f32[384,64]{1,0:T(8,128)}, u32[]{:S(2)}) copy-start(f32[384,64]{1,0:T(8,128)} %get-tuple-element.207.log_ref.refs_6_) | copy-start | bytes 294916
  328.4 80.4 %copy-start.37 = (bf16[384,512]{1,0:T(8,128)(2,1)S(1)}, bf16[384,512]{1,0:T(8,128)(2,1)}, u32[]{:S(2)}) copy-start(bf16[384,512]{1,0:T(8,128)(2,1)} %copy-done.34) | copy-start | bytes 1179652
  328.4 80.4 %copy-start.41 = (bf16[384,512]{1,0:T(8,128)(2,1)S(1)}, bf16[384,512]{1,0:T(8,128)(2,1)}, u32[]{:S(2)}) copy-start(bf16[384,512]{1,0:T(8,128)(2,1)} %copy-done.38) | copy-start | bytes 1179652
  328.4 80.4 %copy-start.43 = (f32[384,512]{1,0:T(8,128)S(1)}, f32[384,512]{1,0:T(8,128)}, u32[]{:S(2)}) copy-start(f32[384,512]{1,0:T(8,128)} %get-tuple-element.118.dk_in_ref) | copy-start | bytes 2359300
  328.4 80.4 %copy-start.44 = (f32[384,512]{1,0:T(8,128)S(1)}, f32[384,512]{1,0:T(8,128)}, u32[]{:S(2)}) copy-start(f32[384,512]{1,0:T(8,128)} %get-tuple-element.119.dv_in_ref) | copy-start | bytes 2359300
  328.4 80.4 %copy-start.45 = (f32[6,64,512]{2,1,0:T(8,128)S(1)}, f32[6,64,512]{2,1,0:T(8,128)}, u32[]{:S(2)}) copy-start(f32[6,64,512]{2,1,0:T(8,128)} %get-tuple-element.122.xk_ref) | copy-start | bytes 2359300
  328.4 80.4 %copy-start.46 = (f32[6,64,512]{2,1,0:T(8,128)S(1)}, f32[6,64,512]{2,1,0:T(8,128)}, u32[]{:S(2)}) copy-start(f32[6,64,512]{2,1,0:T(8,128)} %get-tuple-element.123.xv_ref) | copy-start | bytes 2359300
  328.4 80.4 %copy-start.50 = (f32[384,64]{1,0:T(8,128)S(1)}, f32[384,64]{1,0:T(8,128)}, u32[]{:S(2)}) copy-start(f32[384,64]{1,0:T(8,128)} %copy-done.49) | copy-start | bytes 294916
  328.4 80.4 %copy-start.52 = (f32[384,64]{1,0:T(8,128)S(1)}, f32[384,64]{1,0:T(8,128)}, u32[]{:S(2)}) copy-start(f32[384,64]{1,0:T(8,128)} %copy-done.51) | copy-start | bytes 294916
  413.4 11.3 %copy-start.16 = (bf16[384,512]{1,0:T(8,128)(2,1)}, bf16[384,512]{1,0:T(8,128)(2,1)S(1)}, u32[]{:S(2)}) copy-start(bf16[384,512]{1,0:T(8,128)(2,1)S(1)} %get-tuple-element.125.refs_14_) | copy-start | bytes 1179652
  413.5 12.4 %copy-start.17 = (bf16[384,512]{1,0:T(8,128)(2,1)}, bf16[384,512]{1,0:T(8,128)(2,1)S(1)}, u32[]{:S(2)}) copy-start(bf16[384,512]{1,0:T(8,128)(2,1)S(1)} %get-tuple-element.126.refs_16_) | copy-start | bytes 1179652
  415.7 7.7 %copy-start.80 = (bf16[2048,16]{0,1:T(8,128)(2,1)S(1)}, bf16[2048,16]{0,1:T(8,128)(2,1)}, u32[]{:S(2)}) copy-start(bf16[2048,16]{0,1:T(8,128)(2,1)} %param.24) | copy-start | bytes 196612
  443.5 221.9 %copy-start.60 = (bf16[384,2048]{1,0:T(8,128)(2,1)S(1)}, bf16[384,2048]{1,0:T(8,128)(2,1)}, u32[]{:S(2)}) copy-start(bf16[384,2048]{1,0:T(8,128)(2,1)} %refs_3_.4) | copy-start | bytes 4718596
  443.5 221.9 %copy-start.85 = (f32[2048]{0:T(1024)S(1)}, f32[2048]{0:T(1024)}, u32[]{:S(2)}) copy-start(f32[2048]{0:T(1024)} %param.19) | copy-start | bytes 24580
  443.5 221.9 %copy-start.88 = (f32[384]{0:T(512)S(1)}, f32[384]{0:T(512)}, u32[]{:S(2)}) copy-start(f32[384]{0:T(512)} %copy-done.87) | copy-start | bytes 4612
  668.3 12.2 %copy-start.77 = (f32[256,512]{1,0:T(8,128)S(1)}, f32[256,512]{1,0:T(8,128)}, u32[]{:S(2)}) copy-start(f32[256,512]{1,0:T(8,128)} %get-tuple-element.137) | copy-start | bytes 1572868
  668.3 13.2 %copy-start.71 = (f32[256,1408]{1,0:T(8,128)S(1)}, f32[256,1408]{1,0:T(8,128)}, u32[]{:S(2)}) copy-start(f32[256,1408]{1,0:T(8,128)} %get-tuple-element.140) | copy-start | bytes 4325380
  683.1 8.7 %copy-start.1 = (bf16[512,2048]{1,0:T(8,128)(2,1)S(1)}, bf16[512,2048]{1,0:T(8,128)(2,1)}, u32[]{:S(2)}) copy-start(bf16[512,2048]{1,0:T(8,128)(2,1)} %param.28) | copy-start | bytes 6291460
  (79 other events, 289.8 us)
Sparse Core Ops, SparseCore 0:
  214.1 104.7 reduce-scatter.2
  321.7 121.7 reduce-scatter.4
